TPU v7x, 256 devices: a whole 4x4x8 slice. The times are simulated.
256 devices in a mesh: flow: 32 (over z, x), lane: 8 (over y, core).
Axes of the slice: x: 4, y: 4, z: 8, core: 2. Of those that a mesh axis runs over, the one named last changes fastest.
Arguments:
- head_prev: float32 [16, 4, 64, 4096], P('lane', None, None, 'flow'), may hold values from -6 to 6
- storage: float32 [4, 64, 4096], P(None, None, 'flow'), may hold values from 6.1035157e-06 to 2.4414063e-05
- cond_flow: float32 [4, 64, 4096], P(None, None, 'flow'), may hold values from 0.5 to 2
- cond_cross: float32 [4, 64, 4096], P(None, None, 'flow'), may hold values from 6.1035157e-06 to 2.4414063e-05
- cond_vert: float32 [4, 64, 4096], P(None, None, 'flow'), may hold values from 6.1035157e-06 to 2.4414063e-05
- active: int32 [4, 64, 4096], P(None, None, 'flow'), may hold values from 0 to 1
- hru_cells: int32 [131072, 4], P('flow'), may hold values from 0 to 24575, as said below
- hru_area: float32 [131072, 4], P('flow'), may hold values from 0.1 to 1
- hru_land: int32 [131072], P('flow'), may hold values from 0 to 15
- hru_bmp: int32 [16, 131072], P('lane', 'flow'), may hold values from 0 to 7
- rain: float32 [131072], P('flow'), may hold values from 0.5 to 4
- perc_table: float32 [16, 8], replicated, may hold values from 6.1035157e-06 to 6.1035156e-05
- hru_live: int32 [32], P('flow'), may hold values from 1024 to 4096, as said below
Outputs:
- head: float32 [16, 4, 64, 4096], P('lane', None, None, 'flow')
- anomaly: float32 [16, 4, 64, 4096], P('lane', None, None, 'flow')
Inputs may be any that keep to these rules, and one draw needn't show every extreme that they name: `hru_cells`: w // 8192 is 0 for the previous device along flow, 1 for the HRU's own device and 2 for the next; no target lies outside the grid. `hru_live`: slots of device k at positions 4096 * k + i with i at or above its count contribute nothing; some device is full.
All inputs are finite; a program needn't handle non-finite values.
Results may differ from a plain program's by a relative error of at most 0.00045.
Values sent between devices are 32-bit elements; how exact they have to be, the bound alone decides.
No kernel may reach another device: no remote copies, remote signals or barrier semaphores. Data moves between devices by JAX's collectives and lax.ppermute only.
A program may use at most 128 MiB of HBM per device.

v0:
```python
import functools

import jax
import jax.numpy as jnp
from jax import lax
from jax.experimental import pallas as pl
from jax.experimental.pallas import tpu as pltpu
from jax.sharding import PartitionSpec as P

STEPS = 16
SUBS = 8
ROWS = 24
F32 = jnp.float32


def halves(fn, a):
    return jnp.concatenate([fn(a[:, :128]), fn(a[:, 128:])], axis=1)


def cross_next(a):
    return halves(lambda h: pltpu.roll(h, 127, 1), a)


def cross_prev(a):
    return halves(lambda h: pltpu.roll(h, 1, 1), a)


def layer_rolls(a):
    lo = lax.broadcasted_iota(jnp.int32, (a.shape[0], 128), 1) < 64
    return lo, pltpu.roll(a[:, :128], 64, 1), pltpu.roll(a[:, 128:], 64, 1)


def layer_next(a):
    lo, r0, r1 = layer_rolls(a)
    return jnp.concatenate([jnp.where(lo, r0, r1), jnp.where(lo, r1, r0)], axis=1)


def layer_prev(a):
    lo, r0, r1 = layer_rolls(a)
    return jnp.concatenate([jnp.where(lo, r1, r0), jnp.where(lo, r0, r1)], axis=1)


def coupled(cross, vert, head):
    out = cross * cross_next(head) + cross_prev(cross * head)
    return out + vert * layer_next(head) + layer_prev(vert * head)


def reduce_chain(leak, face):
    n = len(leak)
    first, link, shunt = leak[0], face[0], leak[1]
    inv, ratio, share = [None] * n, [None] * n, [None] * n
    for i in range(1, n - 1):
        inv[i] = 1.0 / (face[i] + (shunt + link))
        ratio[i] = face[i] * inv[i]
        share[i] = link * inv[i]
        first = first + shunt * share[i]
        shunt = leak[i + 1] + shunt * ratio[i]
        link = link * ratio[i]
    return (inv, ratio, share), first, shunt, link


def reduce_source(ratio, share, rhs):
    n = len(rhs)
    first = rhs[0]
    part = [None] * n
    part[1] = rhs[1]
    for i in range(1, n - 1):
        first = first + share[i] * part[i]
        part[i + 1] = rhs[i + 1] + ratio[i] * part[i]
    return part, first, part[n - 1]


def fill_chain(coef, part, first, last):
    inv, ratio, share = coef
    n = len(ratio)
    out = [None] * n
    out[0], out[n - 1] = first, last
    for i in range(n - 2, 0, -1):
        value = share[i] * first + ratio[i] * out[i + 1]
        out[i] = value if part is None else value + inv[i] * part[i]
    return out


def full_factor(leak, face):
    n = len(leak)
    shunt = leak[0]
    inv, ratio = [None] * n, [None] * n
    for i in range(n - 1):
        inv[i] = 1.0 / (face[i] + shunt)
        ratio[i] = face[i] * inv[i]
        shunt = leak[i + 1] + shunt * ratio[i]
    inv[n - 1] = 1.0 / shunt
    return inv, ratio


def full_solve(inv, ratio, rhs):
    n = len(rhs)
    part = [rhs[0]]
    for i in range(n - 1):
        part.append(rhs[i + 1] + ratio[i] * part[i])
    out = [None] * n
    out[n - 1] = inv[n - 1] * part[n - 1]
    for i in range(n - 2, -1, -1):
        out[i] = inv[i] * part[i] + ratio[i] * out[i + 1]
    return out


def to_rows(a):
    return [a[k : k + 1] for k in range(SUBS)]


def interleave(a, b):
    return [x for pair in zip(to_rows(a), to_rows(b)) for x in pair]


def stack_ends(nodes):
    return jnp.concatenate(nodes[0::2], axis=0), jnp.concatenate(nodes[1::2], axis=0)


def column_sum(a):
    return jnp.sum(a, axis=0, keepdims=True)


def both(fn):
    return jnp.concatenate([fn(0), fn(1)], axis=1)


def step_rows(i):
    return pl.ds(i, SUBS, stride=STEPS)


def scatter_kernel(cells_ref, area_ref, land_ref, bmp_ref, rain_ref, table_ref, live_ref,
                   before_ref, own_ref, after_ref, amount_ref, acc_ref):
    slots = land_ref.shape[1]
    land = land_ref[...]
    rates = jnp.zeros((8, slots), F32)
    for use in range(table_ref.shape[1]):
        rates = jnp.where(land == use, table_ref[:, use : use + 1], rates)
    bmp = bmp_ref[...]
    chosen = jnp.zeros(bmp.shape, F32)
    for code in range(table_ref.shape[0]):
        chosen = jnp.where(bmp == code, rates[code : code + 1], chosen)
    alive = lax.broadcasted_iota(jnp.int32, (1, slots), 1) < live_ref[0]
    perc = jnp.where(alive, rain_ref[...] * chosen, 0.0)
    for q in range(4):
        amount = perc * area_ref[q : q + 1, :]
        high = amount.astype(jnp.bfloat16).astype(F32)
        amount_ref[q, 0:2, :] = high
        amount_ref[q, 2:4, :] = amount - high
    acc_ref[...] = jnp.zeros_like(acc_ref)
    width = 1024
    column = lax.broadcasted_iota(jnp.int32, (128, width), 0)
    line = lax.broadcasted_iota(jnp.int32, (192, width), 0)
    for q in range(4):

        @pl.loop(0, slots // width)
        def _(c):
            at = pl.ds(pl.multiple_of(c * width, width), width)
            cell = cells_ref[q : q + 1, at]
            hit = column == (cell & 127)
            put = [jnp.where(hit, amount_ref[q, k : k + 1, at], 0.0).astype(jnp.bfloat16) for k in (0, 2, 1, 3)]
            rows = jnp.where(line == (cell >> 7), 1.0, 0.0).astype(jnp.bfloat16)
            acc_ref[...] += lax.dot_general(
                jnp.concatenate(put, axis=0), rows, (((1,), (1,)), ((), ())), preferred_element_type=F32
            )

    lane0 = acc_ref[0:128, :] + acc_ref[128:256, :]
    lane1 = acc_ref[256:384, :] + acc_ref[384:512, :]
    for k, ref in enumerate((before_ref, own_ref, after_ref)):
        ref[...] = jnp.concatenate([lane0[:, 64 * k : 64 * k + 64], lane1[:, 64 * k : 64 * k + 64]], axis=1)


def coefficient_kernel(head_ref, storage_ref, flow_ref, cross_ref, vert_ref, active_ref,
                       fields_ref, small_ref, base_ref, gather_ref, turned):
    def turn(slot, part):
        for h in range(2):
            turned[slot, h] = part(h).T

    for slot, ref in enumerate((storage_ref, flow_ref, cross_ref, vert_ref)):
        turn(slot, lambda h: ref[2 * h : 2 * h + 2].reshape(128, 128))
    turn(4, lambda h: active_ref[2 * h : 2 * h + 2].reshape(128, 128).astype(F32))
    for s in range(2):
        turn(5 + s, lambda h: head_ref[s, 2 * h : 2 * h + 2].reshape(128, 128))

    def step(slot, i):
        return both(lambda h: turned[slot, h, step_rows(i), :])

    lane = lax.broadcasted_iota(jnp.int32, (SUBS, 256), 1)
    inner_cross = lane % 64 != 63
    inner_vert = lane < 192
    mask = [step(4, i) for i in range(STEPS)]
    leak, face, crosses, verts = [], [], [], []
    for i in range(STEPS):
        m = mask[i]
        cross = jnp.where(inner_cross, step(2, i) * m * cross_next(m), 0.0)
        vert = jnp.where(inner_vert, step(3, i) * m * layer_next(m), 0.0)
        store = step(0, i)
        leak.append(store + cross + cross_prev(cross) + vert + layer_prev(vert))
        after = mask[i + 1] if i + 1 < STEPS else pltpu.roll(mask[0], SUBS - 1, 0)
        face.append(step(1, i) * m * after)
        crosses.append(cross)
        verts.append(vert)
        fields_ref[0, i] = cross
        fields_ref[1, i] = vert
        fields_ref[2, i] = m
        for s in range(2):
            head = step(5 + s, i)
            base = store * head
            base_ref[s, i] = base
            base_ref[2 + s, i] = base + coupled(cross, vert, head)
    coef, first, last, link = reduce_chain(leak, face[: STEPS - 1])
    leak1 = interleave(first, last)
    face1 = interleave(link, face[STEPS - 1])[: 2 * SUBS - 1]
    coef1, first1, last1, link1 = reduce_chain(leak1, face1)
    for k in range(3):
        for i in range(1, STEPS - 1):
            fields_ref[3 + k, i] = coef[k][i]
        for i in range(1, 2 * SUBS - 1):
            small_ref[k, i : i + 1] = coef1[k][i]
    one, zero = jnp.ones((1, 256), F32), jnp.zeros((1, 256), F32)
    basis = []
    for ends in ((one, zero), (zero, one)):
        basis.append(fill_chain(coef, None, *stack_ends(fill_chain(coef1, None, *ends))))
    for k in range(2):
        for i in range(STEPS):
            fields_ref[6 + k, i] = basis[k][i]
    gather_ref[0:1] = first1
    gather_ref[1:2] = last1
    gather_ref[2:3] = link1
    gather_ref[3:4] = both(lambda h: turned[1, h, 127:128, :] * turned[4, h, 127:128, :])
    gather_ref[4:5] = both(lambda h: turned[4, h, 0:1, :])
    for row, weight, move in ((5, crosses, cross_next), (9, verts, layer_next)):
        sums = [jnp.zeros((SUBS, 256), F32)] * 4
        for i in range(STEPS):
            moved = [move(basis[k][i]) for k in range(2)]
            for a in range(2):
                weighted = weight[i] * basis[a][i]
                for b in range(2):
                    sums[2 * a + b] = sums[2 * a + b] + weighted * moved[b]
        for k in range(4):
            gather_ref[row + k : row + k + 1] = column_sum(sums[k])


def load_coef(fields_ref, small_ref):
    coef = tuple([None] + [fields_ref[3 + k, i] for i in range(1, STEPS - 1)] + [None] for k in range(3))
    coef1 = tuple([None] + [small_ref[k, i : i + 1] for i in range(1, 2 * SUBS - 1)] + [None] for k in range(3))
    return coef, coef1


def local_solve(coef, coef1, rhs, first, last):
    part, ends_first, ends_last = reduce_source(coef[1], coef[2], rhs)
    part1, source_first, source_last = reduce_source(coef1[1], coef1[2], interleave(ends_first, ends_last))
    ends = stack_ends(fill_chain(coef1, part1, first, last))
    return fill_chain(coef, part, *ends), source_first, source_last


def source_kernel(fields_ref, small_ref, base_ref, own_ref, low_ref, high_ref, coefs_ref,
                  source_ref, inner_ref, out_ref, rain_scratch):
    rain_scratch[...] = own_ref[...] + low_ref[...] + high_ref[...]
    coef, coef1 = load_coef(fields_ref, small_ref)
    top = lax.broadcasted_iota(jnp.int32, (SUBS, 128), 1) < 64
    zero = jnp.zeros((1, 256), F32)
    none = jnp.zeros((SUBS, 128), F32)
    rows = []
    for s in range(2):
        rhs = []
        for i in range(STEPS):
            water = rain_scratch[step_rows(i), :]
            if s:
                water = pltpu.roll(water, 64, 1)
            water = jnp.concatenate([jnp.where(top, water, 0.0), none], axis=1) * fields_ref[2, i]
            source_ref[s, i] = base_ref[s, i] + water
            rhs.append(base_ref[2 + s, i] + water)
        inner, first, last = local_solve(coef, coef1, rhs, zero, zero)
        sums = [jnp.zeros((SUBS, 256), F32)] * 2
        for i in range(STEPS):
            inner_ref[s, i] = inner[i]
            later = source_ref[s, i] + coupled(fields_ref[0, i], fields_ref[1, i], inner[i])
            for k in range(2):
                sums[k] = sums[k] + fields_ref[6 + k, i] * later
        rows += [first, last, column_sum(sums[0]), column_sum(sums[1])]
    head = coefs_ref[0:13]
    block = jnp.concatenate([head] + rows + [jnp.zeros((3, 256), F32)], axis=0)
    for k in range(out_ref.shape[0]):
        for h in range(2):
            out_ref[k, ROWS * h : ROWS * h + ROWS] = block[:, 128 * h : 128 * h + 128]


def sweep_kernel(place_ref, gathered_ref, fields_ref, small_ref, source_ref, inner_ref,
                 head_ref, total_ref, ends_scratch, turned):
    devices = gathered_ref.shape[0] // (2 * ROWS)
    per = devices // SUBS

    def got(row, i):
        return both(lambda h: gathered_ref[pl.ds((2 * i + h) * ROWS + row, SUBS, stride=2 * per * ROWS), :])

    leak, face = [], []
    for i in range(per):
        leak += [got(0, i), got(1, i)]
        after = got(4, i + 1) if i + 1 < per else pltpu.roll(got(4, 0), SUBS - 1, 0)
        face += [got(2, i), got(3, i) * after]
    coef, first, last, link = reduce_chain(leak, face[: 2 * per - 1])
    leak1 = interleave(first, last)
    face1 = interleave(link, face[2 * per - 1])[: 2 * SUBS - 1]
    inv1, ratio1 = full_factor(leak1, face1)

    def across_devices(rhs):
        part, ends_first, ends_last = reduce_source(coef[1], coef[2], rhs)
        ends = full_solve(inv1, ratio1, interleave(ends_first, ends_last))
        return fill_chain(coef, part, *stack_ends(ends))

    cross_k = [[got(5 + k, i) for k in range(4)] for i in range(per)]
    vert_k = [[got(9 + k, i) for k in range(4)] for i in range(per)]
    for s in range(2):
        row = 13 + 4 * s
        ends = across_devices([got(row + a, i) for i in range(per) for a in range(2)])
        rhs = []
        for i in range(per):
            low, high = ends[2 * i], ends[2 * i + 1]
            later = [got(row + 2 + a, i) for a in range(2)]
            for k, ahead, back in ((cross_k[i], cross_next, cross_prev), (vert_k[i], layer_next, layer_prev)):
                low_ahead, high_ahead = ahead(low), ahead(high)
                later[0] = later[0] + k[0] * low_ahead + k[1] * high_ahead + back(k[0] * low + k[2] * high)
                later[1] = later[1] + k[2] * low_ahead + k[3] * high_ahead + back(k[1] * low + k[3] * high)
            rhs += later
        ends2 = across_devices(rhs)
        for i in range(per):
            for k, value in enumerate((ends[2 * i], ends[2 * i + 1], ends2[2 * i], ends2[2 * i + 1])):
                ends_scratch[4 * s + k, SUBS * i : SUBS * i + SUBS] = value
    coef, coef1 = load_coef(fields_ref, small_ref)
    place = place_ref[0]
    at = pl.ds((place % per) * SUBS + place // per, 1)
    for s in range(2):
        low1, high1, low2, high2 = [ends_scratch[4 * s + k, at, :] for k in range(4)]
        rhs = []
        for i in range(STEPS):
            head = inner_ref[s, i] + fields_ref[6, i] * low1 + fields_ref[7, i] * high1
            rhs.append(source_ref[s, i] + coupled(fields_ref[0, i], fields_ref[1, i], head))
        solved, _, _ = local_solve(coef, coef1, rhs, low2, high2)
        for i in range(STEPS):
            for h in range(2):
                turned[s, h, step_rows(i), :] = solved[i][:, 128 * h : 128 * h + 128]
    for h in range(2):
        lanes = [turned[s, h].T for s in range(2)]
        for s in range(2):
            head_ref[s, 2 * h : 2 * h + 2] = lanes[s].reshape(2, 64, 128)
        total_ref[2 * h : 2 * h + 2] = (lanes[0] + lanes[1]).reshape(2, 64, 128)


VMEM = pl.BlockSpec(memory_space=pltpu.VMEM)
SMEM = pl.BlockSpec(memory_space=pltpu.SMEM)


def kernel_call(body, name, specs, outs, scratch, flops):
    return pl.pallas_call(
        body,
        name=name,
        in_specs=specs,
        out_specs=[VMEM] * len(outs),
        out_shape=[jax.ShapeDtypeStruct(shape, F32) for shape in outs],
        scratch_shapes=[pltpu.VMEM(shape, F32) for shape in scratch],
        compiler_params=pltpu.CompilerParams(vmem_limit_bytes=48 * 2**20),
        cost_estimate=pl.CostEstimate(flops=flops, bytes_accessed=2 * 2**20, transcendentals=0),
    )


def on_device(
    head_prev,
    storage,
    cond_flow,
    cond_cross,
    cond_vert,
    active,
    hru_cells,
    hru_area,
    hru_land,
    hru_bmp,
    rain,
    perc_table,
    hru_live,
):
    slots = hru_land.shape[0]
    devices = lax.axis_size("flow")
    tile = (128, 128)
    before, own, after = kernel_call(
        scatter_kernel, "scatter", [VMEM] * 6 + [SMEM], [tile] * 3, [(4, 4, slots), (512, 192)], 4 * 10**9
    )(
        hru_cells.T, hru_area.T, hru_land.reshape(1, slots), hru_bmp, rain.reshape(1, slots), perc_table.T, hru_live
    )
    high = lax.ppermute(before, "flow", [(i + 1, i) for i in range(devices - 1)])
    low = lax.ppermute(after, "flow", [(i, i + 1) for i in range(devices - 1)])
    fields, small, base, coefs = kernel_call(
        coefficient_kernel,
        "coefficients",
        [VMEM] * 6,
        [(8, STEPS, SUBS, 256), (3, 2 * SUBS, 256), (4, STEPS, SUBS, 256), (16, 256)],
        [(7, 2, 128, 128)],
        4 * 10**9,
    )(head_prev, storage, cond_flow, cond_cross, cond_vert, active)
    source, inner, block = kernel_call(
        source_kernel,
        "sources",
        [VMEM] * 7,
        [(2, STEPS, SUBS, 256), (2, STEPS, SUBS, 256), (devices, 2 * ROWS, 128)],
        [tile],
        10**9,
    )(fields, small, base, own, low, high, coefs)
    gathered = lax.all_to_all(block, "flow", split_axis=0, concat_axis=0, tiled=True)
    place = lax.axis_index("flow").astype(jnp.int32).reshape(1)
    head, total = kernel_call(
        sweep_kernel,
        "sweeps",
        [SMEM] + [VMEM] * 5,
        [head_prev.shape, storage.shape],
        [(8, devices, 256), (2, 2, 128, 128)],
        10**9,
    )(place, gathered.reshape(devices * 2 * ROWS, 128), fields, small, source, inner)
    lanes = lax.axis_size("lane")
    total = total + lax.ppermute(total, "lane", [(i, i ^ 1) for i in range(lanes)])
    whole = total
    for k in range(2, lanes, 2):
        whole = whole + lax.ppermute(total, "lane", [(i, (i + k) % lanes) for i in range(lanes)])
    anomaly = head - whole[None] / (2 * lanes)
    return head, anomaly


def solution(mesh):
    return jax.shard_map(
        on_device,
        mesh=mesh,
        in_specs=(
            P("lane", None, None, "flow"),
            P(None, None, "flow"),
            P(None, None, "flow"),
            P(None, None, "flow"),
            P(None, None, "flow"),
            P(None, None, "flow"),
            P("flow", None),
            P("flow", None),
            P("flow"),
            P("lane", "flow"),
            P("flow"),
            P(),
            P("flow"),
        ),
        out_specs=(P("lane", None, None, "flow"), P("lane", None, None, "flow")),
        check_vma=False,
    )
```

profile of v0, /device:TPU:1, one launch (start us, length us, event | category | flops | bytes accessed | tf_op | source)
XLA Modules:
  0.0 76.0 jit_solution(15695306553031585347)
XLA Ops:
  1.3 0.7 copy-done.11
  2.0 0.8 %copy-done.6 = s32[4096,4]{0,1:T(4,128)S(1)} copy-done((s32[4096,4]{0,1:T(4,128)S(1)}, s32[4096,4]{0,1:T(4,128)}, u32[]{:S(2)}) %copy-start.6) | copy-done | bytes 65560
  2.8 0.8 %copy-done.7 = f32[4096,4]{0,1:T(4,128)S(1)} copy-done((f32[4096,4]{0,1:T(4,128)S(1)}, f32[4096,4]{0,1:T(4,128)}, u32[]{:S(2)}) %copy-start.7) | copy-done | bytes 65560
  3.7 0.8 copy-done.8
  4.4 0.7 copy-done.9
  5.1 0.7 copy-done.10
  5.9 8.3 %scatter.1 = (f32[128,128]{1,0:T(8,128)S(1)}, f32[128,128]{1,0:T(8,128)S(1)}, f32[128,128]{1,0:T(8,128)S(1)}) custom-call(s32[4,4096]{1,0:T(4,128)S(1)} %bitcast.8, f32[4,4096]{1,0:T(4,128)S(1)} %bitcast.9, s32[1,4096]{1,0:T(1,128)S(1)} %bitcast.10, s32[2,4096]{1,0:T(2,128)S(1)} %copy-done.8, f32[1,4096]{1,0:T(1,128)S(1)} %bitcast.11, f32[8,16]{1,0:T(8,128)S(1)} %bitcast.12, ...), custom_call_target="tpu_custom_call" | custom-call | flops 4000000000 | bytes 2097152 | tf_op jit(solution)/shard_map/scatter/pallas_call | solution.py:385
  14.2 3.9 %collective-permute-start = (f32[128,128]{1,0:T(8,128)S(1)}, f32[128,128]{1,0:T(8,128)S(1)}, u32[]{:S(2)}, u32[]{:S(2)}) collective-permute-start(f32[128,128]{1,0:T(8,128)S(1)} %get-tuple-element.18), channel_id=1, source_target_pairs={{0,8},{8,16},{16,24},{24,32},{32,40},{40,48},{48,56},{56,64},{64,7... | collective-permute-start | bytes 196616 | tf_op jit(solution)/shard_map/ppermute | solution.py:391
  18.1 1.3 %collective-permute-start.1 = (f32[128,128]{1,0:T(8,128)S(1)}, f32[128,128]{1,0:T(8,128)S(1)}, u32[]{:S(2)}, u32[]{:S(2)}) collective-permute-start(f32[128,128]{1,0:T(8,128)S(1)} %get-tuple-element.19), channel_id=1, source_target_pairs={{8,0},{16,8},{24,16},{32,24},{40,32},{48,40},{56,48},{64,56},{72,6... | collective-permute-start | bytes 196616 | tf_op jit(solution)/shard_map/ppermute | solution.py:390
  19.5 1.3 %coefficients.1 = (f32[8,16,8,256]{3,2,1,0:T(8,128)S(1)}, f32[3,16,256]{2,1,0:T(8,128)S(1)}, f32[4,16,8,256]{3,2,1,0:T(8,128)S(1)}, f32[16,256]{1,0:T(8,128)S(1)}) custom-call(f32[2,4,64,128]{3,2,1,0:T(8,128)S(1)} %copy-done, f32[4,64,128]{2,1,0:T(8,128)S(1)} %copy-done.1, f32[4,64,128]{2,1,0:T(8,128)S(1)} %copy-done.2, f32[4,64,128]{2,1,0:T(8,128)S(1)} %copy-done.3, ...), custom_call_target="tpu_custom_call" | custom-call | flops 4000000000 | bytes 2097152 | tf_op jit(solution)/shard_map/coefficients/pallas_call | solution.py:392
  20.8 2.3 %collective-permute-done.1.high_ref = f32[128,128]{1,0:T(8,128)S(1)} collective-permute-done((f32[128,128]{1,0:T(8,128)S(1)}, f32[128,128]{1,0:T(8,128)S(1)}, u32[]{:S(2)}, u32[]{:S(2)}) %collective-permute-start.1) | collective-permute-done | bytes 65568 | tf_op jit(solution)/shard_map/ppermute | solution.py:390
  23.1 1.5 %sources.1 = (f32[2,16,8,256]{3,2,1,0:T(8,128)S(1)}, f32[2,16,8,256]{3,2,1,0:T(8,128)S(1)}, f32[32,48,128]{2,1,0:T(8,128)}) custom-call(f32[8,16,8,256]{3,2,1,0:T(8,128)S(1)} %get-tuple-element.14.fields_ref, f32[3,16,256]{2,1,0:T(8,128)S(1)} %get-tuple-element.15.small_ref, f32[4,16,8,256]{3,2,1,0:T(8,128)S(1)} %get-tuple-element.16.base_ref, ...), custom_call_target="tpu_custom_call" | custom-call | flops 1000000000 | bytes 2097152 | tf_op jit(solution)/shard_map/sources/pallas_call | solution.py:400
  24.6 13.1 %all-to-all-start = ((f32[32,48,128]{2,1,0:T(8,128)}), f32[32,48,128]{2,1,0:T(8,128)S(1)}, u32[]{:S(2)}, u32[]{:S(2)}) async-start(f32[32,48,128]{2,1,0:T(8,128)} %get-tuple-element.21), calls=%async_computation | async-start | bytes 1572864 | tf_op jit(solution)/shard_map/all_to_all | solution.py:408
  37.7 19.6 %all-to-all-done = f32[32,48,128]{2,1,0:T(8,128)S(1)} async-done(((f32[32,48,128]{2,1,0:T(8,128)}), f32[32,48,128]{2,1,0:T(8,128)S(1)}, u32[]{:S(2)}, u32[]{:S(2)}) %all-to-all-start) | async-done | bytes 786464 | tf_op jit(solution)/shard_map/all_to_all | solution.py:408
  57.3 2.2 %sweeps.1 = (f32[2,4,64,128]{3,2,1,0:T(8,128)}, f32[4,64,128]{2,1,0:T(8,128)S(1)}) custom-call(s32[1]{0:T(128)} %bitcast.place_ref, f32[1536,128]{1,0:T(8,128)S(1)} %bitcast.7, f32[8,16,8,256]{3,2,1,0:T(8,128)S(1)} %get-tuple-element.14.fields_ref, f32[3,16,256]{2,1,0:T(8,128)S(1)} %get-tuple-element.15.small_ref, ...), custom_call_target="tpu_custom_call" | custom-call | flops 1000000000 | bytes 2097152 | tf_op jit(solution)/shard_map/sweeps/pallas_call | solution.py:410
  59.5 4.6 %collective-permute-start.2 = (f32[4,64,128]{2,1,0:T(8,128)S(1)}, f32[4,64,128]{2,1,0:T(8,128)S(1)}, u32[]{:S(2)}, u32[]{:S(2)}) collective-permute-start(f32[4,64,128]{2,1,0:T(8,128)S(1)} %get-tuple-element.25), channel_id=1, source_target_pairs={{0,1},{1,0},{2,3},{3,2},{4,5},{5,4},{6,7},{7,6},{8,9},{9,8},{10,11... | collective-permute-start | bytes 393224 | tf_op jit(solution)/shard_map/ppermute | solution.py:419
  64.1 1.0 %collective-permute-done.2 = f32[4,64,128]{2,1,0:T(8,128)S(1)} collective-permute-done((f32[4,64,128]{2,1,0:T(8,128)S(1)}, f32[4,64,128]{2,1,0:T(8,128)S(1)}, u32[]{:S(2)}, u32[]{:S(2)}) %collective-permute-start.2) | collective-permute-done | bytes 131104 | tf_op jit(solution)/shard_map/ppermute | solution.py:419
  65.1 0.0 copy-start.12
  65.1 1.4 %collective-permute-start.3 = (f32[4,64,128]{2,1,0:T(8,128)S(1)}, f32[4,64,128]{2,1,0:T(8,128)S(1)}, u32[]{:S(2)}, u32[]{:S(2)}) collective-permute-start(f32[4,64,128]{2,1,0:T(8,128)S(1)} %add.12), channel_id=1, source_target_pairs={{0,2},{1,3},{2,4},{3,5},{4,6},{5,7},{6,0},{7,1},{8,10},{9,11},{10,... | collective-permute-start | bytes 393224 | tf_op jit(solution)/shard_map/ppermute | solution.py:422
  66.5 2.6 %collective-permute-start.4 = (f32[4,64,128]{2,1,0:T(8,128)S(1)}, f32[4,64,128]{2,1,0:T(8,128)S(1)}, u32[]{:S(2)}, u32[]{:S(2)}) collective-permute-start(f32[4,64,128]{2,1,0:T(8,128)S(1)} %add.12), channel_id=1, source_target_pairs={{0,4},{1,5},{2,6},{3,7},{4,0},{5,1},{6,2},{7,3},{8,12},{9,13},{10,... | collective-permute-start | bytes 393224 | tf_op jit(solution)/shard_map/ppermute | solution.py:422
  69.2 1.1 %collective-permute-start.5 = (f32[4,64,128]{2,1,0:T(8,128)S(1)}, f32[4,64,128]{2,1,0:T(8,128)S(1)}, u32[]{:S(2)}, u32[]{:S(2)}) collective-permute-start(f32[4,64,128]{2,1,0:T(8,128)S(1)} %add.12), channel_id=1, source_target_pairs={{0,6},{1,7},{2,0},{3,1},{4,2},{5,3},{6,4},{7,5},{8,14},{9,15},{10,... | collective-permute-start | bytes 393224 | tf_op jit(solution)/shard_map/ppermute | solution.py:422
  70.2 1.1 %collective-permute-done.3 = f32[4,64,128]{2,1,0:T(8,128)S(1)} collective-permute-done((f32[4,64,128]{2,1,0:T(8,128)S(1)}, f32[4,64,128]{2,1,0:T(8,128)S(1)}, u32[]{:S(2)}, u32[]{:S(2)}) %collective-permute-start.3) | collective-permute-done | bytes 131104 | tf_op jit(solution)/shard_map/ppermute | solution.py:422
  71.3 3.9 %collective-permute-done.4 = f32[4,64,128]{2,1,0:T(8,128)S(1)} collective-permute-done((f32[4,64,128]{2,1,0:T(8,128)S(1)}, f32[4,64,128]{2,1,0:T(8,128)S(1)}, u32[]{:S(2)}, u32[]{:S(2)}) %collective-permute-start.4) | collective-permute-done | bytes 131104 | tf_op jit(solution)/shard_map/ppermute | solution.py:422
  75.3 0.7 broadcast_subtract_fusion
  (23 shorter events, 0.1 us)
Async XLA Ops:
  1.3 0.7 copy-start.11
  2.0 0.8 %copy-start.6 = (s32[4096,4]{0,1:T(4,128)S(1)}, s32[4096,4]{0,1:T(4,128)}, u32[]{:S(2)}) copy-start(s32[4096,4]{0,1:T(4,128)} %param.19) | copy-start | bytes 196612
  2.8 0.8 %copy-start.7 = (f32[4096,4]{0,1:T(4,128)S(1)}, f32[4096,4]{0,1:T(4,128)}, u32[]{:S(2)}) copy-start(f32[4096,4]{0,1:T(4,128)} %param.20) | copy-start | bytes 196612
  3.6 0.8 copy-start.8
  4.4 0.7 copy-start.9
  5.1 0.7 copy-start.10
  5.8 13.6 %copy-start = (f32[2,4,64,128]{3,2,1,0:T(8,128)S(1)}, f32[2,4,64,128]{3,2,1,0:T(8,128)}, u32[]{:S(2)}) copy-start(f32[2,4,64,128]{3,2,1,0:T(8,128)} %head_ref.1) | copy-start | bytes 786436
  5.8 13.6 %copy-start.1 = (f32[4,64,128]{2,1,0:T(8,128)S(1)}, f32[4,64,128]{2,1,0:T(8,128)}, u32[]{:S(2)}) copy-start(f32[4,64,128]{2,1,0:T(8,128)} %storage_ref.1) | copy-start | bytes 393220
  5.8 13.6 %copy-start.2 = (f32[4,64,128]{2,1,0:T(8,128)S(1)}, f32[4,64,128]{2,1,0:T(8,128)}, u32[]{:S(2)}) copy-start(f32[4,64,128]{2,1,0:T(8,128)} %flow_ref.1) | copy-start | bytes 393220
  5.8 13.6 %copy-start.3 = (f32[4,64,128]{2,1,0:T(8,128)S(1)}, f32[4,64,128]{2,1,0:T(8,128)}, u32[]{:S(2)}) copy-start(f32[4,64,128]{2,1,0:T(8,128)} %cross_ref.1) | copy-start | bytes 393220
  5.9 13.6 %copy-start.4 = (f32[4,64,128]{2,1,0:T(8,128)S(1)}, f32[4,64,128]{2,1,0:T(8,128)}, u32[]{:S(2)}) copy-start(f32[4,64,128]{2,1,0:T(8,128)} %vert_ref.1) | copy-start | bytes 393220
  5.9 13.6 %copy-start.5 = (s32[4,64,128]{2,1,0:T(8,128)S(1)}, s32[4,64,128]{2,1,0:T(8,128)}, u32[]{:S(2)}) copy-start(s32[4,64,128]{2,1,0:T(8,128)} %active_ref.1) | copy-start | bytes 393220
  14.2 6.6 %collective-permute-start = (f32[128,128]{1,0:T(8,128)S(1)}, f32[128,128]{1,0:T(8,128)S(1)}, u32[]{:S(2)}, u32[]{:S(2)}) collective-permute-start(f32[128,128]{1,0:T(8,128)S(1)} %get-tuple-element.18), channel_id=1, source_target_pairs={{0,8},{8,16},{16,24},{24,32},{32,40},{40,48},{48,56},{56,64},{64,7... | collective-permute-start | bytes 196616 | tf_op jit(solution)/shard_map/ppermute | solution.py:391
  18.1 5.0 %collective-permute-start.1 = (f32[128,128]{1,0:T(8,128)S(1)}, f32[128,128]{1,0:T(8,128)S(1)}, u32[]{:S(2)}, u32[]{:S(2)}) collective-permute-start(f32[128,128]{1,0:T(8,128)S(1)} %get-tuple-element.19), channel_id=1, source_target_pairs={{8,0},{16,8},{24,16},{32,24},{40,32},{48,40},{56,48},{64,56},{72,6... | collective-permute-start | bytes 196616 | tf_op jit(solution)/shard_map/ppermute | solution.py:390
  24.6 32.7 %all-to-all-start = ((f32[32,48,128]{2,1,0:T(8,128)}), f32[32,48,128]{2,1,0:T(8,128)S(1)}, u32[]{:S(2)}, u32[]{:S(2)}) async-start(f32[32,48,128]{2,1,0:T(8,128)} %get-tuple-element.21), calls=%async_computation | async-start | bytes 1572864 | tf_op jit(solution)/shard_map/all_to_all | solution.py:408
  59.5 5.6 %collective-permute-start.2 = (f32[4,64,128]{2,1,0:T(8,128)S(1)}, f32[4,64,128]{2,1,0:T(8,128)S(1)}, u32[]{:S(2)}, u32[]{:S(2)}) collective-permute-start(f32[4,64,128]{2,1,0:T(8,128)S(1)} %get-tuple-element.25), channel_id=1, source_target_pairs={{0,1},{1,0},{2,3},{3,2},{4,5},{5,4},{6,7},{7,6},{8,9},{9,8},{10,11... | collective-permute-start | bytes 393224 | tf_op jit(solution)/shard_map/ppermute | solution.py:419
  65.1 10.1 %copy-start.12 = (f32[2,4,64,128]{3,2,1,0:T(8,128)S(1)}, f32[2,4,64,128]{3,2,1,0:T(8,128)}, u32[]{:S(2)}) copy-start(f32[2,4,64,128]{3,2,1,0:T(8,128)} %get-tuple-element.12) | copy-start | bytes 786436
  65.1 6.2 %collective-permute-start.3 = (f32[4,64,128]{2,1,0:T(8,128)S(1)}, f32[4,64,128]{2,1,0:T(8,128)S(1)}, u32[]{:S(2)}, u32[]{:S(2)}) collective-permute-start(f32[4,64,128]{2,1,0:T(8,128)S(1)} %add.12), channel_id=1, source_target_pairs={{0,2},{1,3},{2,4},{3,5},{4,6},{5,7},{6,0},{7,1},{8,10},{9,11},{10,... | collective-permute-start | bytes 393224 | tf_op jit(solution)/shard_map/ppermute | solution.py:422
  66.5 8.7 %collective-permute-start.4 = (f32[4,64,128]{2,1,0:T(8,128)S(1)}, f32[4,64,128]{2,1,0:T(8,128)S(1)}, u32[]{:S(2)}, u32[]{:S(2)}) collective-permute-start(f32[4,64,128]{2,1,0:T(8,128)S(1)} %add.12), channel_id=1, source_target_pairs={{0,4},{1,5},{2,6},{3,7},{4,0},{5,1},{6,2},{7,3},{8,12},{9,13},{10,... | collective-permute-start | bytes 393224 | tf_op jit(solution)/shard_map/ppermute | solution.py:422
  69.2 6.1 %collective-permute-start.5 = (f32[4,64,128]{2,1,0:T(8,128)S(1)}, f32[4,64,128]{2,1,0:T(8,128)S(1)}, u32[]{:S(2)}, u32[]{:S(2)}) collective-permute-start(f32[4,64,128]{2,1,0:T(8,128)S(1)} %add.12), channel_id=1, source_target_pairs={{0,6},{1,7},{2,0},{3,1},{4,2},{5,3},{6,4},{7,5},{8,14},{9,15},{10,... | collective-permute-start | bytes 393224 | tf_op jit(solution)/shard_map/ppermute | solution.py:422
where the time goes:
time: 76.5 us; the launch traced here: 76 us
  starting transfers between devices  28 us (37%)
  waiting for transfers between devices  27.9 us (36%)
  Pallas kernels  13.2 us (17%)
  local copies, waits for them, and re-layouts  4.58 us (6%)
  between operations  1.44 us (2%)
  other arithmetic  0.77 us (1%)
    all_to_all x1, waiting for transfers between devices, on_device(): lax.all_to_all(block, 'flow', split_axis=0, concat_axis=0, tiled=True)  19.6 us
    all_to_all x1, starting transfers between devices, on_device(): lax.all_to_all(block, 'flow', split_axis=0, concat_axis=0, tiled=True)  13.1 us
    pallas_call x1, Pallas kernels, on_device(): kernel_call(scatter_kernel, 'scatter', [VMEM] * 6 + [SMEM], [tile] * 3, [...  8.27 us
    ppermute x3, starting transfers between devices, on_device(): lax.ppermute(total, 'lane', [(i, (i + k) % lanes) for i in range(lanes)])  5.07 us
    ppermute x3, waiting for transfers between devices, on_device(): lax.ppermute(total, 'lane', [(i, (i + k) % lanes) for i in range(lanes)])  5 us
    ppermute x1, starting transfers between devices, on_device(): lax.ppermute(total, 'lane', [(i, i ^ 1) for i in range(lanes)])  4.63 us
    unnamed x26, local copies, waits for them, and re-layouts  4.58 us
    ppermute x1, starting transfers between devices, on_device(): low = lax.ppermute(after, 'flow', [(i, i + 1) for i in range(devices - 1)])  3.94 us
  transfers between devices with their start and end apart: 7, of which 5 were waited for; matrix products, arithmetic and copies ran while one was open for 0% of the time, Pallas kernels for 2%

commit v1 on v0

--- a/solution.py
+++ b/solution.py
@@ -11,6 +11,7 @@
 SUBS = 8
 ROWS = 24
 F32 = jnp.float32
+BF16 = jnp.bfloat16
 
 
 def halves(fn, a):
@@ -130,7 +131,7 @@
 
 
 def scatter_kernel(cells_ref, area_ref, land_ref, bmp_ref, rain_ref, table_ref, live_ref,
-                   before_ref, own_ref, after_ref, amount_ref, acc_ref):
+                   before_ref, own_ref, after_ref, amount_ref, window_ref):
     slots = land_ref.shape[1]
     land = land_ref[...]
     rates = jnp.zeros((8, slots), F32)
@@ -144,30 +145,31 @@
     perc = jnp.where(alive, rain_ref[...] * chosen, 0.0)
     for q in range(4):
         amount = perc * area_ref[q : q + 1, :]
-        high = amount.astype(jnp.bfloat16).astype(F32)
+        high = amount.astype(BF16).astype(F32)
         amount_ref[q, 0:2, :] = high
         amount_ref[q, 2:4, :] = amount - high
-    acc_ref[...] = jnp.zeros_like(acc_ref)
-    width = 1024
-    column = lax.broadcasted_iota(jnp.int32, (128, width), 0)
-    line = lax.broadcasted_iota(jnp.int32, (192, width), 0)
+    column = lax.broadcasted_iota(jnp.int32, (256, slots), 0).astype(F32).astype(BF16)
+    line = lax.broadcasted_iota(jnp.int32, (96, slots), 0).astype(F32).astype(BF16)
+    one, zero = jnp.ones((), BF16), jnp.zeros((), BF16)
+    total = None
     for q in range(4):
-
-        @pl.loop(0, slots // width)
-        def _(c):
-            at = pl.ds(pl.multiple_of(c * width, width), width)
-            cell = cells_ref[q : q + 1, at]
-            hit = column == (cell & 127)
-            put = [jnp.where(hit, amount_ref[q, k : k + 1, at], 0.0).astype(jnp.bfloat16) for k in (0, 2, 1, 3)]
-            rows = jnp.where(line == (cell >> 7), 1.0, 0.0).astype(jnp.bfloat16)
-            acc_ref[...] += lax.dot_general(
-                jnp.concatenate(put, axis=0), rows, (((1,), (1,)), ((), ())), preferred_element_type=F32
-            )
-
-    lane0 = acc_ref[0:128, :] + acc_ref[128:256, :]
-    lane1 = acc_ref[256:384, :] + acc_ref[384:512, :]
+        cell = cells_ref[q : q + 1, :]
+        columns = jnp.where(column == (cell & 255).astype(F32).astype(BF16), one, zero)
+        hit = line == (cell >> 8).astype(F32).astype(BF16)
+        put = [jnp.where(hit, amount_ref[q, k : k + 1, :].astype(BF16), zero) for k in (0, 2, 1, 3)]
+        product = lax.dot_general(
+            jnp.concatenate(put, axis=0), columns, (((1,), (1,)), ((), ())), preferred_element_type=F32
+        )
+        total = product if total is None else total + product
+    for s in range(2):
+        summed = total[192 * s : 192 * s + 96] + total[192 * s + 96 : 192 * s + 192]
+        for k in range(3):
+            for odd in range(2):
+                window_ref[k, pl.ds(64 * s + odd, 32, stride=2), :] = summed[
+                    32 * k : 32 * k + 32, 128 * odd : 128 * odd + 128
+                ]
     for k, ref in enumerate((before_ref, own_ref, after_ref)):
-        ref[...] = jnp.concatenate([lane0[:, 64 * k : 64 * k + 64], lane1[:, 64 * k : 64 * k + 64]], axis=1)
+        ref[...] = window_ref[k].T
 
 
 def coefficient_kernel(head_ref, storage_ref, flow_ref, cross_ref, vert_ref, active_ref,
@@ -382,8 +384,17 @@
     slots = hru_land.shape[0]
     devices = lax.axis_size("flow")
     tile = (128, 128)
-    before, own, after = kernel_call(
-        scatter_kernel, "scatter", [VMEM] * 6 + [SMEM], [tile] * 3, [(4, 4, slots), (512, 192)], 4 * 10**9
+    blocks = [(4, slots), (4, slots), (1, slots), (2, slots), (1, slots), (8, 16)]
+    before, own, after = pl.pallas_call(
+        scatter_kernel,
+        name="scatter",
+        grid=(1,),
+        in_specs=[pl.BlockSpec(shape, lambda i: (0, 0)) for shape in blocks] + [SMEM],
+        out_specs=[pl.BlockSpec(tile, lambda i: (0, 0))] * 3,
+        out_shape=[jax.ShapeDtypeStruct(tile, F32)] * 3,
+        scratch_shapes=[pltpu.VMEM((4, 4, slots), F32), pltpu.VMEM((3,) + tile, F32)],
+        compiler_params=pltpu.CompilerParams(vmem_limit_bytes=60 * 2**20),
+        cost_estimate=pl.CostEstimate(flops=4 * 10**9, bytes_accessed=2 * 2**20, transcendentals=0),
     )(
         hru_cells.T, hru_area.T, hru_land.reshape(1, slots), hru_bmp, rain.reshape(1, slots), perc_table.T, hru_live
     )
@@ -405,8 +416,9 @@
         [tile],
         10**9,
     )(fields, small, base, own, low, high, coefs)
+    place = lax.axis_index("flow").astype(jnp.int32).reshape(1)
+    block, place = lax.optimization_barrier((block, place))
     gathered = lax.all_to_all(block, "flow", split_axis=0, concat_axis=0, tiled=True)
-    place = lax.axis_index("flow").astype(jnp.int32).reshape(1)
     head, total = kernel_call(
         sweep_kernel,
         "sweeps",

time: 76.5 us -> 70.4 us (0.920)
  blocking collectives: 0 us -> 32.5 us
  waiting for transfers between devices: 27.9 us -> 12.2 us
  starting transfers between devices: 28 us -> 13.8 us
  local copies, waits for them, and re-layouts: 4.58 us -> 0.04 us
  Pallas kernels: 13.2 us -> 9.4 us
    all_to_all x0 -> x1, blocking collectives: none -> 32.5 us  [on_device(): lax.all_to_all(block, 'flow', split_axis=0, concat_axis=0, tiled=True)]
    all_to_all x1 -> x0, waiting for transfers between devices: 19.6 us -> none  [on_device(): lax.all_to_all(block, 'flow', split_axis=0, concat_axis=0, tiled=True)]
    all_to_all x1 -> x0, starting transfers between devices: 13.1 us -> none  [on_device(): lax.all_to_all(block, 'flow', split_axis=0, concat_axis=0, tiled=True)]
    unnamed x26 -> x16, local copies, waits for them, and re-layouts: 4.58 us -> 0.04 us
    ppermute x3, waiting for transfers between devices: 5 us -> 8.69 us  [on_device(): lax.ppermute(total, 'lane', [(i, (i + k) % lanes) for i in range(lanes)])]
    pallas_call x1, Pallas kernels: 8.27 us -> 5.29 us  [on_device(): pl.pallas_call(scatter_kernel, name='scatter', grid=(1,), in_specs=[pl.Bl...]
    ppermute x3, starting transfers between devices: 5.07 us -> 3.85 us  [on_device(): lax.ppermute(total, 'lane', [(i, (i + k) % lanes) for i in range(lanes)])]
    pallas_call x1, Pallas kernels: 1.52 us -> 0.64 us  [on_device(): kernel_call(source_kernel, 'sources', [VMEM] * 7, [(2, STEPS, SUBS, 256),...]
  transfers between devices with their start and end apart: 7 -> 6, of which waited for: 5 -> 5; matrix products, arithmetic and copies ran while one was open for 0% -> 0% of each run, Pallas kernels for 2% -> 2%
where the time goes in v1:
time: 70.4 us; the launch traced here: 70.2 us
  blocking collectives  32.5 us (46%)
  starting transfers between devices  13.8 us (20%)
  waiting for transfers between devices  12.2 us (17%)
  Pallas kernels  9.4 us (13%)
  between operations  1.46 us (2%)
  other arithmetic  0.77 us (1%)
    all_to_all x1, blocking collectives, on_device(): lax.all_to_all(block, 'flow', split_axis=0, concat_axis=0, tiled=True)  32.5 us
    ppermute x3, waiting for transfers between devices, on_device(): lax.ppermute(total, 'lane', [(i, (i + k) % lanes) for i in range(lanes)])  8.69 us
    pallas_call x1, Pallas kernels, on_device(): pl.pallas_call(scatter_kernel, name='scatter', grid=(1,), in_specs=[pl.Bl...  5.29 us
    ppermute x1, starting transfers between devices, on_device(): lax.ppermute(total, 'lane', [(i, i ^ 1) for i in range(lanes)])  4.61 us
    ppermute x1, starting transfers between devices, on_device(): low = lax.ppermute(after, 'flow', [(i, i + 1) for i in range(devices - 1)])  3.93 us
    ppermute x3, starting transfers between devices, on_device(): lax.ppermute(total, 'lane', [(i, (i + k) % lanes) for i in range(lanes)])  3.85 us
    ppermute x1, waiting for transfers between devices, on_device(): lax.ppermute(before, 'flow', [(i + 1, i) for i in range(devices - 1)])  2.56 us
    pallas_call x1, Pallas kernels, on_device(): kernel_call(sweep_kernel, 'sweeps', [SMEM] + [VMEM] * 5, [head_prev.shape...  2.2 us
  transfers between devices with their start and end apart: 6, of which 5 were waited for; matrix products, arithmetic and copies ran while one was open for 0% of the time, Pallas kernels for 2%

profile of v1, /device:TPU:1, one launch (start us, length us, event | category | flops | bytes accessed | tf_op | source)
XLA Modules:
  0.0 70.2 jit_solution(11731418617847935764)
XLA Ops:
  1.3 5.3 %scatter.1 = (f32[128,128]{1,0:T(8,128)}, f32[128,128]{1,0:T(8,128)}, f32[128,128]{1,0:T(8,128)}) custom-call(s32[4,4096]{1,0:T(4,128)} %bitcast.8, f32[4,4096]{1,0:T(4,128)} %bitcast.9, s32[1,4096]{1,0:T(1,128)} %bitcast.10, s32[2,4096]{1,0:T(2,128)} %bmp_ref.1, f32[1,4096]{1,0:T(1,128)} %bitcast.11, f32[8,16]{1,0:T(8,128)} %bitcast.12, s32[1]{0:T(128)S(6)} %copy.15.live_ref), custom_call_target="tpu_custom_call" | custom-call | flops 4000000000 | bytes 2097152 | tf_op jit(solution)/shard_map/scatter/pallas_call | solution.py:388
  6.6 3.9 %collective-permute-start = (f32[128,128]{1,0:T(8,128)}, f32[128,128]{1,0:T(8,128)S(1)}, u32[]{:S(2)}, u32[]{:S(2)}) collective-permute-start(f32[128,128]{1,0:T(8,128)} %get-tuple-element.20), channel_id=1, source_target_pairs={{0,8},{8,16},{16,24},{24,32},{32,40},{40,48},{48,56},{56,64},{64,7... | collective-permute-start | bytes 196616 | tf_op jit(solution)/shard_map/ppermute | solution.py:402
  10.6 0.0 copy-start.6
  10.6 1.4 %collective-permute-start.1 = (f32[128,128]{1,0:T(8,128)}, f32[128,128]{1,0:T(8,128)S(1)}, u32[]{:S(2)}, u32[]{:S(2)}) collective-permute-start(f32[128,128]{1,0:T(8,128)} %get-tuple-element.21), channel_id=1, source_target_pairs={{8,0},{16,8},{24,16},{32,24},{40,32},{48,40},{56,48},{64,56},{72,6... | collective-permute-start | bytes 196616 | tf_op jit(solution)/shard_map/ppermute | solution.py:401
  12.0 0.0 copy-done
  12.0 0.0 copy-done.1
  12.0 0.0 copy-done.2
  12.0 0.0 copy-done.3
  12.1 1.3 %coefficients.1 = (f32[8,16,8,256]{3,2,1,0:T(8,128)S(1)}, f32[3,16,256]{2,1,0:T(8,128)S(1)}, f32[4,16,8,256]{3,2,1,0:T(8,128)S(1)}, f32[16,256]{1,0:T(8,128)S(1)}) custom-call(f32[2,4,64,128]{3,2,1,0:T(8,128)S(1)} %copy-done, f32[4,64,128]{2,1,0:T(8,128)S(1)} %copy-done.1, f32[4,64,128]{2,1,0:T(8,128)S(1)} %copy-done.2, f32[4,64,128]{2,1,0:T(8,128)S(1)} %copy-done.3, ...), custom_call_target="tpu_custom_call" | custom-call | flops 4000000000 | bytes 2097152 | tf_op jit(solution)/shard_map/coefficients/pallas_call | solution.py:403
  13.4 0.0 collective-permute-done.low_ref
  13.4 2.6 %collective-permute-done.1.high_ref = f32[128,128]{1,0:T(8,128)S(1)} collective-permute-done((f32[128,128]{1,0:T(8,128)}, f32[128,128]{1,0:T(8,128)S(1)}, u32[]{:S(2)}, u32[]{:S(2)}) %collective-permute-start.1) | collective-permute-done | bytes 65568 | tf_op jit(solution)/shard_map/ppermute | solution.py:401
  15.9 0.6 sources.1
  16.6 32.5 %all_to_all.5 = f32[32,48,128]{2,1,0:T(8,128)S(1)} all-to-all(f32[32,48,128]{2,1,0:T(8,128)S(1)} %get-tuple-element.25), channel_id=1, replica_groups=mesh['flow'=32,'lane'=8] {'flow'}, dimensions={0} | all-to-all | bytes 1572864 | tf_op jit(solution)/shard_map/all_to_all | solution.py:421
  49.1 2.2 %sweeps.1 = (f32[2,4,64,128]{3,2,1,0:T(8,128)}, f32[4,64,128]{2,1,0:T(8,128)S(1)}) custom-call(s32[1]{0:T(128)} %bitcast.5.place_ref, f32[1536,128]{1,0:T(8,128)S(1)} %bitcast.7, f32[8,16,8,256]{3,2,1,0:T(8,128)S(1)} %get-tuple-element.16.fields_ref, f32[3,16,256]{2,1,0:T(8,128)S(1)} %get-tuple-element.17.small_ref, ...), custom_call_target="tpu_custom_call" | custom-call | flops 1000000000 | bytes 2097152 | tf_op jit(solution)/shard_map/sweeps/pallas_call | solution.py:422
  51.3 4.6 %collective-permute-start.2 = (f32[4,64,128]{2,1,0:T(8,128)S(1)}, f32[4,64,128]{2,1,0:T(8,128)S(1)}, u32[]{:S(2)}, u32[]{:S(2)}) collective-permute-start(f32[4,64,128]{2,1,0:T(8,128)S(1)} %get-tuple-element.29), channel_id=1, source_target_pairs={{0,1},{1,0},{2,3},{3,2},{4,5},{5,4},{6,7},{7,6},{8,9},{9,8},{10,11... | collective-permute-start | bytes 393224 | tf_op jit(solution)/shard_map/ppermute | solution.py:431
  55.9 1.0 %collective-permute-done.2 = f32[4,64,128]{2,1,0:T(8,128)S(1)} collective-permute-done((f32[4,64,128]{2,1,0:T(8,128)S(1)}, f32[4,64,128]{2,1,0:T(8,128)S(1)}, u32[]{:S(2)}, u32[]{:S(2)}) %collective-permute-start.2) | collective-permute-done | bytes 131104 | tf_op jit(solution)/shard_map/ppermute | solution.py:431
  56.9 0.0 copy-start.7
  56.9 2.8 %collective-permute-start.5 = (f32[4,64,128]{2,1,0:T(8,128)S(1)}, f32[4,64,128]{2,1,0:T(8,128)S(1)}, u32[]{:S(2)}, u32[]{:S(2)}) collective-permute-start(f32[4,64,128]{2,1,0:T(8,128)S(1)} %add.12), channel_id=1, source_target_pairs={{0,6},{1,7},{2,0},{3,1},{4,2},{5,3},{6,4},{7,5},{8,14},{9,15},{10,... | collective-permute-start | bytes 393224 | tf_op jit(solution)/shard_map/ppermute | solution.py:434
  59.7 0.3 collective-permute-start.4
  60.1 0.7 collective-permute-start.3
  60.8 4.1 %collective-permute-done.5 = f32[4,64,128]{2,1,0:T(8,128)S(1)} collective-permute-done((f32[4,64,128]{2,1,0:T(8,128)S(1)}, f32[4,64,128]{2,1,0:T(8,128)S(1)}, u32[]{:S(2)}, u32[]{:S(2)}) %collective-permute-start.5) | collective-permute-done | bytes 131104 | tf_op jit(solution)/shard_map/ppermute | solution.py:434
  64.9 0.7 %collective-permute-done.4 = f32[4,64,128]{2,1,0:T(8,128)S(1)} collective-permute-done((f32[4,64,128]{2,1,0:T(8,128)S(1)}, f32[4,64,128]{2,1,0:T(8,128)S(1)}, u32[]{:S(2)}, u32[]{:S(2)}) %collective-permute-start.4) | collective-permute-done | bytes 131104 | tf_op jit(solution)/shard_map/ppermute | solution.py:434
  65.6 3.8 %collective-permute-done.3 = f32[4,64,128]{2,1,0:T(8,128)S(1)} collective-permute-done((f32[4,64,128]{2,1,0:T(8,128)S(1)}, f32[4,64,128]{2,1,0:T(8,128)S(1)}, u32[]{:S(2)}, u32[]{:S(2)}) %collective-permute-start.3) | collective-permute-done | bytes 131104 | tf_op jit(solution)/shard_map/ppermute | solution.py:434
  69.5 0.7 %broadcast_subtract_fusion = f32[2,4,64,128]{3,2,1,0:T(8,128)} fusion(f32[2,4,64,128]{3,2,1,0:T(8,128)S(1)} %copy-done.7, f32[4,64,128]{2,1,0:T(8,128)S(1)} %add_multiply_fusion), kind=kLoop, calls=%fused_computation | loop fusion | flops 65536 | bytes 655360 | tf_op jit(solution)/shard_map/sub | solution.py:435
  (12 shorter events, 0.1 us)
Async XLA Ops:
  1.3 10.7 %copy-start = (f32[2,4,64,128]{3,2,1,0:T(8,128)S(1)}, f32[2,4,64,128]{3,2,1,0:T(8,128)}, u32[]{:S(2)}) copy-start(f32[2,4,64,128]{3,2,1,0:T(8,128)} %head_ref.1) | copy-start | bytes 786436
  1.3 10.7 %copy-start.1 = (f32[4,64,128]{2,1,0:T(8,128)S(1)}, f32[4,64,128]{2,1,0:T(8,128)}, u32[]{:S(2)}) copy-start(f32[4,64,128]{2,1,0:T(8,128)} %storage_ref.1) | copy-start | bytes 393220
  1.3 10.7 %copy-start.2 = (f32[4,64,128]{2,1,0:T(8,128)S(1)}, f32[4,64,128]{2,1,0:T(8,128)}, u32[]{:S(2)}) copy-start(f32[4,64,128]{2,1,0:T(8,128)} %flow_ref.1) | copy-start | bytes 393220
  1.3 10.7 %copy-start.3 = (f32[4,64,128]{2,1,0:T(8,128)S(1)}, f32[4,64,128]{2,1,0:T(8,128)}, u32[]{:S(2)}) copy-start(f32[4,64,128]{2,1,0:T(8,128)} %cross_ref.1) | copy-start | bytes 393220
  1.3 10.7 %copy-start.4 = (f32[4,64,128]{2,1,0:T(8,128)S(1)}, f32[4,64,128]{2,1,0:T(8,128)}, u32[]{:S(2)}) copy-start(f32[4,64,128]{2,1,0:T(8,128)} %vert_ref.1) | copy-start | bytes 393220
  1.3 10.7 %copy-start.5 = (s32[4,64,128]{2,1,0:T(8,128)S(1)}, s32[4,64,128]{2,1,0:T(8,128)}, u32[]{:S(2)}) copy-start(s32[4,64,128]{2,1,0:T(8,128)} %active_ref.1) | copy-start | bytes 393220
  6.6 6.7 %collective-permute-start = (f32[128,128]{1,0:T(8,128)}, f32[128,128]{1,0:T(8,128)S(1)}, u32[]{:S(2)}, u32[]{:S(2)}) collective-permute-start(f32[128,128]{1,0:T(8,128)} %get-tuple-element.20), channel_id=1, source_target_pairs={{0,8},{8,16},{16,24},{24,32},{32,40},{40,48},{48,56},{56,64},{64,7... | collective-permute-start | bytes 196616 | tf_op jit(solution)/shard_map/ppermute | solution.py:402
  10.6 5.4 %copy-start.6 = (f32[128,128]{1,0:T(8,128)S(1)}, f32[128,128]{1,0:T(8,128)}, u32[]{:S(2)}) copy-start(f32[128,128]{1,0:T(8,128)} %get-tuple-element.19.own_ref) | copy-start | bytes 196612
  10.6 5.4 %collective-permute-start.1 = (f32[128,128]{1,0:T(8,128)}, f32[128,128]{1,0:T(8,128)S(1)}, u32[]{:S(2)}, u32[]{:S(2)}) collective-permute-start(f32[128,128]{1,0:T(8,128)} %get-tuple-element.21), channel_id=1, source_target_pairs={{8,0},{16,8},{24,16},{32,24},{40,32},{48,40},{56,48},{64,56},{72,6... | collective-permute-start | bytes 196616 | tf_op jit(solution)/shard_map/ppermute | solution.py:401
  51.3 5.6 %collective-permute-start.2 = (f32[4,64,128]{2,1,0:T(8,128)S(1)}, f32[4,64,128]{2,1,0:T(8,128)S(1)}, u32[]{:S(2)}, u32[]{:S(2)}) collective-permute-start(f32[4,64,128]{2,1,0:T(8,128)S(1)} %get-tuple-element.29), channel_id=1, source_target_pairs={{0,1},{1,0},{2,3},{3,2},{4,5},{5,4},{6,7},{7,6},{8,9},{9,8},{10,11... | collective-permute-start | bytes 393224 | tf_op jit(solution)/shard_map/ppermute | solution.py:431
  56.9 12.6 %copy-start.7 = (f32[2,4,64,128]{3,2,1,0:T(8,128)S(1)}, f32[2,4,64,128]{3,2,1,0:T(8,128)}, u32[]{:S(2)}) copy-start(f32[2,4,64,128]{3,2,1,0:T(8,128)} %get-tuple-element.14) | copy-start | bytes 786436
  56.9 8.0 %collective-permute-start.5 = (f32[4,64,128]{2,1,0:T(8,128)S(1)}, f32[4,64,128]{2,1,0:T(8,128)S(1)}, u32[]{:S(2)}, u32[]{:S(2)}) collective-permute-start(f32[4,64,128]{2,1,0:T(8,128)S(1)} %add.12), channel_id=1, source_target_pairs={{0,6},{1,7},{2,0},{3,1},{4,2},{5,3},{6,4},{7,5},{8,14},{9,15},{10,... | collective-permute-start | bytes 393224 | tf_op jit(solution)/shard_map/ppermute | solution.py:434
  59.7 5.9 %collective-permute-start.4 = (f32[4,64,128]{2,1,0:T(8,128)S(1)}, f32[4,64,128]{2,1,0:T(8,128)S(1)}, u32[]{:S(2)}, u32[]{:S(2)}) collective-permute-start(f32[4,64,128]{2,1,0:T(8,128)S(1)} %add.12), channel_id=1, source_target_pairs={{0,4},{1,5},{2,6},{3,7},{4,0},{5,1},{6,2},{7,3},{8,12},{9,13},{10,... | collective-permute-start | bytes 393224 | tf_op jit(solution)/shard_map/ppermute | solution.py:434
  60.1 9.4 %collective-permute-start.3 = (f32[4,64,128]{2,1,0:T(8,128)S(1)}, f32[4,64,128]{2,1,0:T(8,128)S(1)}, u32[]{:S(2)}, u32[]{:S(2)}) collective-permute-start(f32[4,64,128]{2,1,0:T(8,128)S(1)} %add.12), channel_id=1, source_target_pairs={{0,2},{1,3},{2,4},{3,5},{4,6},{5,7},{6,0},{7,1},{8,10},{9,11},{10,... | collective-permute-start | bytes 393224 | tf_op jit(solution)/shard_map/ppermute | solution.py:434

commit v2 on v1

--- a/solution.py
+++ b/solution.py
@@ -281,59 +281,117 @@
             for k in range(2):
                 sums[k] = sums[k] + fields_ref[6 + k, i] * later
         rows += [first, last, column_sum(sums[0]), column_sum(sums[1])]
-    head = coefs_ref[0:13]
-    block = jnp.concatenate([head] + rows + [jnp.zeros((3, 256), F32)], axis=0)
+    put_block(out_ref, [coefs_ref[k : k + 1] for k in range(13)] + rows)
+
+
+def put_block(ref, rows):
+    for k in range(ROWS):
+        row = rows[k] if k < len(rows) else jnp.zeros((1, 256), F32)
+        for h in range(2):
+            ref[ROWS * h + k : ROWS * h + k + 1] = row[:, 128 * h : 128 * h + 128]
+
+
+def coupled_ends(got, later, low, high):
+    for row, ahead, back in ((5, cross_next, cross_prev), (9, layer_next, layer_prev)):
+        k = [got(row + m) for m in range(4)]
+        low_ahead, high_ahead = ahead(low), ahead(high)
+        later = (
+            later[0] + k[0] * low_ahead + k[1] * high_ahead + back(k[0] * low + k[2] * high),
+            later[1] + k[2] * low_ahead + k[3] * high_ahead + back(k[1] * low + k[3] * high),
+        )
+    return later
+
+
+def member(blocks_ref, p):
+    return lambda row: both(lambda h: blocks_ref[p, ROWS * h + row : ROWS * h + row + 1, :])
+
+
+def group_later(blocks_ref, s, nodes):
+    out = []
+    for p in range(blocks_ref.shape[0]):
+        got = member(blocks_ref, p)
+        out += coupled_ends(got, (got(15 + 4 * s), got(16 + 4 * s)), nodes[2 * p], nodes[2 * p + 1])
+    return out
+
+
+def group_kernel(place_ref, own_ref, from1_ref, from2_ref, from3_ref, blocks_ref, saved_ref, out_ref, block):
+    per = blocks_ref.shape[0]
+    place = lax.rem(place_ref[0], per)
+    for k, ref in enumerate((own_ref, from1_ref, from2_ref, from3_ref)):
+        blocks_ref[lax.rem(place + per - k, per)] = ref[...]
+    got = [member(blocks_ref, p) for p in range(per)]
+    leak, face = [], []
+    for p in range(per):
+        leak += [got[p](0), got[p](1)]
+        face.append(got[p](2))
+        if p + 1 < per:
+            face.append(got[p](3) * got[p + 1](4))
+    coef, first, last, link = reduce_chain(leak, face)
+    nodes = 2 * per
+    one, zero = jnp.ones((1, 256), F32), jnp.zeros((1, 256), F32)
+    basis = [fill_chain(coef, None, one, zero), fill_chain(coef, None, zero, one)]
+    for k in range(3):
+        for i in range(1, nodes - 1):
+            saved_ref[nodes * k + i : nodes * k + i + 1] = coef[k][i]
+    rows = [first, last, link, got[per - 1](3), got[0](4)]
+    for row, move in ((5, cross_next), (9, layer_next)):
+        sums = [zero] * 4
+        for p in range(per):
+            moved = [[move(basis[b][2 * p + e]) for e in range(2)] for b in range(2)]
+            k = [got[p](row + m) for m in range(4)]
+            for b in range(2):
+                ends = [k[2 * e] * moved[b][0] + k[2 * e + 1] * moved[b][1] for e in range(2)]
+                for a in range(2):
+                    sums[2 * a + b] = sums[2 * a + b] + basis[a][2 * p] * ends[0] + basis[a][2 * p + 1] * ends[1]
+        rows += sums
+    for s in range(2):
+        rhs = [got[p](13 + 4 * s + e) for p in range(per) for e in range(2)]
+        part, source_first, source_last = reduce_source(coef[1], coef[2], rhs)
+        inner = fill_chain(coef, part, zero, zero)
+        _, later_first, later_last = reduce_source(coef[1], coef[2], group_later(blocks_ref, s, inner))
+        rows += [source_first, source_last, later_first, later_last]
+        for i in range(nodes):
+            saved_ref[nodes * (5 + s) + i : nodes * (5 + s) + i + 1] = inner[i]
+            saved_ref[nodes * (3 + s) + i : nodes * (3 + s) + i + 1] = basis[s][i]
+    put_block(block, rows)
     for k in range(out_ref.shape[0]):
-        for h in range(2):
-            out_ref[k, ROWS * h : ROWS * h + ROWS] = block[:, 128 * h : 128 * h + 128]
-
-
-def sweep_kernel(place_ref, gathered_ref, fields_ref, small_ref, source_ref, inner_ref,
+        out_ref[k] = block[...]
+
+
+def sweep_kernel(place_ref, gathered_ref, blocks_ref, saved_ref, fields_ref, small_ref, source_ref, inner_ref,
                  head_ref, total_ref, ends_scratch, turned):
-    devices = gathered_ref.shape[0] // (2 * ROWS)
-    per = devices // SUBS
-
-    def got(row, i):
-        return both(lambda h: gathered_ref[pl.ds((2 * i + h) * ROWS + row, SUBS, stride=2 * per * ROWS), :])
-
-    leak, face = [], []
-    for i in range(per):
-        leak += [got(0, i), got(1, i)]
-        after = got(4, i + 1) if i + 1 < per else pltpu.roll(got(4, 0), SUBS - 1, 0)
-        face += [got(2, i), got(3, i) * after]
-    coef, first, last, link = reduce_chain(leak, face[: 2 * per - 1])
-    leak1 = interleave(first, last)
-    face1 = interleave(link, face[2 * per - 1])[: 2 * SUBS - 1]
-    inv1, ratio1 = full_factor(leak1, face1)
-
-    def across_devices(rhs):
-        part, ends_first, ends_last = reduce_source(coef[1], coef[2], rhs)
-        ends = full_solve(inv1, ratio1, interleave(ends_first, ends_last))
-        return fill_chain(coef, part, *stack_ends(ends))
-
-    cross_k = [[got(5 + k, i) for k in range(4)] for i in range(per)]
-    vert_k = [[got(9 + k, i) for k in range(4)] for i in range(per)]
+    per = blocks_ref.shape[0]
+    groups = gathered_ref.shape[0] // (2 * ROWS)
+    place = place_ref[0]
+
+    def got(row):
+        return both(lambda h: gathered_ref[pl.ds(ROWS * h + row, groups, stride=2 * ROWS), :])
+
+    face = got(3) * pltpu.roll(got(4), groups - 1, 0)
+    inv, ratio = full_factor(interleave(got(0), got(1)), interleave(got(2), face)[: 2 * groups - 1])
+    nodes = 2 * per
+    saved = [[saved_ref[nodes * k + i : nodes * k + i + 1] for i in range(nodes)] for k in range(7)]
+    at = pl.ds(place // per, 1)
+    pick = pl.ds(lax.rem(place, per), 1)
+    ends = []
     for s in range(2):
         row = 13 + 4 * s
-        ends = across_devices([got(row + a, i) for i in range(per) for a in range(2)])
-        rhs = []
-        for i in range(per):
-            low, high = ends[2 * i], ends[2 * i + 1]
-            later = [got(row + 2 + a, i) for a in range(2)]
-            for k, ahead, back in ((cross_k[i], cross_next, cross_prev), (vert_k[i], layer_next, layer_prev)):
-                low_ahead, high_ahead = ahead(low), ahead(high)
-                later[0] = later[0] + k[0] * low_ahead + k[1] * high_ahead + back(k[0] * low + k[2] * high)
-                later[1] = later[1] + k[2] * low_ahead + k[3] * high_ahead + back(k[1] * low + k[3] * high)
-            rhs += later
-        ends2 = across_devices(rhs)
-        for i in range(per):
-            for k, value in enumerate((ends[2 * i], ends[2 * i + 1], ends2[2 * i], ends2[2 * i + 1])):
-                ends_scratch[4 * s + k, SUBS * i : SUBS * i + SUBS] = value
+        low, high = stack_ends(full_solve(inv, ratio, interleave(got(row), got(row + 1))))
+        later = coupled_ends(got, (got(row + 2), got(row + 3)), low, high)
+        low2, high2 = stack_ends(full_solve(inv, ratio, interleave(*later)))
+        for k, value in enumerate((low, high, low2, high2)):
+            ends_scratch[k] = value
+        low, high, low2, high2 = [ends_scratch[k, at, :] for k in range(4)]
+        first = [saved[5 + s][i] + saved[3][i] * low + saved[4][i] * high for i in range(nodes)]
+        part, _, _ = reduce_source(saved[1], saved[2], group_later(blocks_ref, s, first))
+        second = fill_chain(tuple(saved[:3]), part, low2, high2)
+        for k, values in enumerate((first[0::2], first[1::2], second[0::2], second[1::2])):
+            for p in range(per):
+                ends_scratch[k, p : p + 1] = values[p]
+        ends.append([ends_scratch[k, pick, :] for k in range(4)])
     coef, coef1 = load_coef(fields_ref, small_ref)
-    place = place_ref[0]
-    at = pl.ds((place % per) * SUBS + place // per, 1)
     for s in range(2):
-        low1, high1, low2, high2 = [ends_scratch[4 * s + k, at, :] for k in range(4)]
+        low1, high1, low2, high2 = ends[s]
         rhs = []
         for i in range(STEPS):
             head = inner_ref[s, i] + fields_ref[6, i] * low1 + fields_ref[7, i] * high1
@@ -412,21 +470,33 @@
         source_kernel,
         "sources",
         [VMEM] * 7,
-        [(2, STEPS, SUBS, 256), (2, STEPS, SUBS, 256), (devices, 2 * ROWS, 128)],
+        [(2, STEPS, SUBS, 256), (2, STEPS, SUBS, 256), (2 * ROWS, 128)],
         [tile],
         10**9,
     )(fields, small, base, own, low, high, coefs)
     place = lax.axis_index("flow").astype(jnp.int32).reshape(1)
-    block, place = lax.optimization_barrier((block, place))
-    gathered = lax.all_to_all(block, "flow", split_axis=0, concat_axis=0, tiled=True)
+    per = devices // SUBS
+    around = [
+        lax.ppermute(block, "flow", [(i, i - i % per + (i + k) % per) for i in range(devices)]) for k in range(1, per)
+    ]
+    blocks, saved, block = kernel_call(
+        group_kernel,
+        "groups",
+        [SMEM] + [VMEM] * per,
+        [(per, 2 * ROWS, 128), (14 * per, 256), (SUBS, 2 * ROWS, 128)],
+        [(2 * ROWS, 128)],
+        10**9,
+    )(place, block, *around)
+    same = [[i + per * k for k in range(SUBS)] for i in range(per)]
+    gathered = lax.all_to_all(block, "flow", split_axis=0, concat_axis=0, axis_index_groups=same, tiled=True)
     head, total = kernel_call(
         sweep_kernel,
         "sweeps",
-        [SMEM] + [VMEM] * 5,
+        [SMEM] + [VMEM] * 7,
         [head_prev.shape, storage.shape],
-        [(8, devices, 256), (2, 2, 128, 128)],
+        [(4, SUBS, 256), (2, 2, 128, 128)],
         10**9,
-    )(place, gathered.reshape(devices * 2 * ROWS, 128), fields, small, source, inner)
+    )(place, gathered.reshape(SUBS * 2 * ROWS, 128), blocks, saved, fields, small, source, inner)
     lanes = lax.axis_size("lane")
     total = total + lax.ppermute(total, "lane", [(i, i ^ 1) for i in range(lanes)])
     whole = total

time: 70.4 us -> 61.7 us (0.88)
  blocking collectives: 32.5 us -> 16.6 us
  starting transfers between devices: 13.8 us -> 21.8 us
  waiting for transfers between devices: 12.2 us -> 11.2 us
    all_to_all x1, blocking collectives: 32.5 us -> 16.6 us  [on_device(): lax.all_to_all(block, 'flow', split_axis=0, concat_axis=0, axis_index_gro...]
    ppermute x0 -> x3, starting transfers between devices: none -> 6.19 us  [on_device(): lax.ppermute(block, 'flow', [(i, i - i % per + (i + k) % per) for i in ra...]
    ppermute x3, waiting for transfers between devices: 8.69 us -> 5 us  [on_device(): lax.ppermute(total, 'lane', [(i, (i + k) % lanes) for i in range(lanes)])]
    ppermute x0 -> x3, waiting for transfers between devices: none -> 2.67 us  [on_device(): lax.ppermute(block, 'flow', [(i, i - i % per + (i + k) % per) for i in ra...]
    ppermute x3, starting transfers between devices: 3.85 us -> 5.06 us  [on_device(): lax.ppermute(total, 'lane', [(i, (i + k) % lanes) for i in range(lanes)])]
    pallas_call x1 -> x2, Pallas kernels: 2.2 us -> 2.52 us  [the longest x1 2.15 us: on_device(): kernel_call(sweep_kernel, 'sweeps', [SMEM] + [VMEM] * 7, [head_prev.shape...]
  transfers between devices with their start and end apart: 6 -> 9, of which waited for: 5 -> 6; matrix products, arithmetic and copies ran while one was open for 0% -> 0% of each run, Pallas kernels for 2% -> 2%
where the time goes in v2:
time: 61.7 us; the launch traced here: 61.5 us
  starting transfers between devices  21.8 us (35%)
  blocking collectives  16.6 us (27%)
  waiting for transfers between devices  11.2 us (18%)
  Pallas kernels  9.69 us (16%)
  between operations  1.45 us (2%)
  other arithmetic  0.78 us (1%)
    all_to_all x1, blocking collectives, on_device(): lax.all_to_all(block, 'flow', split_axis=0, concat_axis=0, axis_index_gro...  16.6 us
    ppermute x3, starting transfers between devices, on_device(): lax.ppermute(block, 'flow', [(i, i - i % per + (i + k) % per) for i in ra...  6.19 us
    pallas_call x1, Pallas kernels, on_device(): pl.pallas_call(scatter_kernel, name='scatter', grid=(1,), in_specs=[pl.Bl...  5.28 us
    ppermute x1, starting transfers between devices, on_device(): lax.ppermute(total, 'lane', [(i, i ^ 1) for i in range(lanes)])  5.14 us
    ppermute x3, starting transfers between devices, on_device(): lax.ppermute(total, 'lane', [(i, (i + k) % lanes) for i in range(lanes)])  5.06 us
    ppermute x3, waiting for transfers between devices, on_device(): lax.ppermute(total, 'lane', [(i, (i + k) % lanes) for i in range(lanes)])  5 us
    ppermute x1, starting transfers between devices, on_device(): low = lax.ppermute(after, 'flow', [(i, i + 1) for i in range(devices - 1)])  3.93 us
    ppermute x3, waiting for transfers between devices, on_device(): lax.ppermute(block, 'flow', [(i, i - i % per + (i + k) % per) for i in ra...  2.67 us
  transfers between devices with their start and end apart: 9, of which 6 were waited for; matrix products, arithmetic and copies ran while one was open for 0% of the time, Pallas kernels for 2%

profile of v2, /device:TPU:1, one launch (start us, length us, event | category | flops | bytes accessed | tf_op | source)
XLA Modules:
  0.0 61.5 jit_solution(4825941887764293156)
XLA Ops:
  1.3 5.3 %scatter.1 = (f32[128,128]{1,0:T(8,128)}, f32[128,128]{1,0:T(8,128)}, f32[128,128]{1,0:T(8,128)}) custom-call(s32[4,4096]{1,0:T(4,128)} %bitcast.8, f32[4,4096]{1,0:T(4,128)} %bitcast.9, s32[1,4096]{1,0:T(1,128)} %bitcast.10, s32[2,4096]{1,0:T(2,128)} %bmp_ref.1, f32[1,4096]{1,0:T(1,128)} %bitcast.11, f32[8,16]{1,0:T(8,128)} %bitcast.12, s32[1]{0:T(128)S(6)} %copy.15.live_ref), custom_call_target="tpu_custom_call" | custom-call | flops 4000000000 | bytes 2097152 | tf_op jit(solution)/shard_map/scatter/pallas_call | solution.py:446
  6.6 3.9 %collective-permute-start = (f32[128,128]{1,0:T(8,128)}, f32[128,128]{1,0:T(8,128)S(1)}, u32[]{:S(2)}, u32[]{:S(2)}) collective-permute-start(f32[128,128]{1,0:T(8,128)} %get-tuple-element.21), channel_id=1, source_target_pairs={{0,8},{8,16},{16,24},{24,32},{32,40},{40,48},{48,56},{56,64},{64,7... | collective-permute-start | bytes 196616 | tf_op jit(solution)/shard_map/ppermute | solution.py:460
  10.6 0.0 copy-start.6
  10.6 1.4 %collective-permute-start.1 = (f32[128,128]{1,0:T(8,128)}, f32[128,128]{1,0:T(8,128)S(1)}, u32[]{:S(2)}, u32[]{:S(2)}) collective-permute-start(f32[128,128]{1,0:T(8,128)} %get-tuple-element.22), channel_id=1, source_target_pairs={{8,0},{16,8},{24,16},{32,24},{40,32},{48,40},{56,48},{64,56},{72,6... | collective-permute-start | bytes 196616 | tf_op jit(solution)/shard_map/ppermute | solution.py:459
  12.1 1.3 %coefficients.1 = (f32[8,16,8,256]{3,2,1,0:T(8,128)S(1)}, f32[3,16,256]{2,1,0:T(8,128)S(1)}, f32[4,16,8,256]{3,2,1,0:T(8,128)S(1)}, f32[16,256]{1,0:T(8,128)S(1)}) custom-call(f32[2,4,64,128]{3,2,1,0:T(8,128)S(1)} %copy-done, f32[4,64,128]{2,1,0:T(8,128)S(1)} %copy-done.1, f32[4,64,128]{2,1,0:T(8,128)S(1)} %copy-done.2, f32[4,64,128]{2,1,0:T(8,128)S(1)} %copy-done.3, ...), custom_call_target="tpu_custom_call" | custom-call | flops 4000000000 | bytes 2097152 | tf_op jit(solution)/shard_map/coefficients/pallas_call | solution.py:461
  13.4 2.6 %collective-permute-done.1.high_ref = f32[128,128]{1,0:T(8,128)S(1)} collective-permute-done((f32[128,128]{1,0:T(8,128)}, f32[128,128]{1,0:T(8,128)S(1)}, u32[]{:S(2)}, u32[]{:S(2)}) %collective-permute-start.1) | collective-permute-done | bytes 65568 | tf_op jit(solution)/shard_map/ppermute | solution.py:459
  15.9 0.6 sources.1
  16.6 1.3 %collective-permute-start.2 = (f32[48,128]{1,0:T(8,128)S(1)}, f32[48,128]{1,0:T(8,128)S(1)}, u32[]{:S(2)}, u32[]{:S(2)}) collective-permute-start(f32[48,128]{1,0:T(8,128)S(1)} %get-tuple-element.24.own_ref), channel_id=1, source_target_pairs={{0,8},{8,16},{16,24},{24,0},{32,40},{40,48},{48,56},{56,32},{64,72... | collective-permute-start | bytes 73736 | tf_op jit(solution)/shard_map/ppermute | solution.py:480
  17.8 4.9 %collective-permute-start.3 = (f32[48,128]{1,0:T(8,128)S(1)}, f32[48,128]{1,0:T(8,128)S(1)}, u32[]{:S(2)}, u32[]{:S(2)}) collective-permute-start(f32[48,128]{1,0:T(8,128)S(1)} %get-tuple-element.24.own_ref), channel_id=1, source_target_pairs={{0,16},{8,24},{16,0},{24,8},{32,48},{40,56},{48,32},{56,40},{64,80... | collective-permute-start | bytes 73736 | tf_op jit(solution)/shard_map/ppermute | solution.py:480
  22.7 0.0 collective-permute-done.2.from1_ref
  22.8 1.4 %collective-permute-done.3.from2_ref = f32[48,128]{1,0:T(8,128)S(1)} collective-permute-done((f32[48,128]{1,0:T(8,128)S(1)}, f32[48,128]{1,0:T(8,128)S(1)}, u32[]{:S(2)}, u32[]{:S(2)}) %collective-permute-start.3) | collective-permute-done | bytes 24608 | tf_op jit(solution)/shard_map/ppermute | solution.py:480
  24.2 1.2 %collective-permute-done.4.from3_ref = f32[48,128]{1,0:T(8,128)S(1)} collective-permute-done((f32[48,128]{1,0:T(8,128)S(1)}, f32[48,128]{1,0:T(8,128)S(1)}, u32[]{:S(2)}, u32[]{:S(2)}) %collective-permute-start.4) | collective-permute-done | bytes 24608 | tf_op jit(solution)/shard_map/ppermute | solution.py:480
  25.4 0.4 groups.1
  25.8 16.6 %all_to_all.5 = f32[8,48,128]{2,1,0:T(8,128)S(1)} all-to-all(f32[8,48,128]{2,1,0:T(8,128)S(1)} %get-tuple-element.25), channel_id=1, replica_groups={{0,32,64,96,128,160,192,224},{8,40,72,104,136,168,200,232},{16,48,80,11..., dimensions={0} | all-to-all | bytes 393216 | tf_op jit(solution)/shard_map/all_to_all | solution.py:491
  42.4 2.1 %sweeps.1 = (f32[2,4,64,128]{3,2,1,0:T(8,128)}, f32[4,64,128]{2,1,0:T(8,128)S(1)}) custom-call(s32[1]{0:T(128)} %bitcast.place_ref, f32[384,128]{1,0:T(8,128)S(1)} %bitcast.7, f32[4,48,128]{2,1,0:T(8,128)S(1)} %get-tuple-element.26.blocks_ref, f32[56,256]{1,0:T(8,128)S(1)} %get-tuple-element.27.saved_ref, ...), custom_call_target="tpu_custom_call" | custom-call | flops 1000000000 | bytes 2097152 | tf_op jit(solution)/shard_map/sweeps/pallas_call | solution.py:492
  44.5 5.1 %collective-permute-start.5 = (f32[4,64,128]{2,1,0:T(8,128)S(1)}, f32[4,64,128]{2,1,0:T(8,128)S(1)}, u32[]{:S(2)}, u32[]{:S(2)}) collective-permute-start(f32[4,64,128]{2,1,0:T(8,128)S(1)} %get-tuple-element.31), channel_id=1, source_target_pairs={{0,1},{1,0},{2,3},{3,2},{4,5},{5,4},{6,7},{7,6},{8,9},{9,8},{10,11... | collective-permute-start | bytes 393224 | tf_op jit(solution)/shard_map/ppermute | solution.py:501
  49.7 1.0 %collective-permute-done.5 = f32[4,64,128]{2,1,0:T(8,128)S(1)} collective-permute-done((f32[4,64,128]{2,1,0:T(8,128)S(1)}, f32[4,64,128]{2,1,0:T(8,128)S(1)}, u32[]{:S(2)}, u32[]{:S(2)}) %collective-permute-start.5) | collective-permute-done | bytes 131104 | tf_op jit(solution)/shard_map/ppermute | solution.py:501
  50.7 0.0 copy-start.7
  50.7 1.4 %collective-permute-start.6 = (f32[4,64,128]{2,1,0:T(8,128)S(1)}, f32[4,64,128]{2,1,0:T(8,128)S(1)}, u32[]{:S(2)}, u32[]{:S(2)}) collective-permute-start(f32[4,64,128]{2,1,0:T(8,128)S(1)} %add.12), channel_id=1, source_target_pairs={{0,2},{1,3},{2,4},{3,5},{4,6},{5,7},{6,0},{7,1},{8,10},{9,11},{10,... | collective-permute-start | bytes 393224 | tf_op jit(solution)/shard_map/ppermute | solution.py:504
  52.0 2.6 %collective-permute-start.7 = (f32[4,64,128]{2,1,0:T(8,128)S(1)}, f32[4,64,128]{2,1,0:T(8,128)S(1)}, u32[]{:S(2)}, u32[]{:S(2)}) collective-permute-start(f32[4,64,128]{2,1,0:T(8,128)S(1)} %add.12), channel_id=1, source_target_pairs={{0,4},{1,5},{2,6},{3,7},{4,0},{5,1},{6,2},{7,3},{8,12},{9,13},{10,... | collective-permute-start | bytes 393224 | tf_op jit(solution)/shard_map/ppermute | solution.py:504
  54.7 1.1 %collective-permute-start.8 = (f32[4,64,128]{2,1,0:T(8,128)S(1)}, f32[4,64,128]{2,1,0:T(8,128)S(1)}, u32[]{:S(2)}, u32[]{:S(2)}) collective-permute-start(f32[4,64,128]{2,1,0:T(8,128)S(1)} %add.12), channel_id=1, source_target_pairs={{0,6},{1,7},{2,0},{3,1},{4,2},{5,3},{6,4},{7,5},{8,14},{9,15},{10,... | collective-permute-start | bytes 393224 | tf_op jit(solution)/shard_map/ppermute | solution.py:504
  55.7 1.1 %collective-permute-done.6 = f32[4,64,128]{2,1,0:T(8,128)S(1)} collective-permute-done((f32[4,64,128]{2,1,0:T(8,128)S(1)}, f32[4,64,128]{2,1,0:T(8,128)S(1)}, u32[]{:S(2)}, u32[]{:S(2)}) %collective-permute-start.6) | collective-permute-done | bytes 131104 | tf_op jit(solution)/shard_map/ppermute | solution.py:504
  56.8 3.9 %collective-permute-done.7 = f32[4,64,128]{2,1,0:T(8,128)S(1)} collective-permute-done((f32[4,64,128]{2,1,0:T(8,128)S(1)}, f32[4,64,128]{2,1,0:T(8,128)S(1)}, u32[]{:S(2)}, u32[]{:S(2)}) %collective-permute-start.7) | collective-permute-done | bytes 131104 | tf_op jit(solution)/shard_map/ppermute | solution.py:504
  60.8 0.7 %broadcast_subtract_fusion = f32[2,4,64,128]{3,2,1,0:T(8,128)} fusion(f32[2,4,64,128]{3,2,1,0:T(8,128)S(1)} %copy-done.7, f32[4,64,128]{2,1,0:T(8,128)S(1)} %add_multiply_fusion), kind=kLoop, calls=%fused_computation | loop fusion | flops 65536 | bytes 655360 | tf_op jit(solution)/shard_map/sub | solution.py:505
  (19 shorter events, 0.1 us)
Async XLA Ops:
  1.3 10.7 %copy-start = (f32[2,4,64,128]{3,2,1,0:T(8,128)S(1)}, f32[2,4,64,128]{3,2,1,0:T(8,128)}, u32[]{:S(2)}) copy-start(f32[2,4,64,128]{3,2,1,0:T(8,128)} %head_ref.1) | copy-start | bytes 786436
  1.3 10.7 %copy-start.1 = (f32[4,64,128]{2,1,0:T(8,128)S(1)}, f32[4,64,128]{2,1,0:T(8,128)}, u32[]{:S(2)}) copy-start(f32[4,64,128]{2,1,0:T(8,128)} %storage_ref.1) | copy-start | bytes 393220
  1.3 10.7 %copy-start.2 = (f32[4,64,128]{2,1,0:T(8,128)S(1)}, f32[4,64,128]{2,1,0:T(8,128)}, u32[]{:S(2)}) copy-start(f32[4,64,128]{2,1,0:T(8,128)} %flow_ref.1) | copy-start | bytes 393220
  1.3 10.7 %copy-start.3 = (f32[4,64,128]{2,1,0:T(8,128)S(1)}, f32[4,64,128]{2,1,0:T(8,128)}, u32[]{:S(2)}) copy-start(f32[4,64,128]{2,1,0:T(8,128)} %cross_ref.1) | copy-start | bytes 393220
  1.3 10.7 %copy-start.4 = (f32[4,64,128]{2,1,0:T(8,128)S(1)}, f32[4,64,128]{2,1,0:T(8,128)}, u32[]{:S(2)}) copy-start(f32[4,64,128]{2,1,0:T(8,128)} %vert_ref.1) | copy-start | bytes 393220
  1.3 10.7 %copy-start.5 = (s32[4,64,128]{2,1,0:T(8,128)S(1)}, s32[4,64,128]{2,1,0:T(8,128)}, u32[]{:S(2)}) copy-start(s32[4,64,128]{2,1,0:T(8,128)} %active_ref.1) | copy-start | bytes 393220
  6.6 6.7 %collective-permute-start = (f32[128,128]{1,0:T(8,128)}, f32[128,128]{1,0:T(8,128)S(1)}, u32[]{:S(2)}, u32[]{:S(2)}) collective-permute-start(f32[128,128]{1,0:T(8,128)} %get-tuple-element.21), channel_id=1, source_target_pairs={{0,8},{8,16},{16,24},{24,32},{32,40},{40,48},{48,56},{56,64},{64,7... | collective-permute-start | bytes 196616 | tf_op jit(solution)/shard_map/ppermute | solution.py:460
  10.6 5.4 %copy-start.6 = (f32[128,128]{1,0:T(8,128)S(1)}, f32[128,128]{1,0:T(8,128)}, u32[]{:S(2)}) copy-start(f32[128,128]{1,0:T(8,128)} %get-tuple-element.20.own_ref) | copy-start | bytes 196612
  10.6 5.4 %collective-permute-start.1 = (f32[128,128]{1,0:T(8,128)}, f32[128,128]{1,0:T(8,128)S(1)}, u32[]{:S(2)}, u32[]{:S(2)}) collective-permute-start(f32[128,128]{1,0:T(8,128)} %get-tuple-element.22), channel_id=1, source_target_pairs={{8,0},{16,8},{24,16},{32,24},{40,32},{48,40},{56,48},{64,56},{72,6... | collective-permute-start | bytes 196616 | tf_op jit(solution)/shard_map/ppermute | solution.py:459
  16.6 6.2 %collective-permute-start.2 = (f32[48,128]{1,0:T(8,128)S(1)}, f32[48,128]{1,0:T(8,128)S(1)}, u32[]{:S(2)}, u32[]{:S(2)}) collective-permute-start(f32[48,128]{1,0:T(8,128)S(1)} %get-tuple-element.24.own_ref), channel_id=1, source_target_pairs={{0,8},{8,16},{16,24},{24,0},{32,40},{40,48},{48,56},{56,32},{64,72... | collective-permute-start | bytes 73736 | tf_op jit(solution)/shard_map/ppermute | solution.py:480
  17.8 6.4 %collective-permute-start.3 = (f32[48,128]{1,0:T(8,128)S(1)}, f32[48,128]{1,0:T(8,128)S(1)}, u32[]{:S(2)}, u32[]{:S(2)}) collective-permute-start(f32[48,128]{1,0:T(8,128)S(1)} %get-tuple-element.24.own_ref), channel_id=1, source_target_pairs={{0,16},{8,24},{16,0},{24,8},{32,48},{40,56},{48,32},{56,40},{64,80... | collective-permute-start | bytes 73736 | tf_op jit(solution)/shard_map/ppermute | solution.py:480
  22.7 2.7 %collective-permute-start.4 = (f32[48,128]{1,0:T(8,128)S(1)}, f32[48,128]{1,0:T(8,128)S(1)}, u32[]{:S(2)}, u32[]{:S(2)}) collective-permute-start(f32[48,128]{1,0:T(8,128)S(1)} %get-tuple-element.24.own_ref), channel_id=1, source_target_pairs={{0,24},{8,0},{16,8},{24,16},{32,56},{40,32},{48,40},{56,48},{64,88... | collective-permute-start | bytes 73736 | tf_op jit(solution)/shard_map/ppermute | solution.py:480
  44.5 6.1 %collective-permute-start.5 = (f32[4,64,128]{2,1,0:T(8,128)S(1)}, f32[4,64,128]{2,1,0:T(8,128)S(1)}, u32[]{:S(2)}, u32[]{:S(2)}) collective-permute-start(f32[4,64,128]{2,1,0:T(8,128)S(1)} %get-tuple-element.31), channel_id=1, source_target_pairs={{0,1},{1,0},{2,3},{3,2},{4,5},{5,4},{6,7},{7,6},{8,9},{9,8},{10,11... | collective-permute-start | bytes 393224 | tf_op jit(solution)/shard_map/ppermute | solution.py:501
  50.7 10.1 %copy-start.7 = (f32[2,4,64,128]{3,2,1,0:T(8,128)S(1)}, f32[2,4,64,128]{3,2,1,0:T(8,128)}, u32[]{:S(2)}) copy-start(f32[2,4,64,128]{3,2,1,0:T(8,128)} %get-tuple-element.15) | copy-start | bytes 786436
  50.7 6.1 %collective-permute-start.6 = (f32[4,64,128]{2,1,0:T(8,128)S(1)}, f32[4,64,128]{2,1,0:T(8,128)S(1)}, u32[]{:S(2)}, u32[]{:S(2)}) collective-permute-start(f32[4,64,128]{2,1,0:T(8,128)S(1)} %add.12), channel_id=1, source_target_pairs={{0,2},{1,3},{2,4},{3,5},{4,6},{5,7},{6,0},{7,1},{8,10},{9,11},{10,... | collective-permute-start | bytes 393224 | tf_op jit(solution)/shard_map/ppermute | solution.py:504
  52.0 8.7 %collective-permute-start.7 = (f32[4,64,128]{2,1,0:T(8,128)S(1)}, f32[4,64,128]{2,1,0:T(8,128)S(1)}, u32[]{:S(2)}, u32[]{:S(2)}) collective-permute-start(f32[4,64,128]{2,1,0:T(8,128)S(1)} %add.12), channel_id=1, source_target_pairs={{0,4},{1,5},{2,6},{3,7},{4,0},{5,1},{6,2},{7,3},{8,12},{9,13},{10,... | collective-permute-start | bytes 393224 | tf_op jit(solution)/shard_map/ppermute | solution.py:504
  54.7 6.1 %collective-permute-start.8 = (f32[4,64,128]{2,1,0:T(8,128)S(1)}, f32[4,64,128]{2,1,0:T(8,128)S(1)}, u32[]{:S(2)}, u32[]{:S(2)}) collective-permute-start(f32[4,64,128]{2,1,0:T(8,128)S(1)} %add.12), channel_id=1, source_target_pairs={{0,6},{1,7},{2,0},{3,1},{4,2},{5,3},{6,4},{7,5},{8,14},{9,15},{10,... | collective-permute-start | bytes 393224 | tf_op jit(solution)/shard_map/ppermute | solution.py:504

commit v3 on v2

--- a/solution.py
+++ b/solution.py
@@ -498,10 +498,10 @@
         10**9,
     )(place, gathered.reshape(SUBS * 2 * ROWS, 128), blocks, saved, fields, small, source, inner)
     lanes = lax.axis_size("lane")
-    total = total + lax.ppermute(total, "lane", [(i, i ^ 1) for i in range(lanes)])
     whole = total
     for k in range(2, lanes, 2):
         whole = whole + lax.ppermute(total, "lane", [(i, (i + k) % lanes) for i in range(lanes)])
+    whole = whole + lax.ppermute(whole, "lane", [(i, i ^ 1) for i in range(lanes)])
     anomaly = head - whole[None] / (2 * lanes)
     return head, anomaly
 

time: 61.7 us -> 61.2 us (level)
  waiting for transfers between devices: 11.2 us -> 8.97 us
  starting transfers between devices: 21.8 us -> 23.5 us
    ppermute x3, waiting for transfers between devices: 5 us -> 2.75 us  [on_device(): lax.ppermute(total, 'lane', [(i, (i + k) % lanes) for i in range(lanes)])]
    ppermute x1, starting transfers between devices: 5.14 us -> 6.94 us  [on_device(): lax.ppermute(whole, 'lane', [(i, i ^ 1) for i in range(lanes)])]
  transfers between devices with their start and end apart: 9 -> 9, of which waited for: 6 -> 7; matrix products, arithmetic and copies ran while one was open for 0% -> 0% of each run, Pallas kernels for 2% -> 2%
where the time goes in v3:
time: 61.2 us; the launch traced here: 61 us
  starting transfers between devices  23.5 us (38%)
  blocking collectives  16.6 us (27%)
  Pallas kernels  9.69 us (16%)
  waiting for transfers between devices  8.97 us (15%)
  between operations  1.45 us (2%)
  other arithmetic  0.78 us (1%)
    all_to_all x1, blocking collectives, on_device(): lax.all_to_all(block, 'flow', split_axis=0, concat_axis=0, axis_index_gro...  16.6 us
    ppermute x1, starting transfers between devices, on_device(): lax.ppermute(whole, 'lane', [(i, i ^ 1) for i in range(lanes)])  6.94 us
    ppermute x3, starting transfers between devices, on_device(): lax.ppermute(block, 'flow', [(i, i - i % per + (i + k) % per) for i in ra...  6.19 us
    pallas_call x1, Pallas kernels, on_device(): pl.pallas_call(scatter_kernel, name='scatter', grid=(1,), in_specs=[pl.Bl...  5.28 us
    ppermute x3, starting transfers between devices, on_device(): lax.ppermute(total, 'lane', [(i, (i + k) % lanes) for i in range(lanes)])  4.99 us
    ppermute x1, starting transfers between devices, on_device(): low = lax.ppermute(after, 'flow', [(i, i + 1) for i in range(devices - 1)])  3.93 us
    ppermute x3, waiting for transfers between devices, on_device(): lax.ppermute(total, 'lane', [(i, (i + k) % lanes) for i in range(lanes)])  2.75 us
    ppermute x3, waiting for transfers between devices, on_device(): lax.ppermute(block, 'flow', [(i, i - i % per + (i + k) % per) for i in ra...  2.67 us
  transfers between devices with their start and end apart: 9, of which 7 were waited for; matrix products, arithmetic and copies ran while one was open for 0% of the time, Pallas kernels for 2%

profile of v3, /device:TPU:1, one launch (start us, length us, event | category | flops | bytes accessed | tf_op | source)
XLA Modules:
  0.0 61.0 jit_solution(1541855096211422727)
XLA Ops:
  1.3 5.3 %scatter.1 = (f32[128,128]{1,0:T(8,128)}, f32[128,128]{1,0:T(8,128)}, f32[128,128]{1,0:T(8,128)}) custom-call(s32[4,4096]{1,0:T(4,128)} %bitcast.8, f32[4,4096]{1,0:T(4,128)} %bitcast.9, s32[1,4096]{1,0:T(1,128)} %bitcast.10, s32[2,4096]{1,0:T(2,128)} %bmp_ref.1, f32[1,4096]{1,0:T(1,128)} %bitcast.11, f32[8,16]{1,0:T(8,128)} %bitcast.12, s32[1]{0:T(128)S(6)} %copy.15.live_ref), custom_call_target="tpu_custom_call" | custom-call | flops 4000000000 | bytes 2097152 | tf_op jit(solution)/shard_map/scatter/pallas_call | solution.py:446
  6.6 3.9 %collective-permute-start = (f32[128,128]{1,0:T(8,128)}, f32[128,128]{1,0:T(8,128)S(1)}, u32[]{:S(2)}, u32[]{:S(2)}) collective-permute-start(f32[128,128]{1,0:T(8,128)} %get-tuple-element.21), channel_id=1, source_target_pairs={{0,8},{8,16},{16,24},{24,32},{32,40},{40,48},{48,56},{56,64},{64,7... | collective-permute-start | bytes 196616 | tf_op jit(solution)/shard_map/ppermute | solution.py:460
  10.6 0.0 copy-start.6
  10.6 1.4 %collective-permute-start.1 = (f32[128,128]{1,0:T(8,128)}, f32[128,128]{1,0:T(8,128)S(1)}, u32[]{:S(2)}, u32[]{:S(2)}) collective-permute-start(f32[128,128]{1,0:T(8,128)} %get-tuple-element.22), channel_id=1, source_target_pairs={{8,0},{16,8},{24,16},{32,24},{40,32},{48,40},{56,48},{64,56},{72,6... | collective-permute-start | bytes 196616 | tf_op jit(solution)/shard_map/ppermute | solution.py:459
  12.1 1.3 %coefficients.1 = (f32[8,16,8,256]{3,2,1,0:T(8,128)S(1)}, f32[3,16,256]{2,1,0:T(8,128)S(1)}, f32[4,16,8,256]{3,2,1,0:T(8,128)S(1)}, f32[16,256]{1,0:T(8,128)S(1)}) custom-call(f32[2,4,64,128]{3,2,1,0:T(8,128)S(1)} %copy-done, f32[4,64,128]{2,1,0:T(8,128)S(1)} %copy-done.1, f32[4,64,128]{2,1,0:T(8,128)S(1)} %copy-done.2, f32[4,64,128]{2,1,0:T(8,128)S(1)} %copy-done.3, ...), custom_call_target="tpu_custom_call" | custom-call | flops 4000000000 | bytes 2097152 | tf_op jit(solution)/shard_map/coefficients/pallas_call | solution.py:461
  13.4 2.6 %collective-permute-done.1.high_ref = f32[128,128]{1,0:T(8,128)S(1)} collective-permute-done((f32[128,128]{1,0:T(8,128)}, f32[128,128]{1,0:T(8,128)S(1)}, u32[]{:S(2)}, u32[]{:S(2)}) %collective-permute-start.1) | collective-permute-done | bytes 65568 | tf_op jit(solution)/shard_map/ppermute | solution.py:459
  15.9 0.6 %sources.1 = (f32[2,16,8,256]{3,2,1,0:T(8,128)S(1)}, f32[2,16,8,256]{3,2,1,0:T(8,128)S(1)}, f32[48,128]{1,0:T(8,128)S(1)}) custom-call(f32[8,16,8,256]{3,2,1,0:T(8,128)S(1)} %get-tuple-element.17.fields_ref, f32[3,16,256]{2,1,0:T(8,128)S(1)} %get-tuple-element.18.small_ref, f32[4,16,8,256]{3,2,1,0:T(8,128)S(1)} %get-tuple-element.19.base_ref, ...), custom_call_target="tpu_custom_call" | custom-call | flops 1000000000 | bytes 2097152 | tf_op jit(solution)/shard_map/sources/pallas_call | solution.py:469
  16.6 1.3 %collective-permute-start.2 = (f32[48,128]{1,0:T(8,128)S(1)}, f32[48,128]{1,0:T(8,128)S(1)}, u32[]{:S(2)}, u32[]{:S(2)}) collective-permute-start(f32[48,128]{1,0:T(8,128)S(1)} %get-tuple-element.24.own_ref), channel_id=1, source_target_pairs={{0,8},{8,16},{16,24},{24,0},{32,40},{40,48},{48,56},{56,32},{64,72... | collective-permute-start | bytes 73736 | tf_op jit(solution)/shard_map/ppermute | solution.py:480
  17.8 4.9 %collective-permute-start.3 = (f32[48,128]{1,0:T(8,128)S(1)}, f32[48,128]{1,0:T(8,128)S(1)}, u32[]{:S(2)}, u32[]{:S(2)}) collective-permute-start(f32[48,128]{1,0:T(8,128)S(1)} %get-tuple-element.24.own_ref), channel_id=1, source_target_pairs={{0,16},{8,24},{16,0},{24,8},{32,48},{40,56},{48,32},{56,40},{64,80... | collective-permute-start | bytes 73736 | tf_op jit(solution)/shard_map/ppermute | solution.py:480
  22.7 0.0 collective-permute-done.2.from1_ref
  22.8 1.4 %collective-permute-done.3.from2_ref = f32[48,128]{1,0:T(8,128)S(1)} collective-permute-done((f32[48,128]{1,0:T(8,128)S(1)}, f32[48,128]{1,0:T(8,128)S(1)}, u32[]{:S(2)}, u32[]{:S(2)}) %collective-permute-start.3) | collective-permute-done | bytes 24608 | tf_op jit(solution)/shard_map/ppermute | solution.py:480
  24.2 1.2 %collective-permute-done.4.from3_ref = f32[48,128]{1,0:T(8,128)S(1)} collective-permute-done((f32[48,128]{1,0:T(8,128)S(1)}, f32[48,128]{1,0:T(8,128)S(1)}, u32[]{:S(2)}, u32[]{:S(2)}) %collective-permute-start.4) | collective-permute-done | bytes 24608 | tf_op jit(solution)/shard_map/ppermute | solution.py:480
  25.4 0.4 groups.1
  25.8 16.6 %all_to_all.5 = f32[8,48,128]{2,1,0:T(8,128)S(1)} all-to-all(f32[8,48,128]{2,1,0:T(8,128)S(1)} %get-tuple-element.25), channel_id=1, replica_groups={{0,32,64,96,128,160,192,224},{8,40,72,104,136,168,200,232},{16,48,80,11..., dimensions={0} | all-to-all | bytes 393216 | tf_op jit(solution)/shard_map/all_to_all | solution.py:491
  42.4 2.1 %sweeps.1 = (f32[2,4,64,128]{3,2,1,0:T(8,128)}, f32[4,64,128]{2,1,0:T(8,128)S(1)}) custom-call(s32[1]{0:T(128)} %bitcast.place_ref, f32[384,128]{1,0:T(8,128)S(1)} %bitcast.7, f32[4,48,128]{2,1,0:T(8,128)S(1)} %get-tuple-element.26.blocks_ref, f32[56,256]{1,0:T(8,128)S(1)} %get-tuple-element.27.saved_ref, ...), custom_call_target="tpu_custom_call" | custom-call | flops 1000000000 | bytes 2097152 | tf_op jit(solution)/shard_map/sweeps/pallas_call | solution.py:492
  44.5 1.3 %collective-permute-start.5 = (f32[4,64,128]{2,1,0:T(8,128)S(1)}, f32[4,64,128]{2,1,0:T(8,128)S(1)}, u32[]{:S(2)}, u32[]{:S(2)}) collective-permute-start(f32[4,64,128]{2,1,0:T(8,128)S(1)} %get-tuple-element.31), channel_id=1, source_target_pairs={{0,2},{1,3},{2,4},{3,5},{4,6},{5,7},{6,0},{7,1},{8,10},{9,11},{10,... | collective-permute-start | bytes 393224 | tf_op jit(solution)/shard_map/ppermute | solution.py:503
  45.8 2.6 %collective-permute-start.6 = (f32[4,64,128]{2,1,0:T(8,128)S(1)}, f32[4,64,128]{2,1,0:T(8,128)S(1)}, u32[]{:S(2)}, u32[]{:S(2)}) collective-permute-start(f32[4,64,128]{2,1,0:T(8,128)S(1)} %get-tuple-element.31), channel_id=1, source_target_pairs={{0,4},{1,5},{2,6},{3,7},{4,0},{5,1},{6,2},{7,3},{8,12},{9,13},{10,... | collective-permute-start | bytes 393224 | tf_op jit(solution)/shard_map/ppermute | solution.py:503
  48.4 1.1 %collective-permute-start.7 = (f32[4,64,128]{2,1,0:T(8,128)S(1)}, f32[4,64,128]{2,1,0:T(8,128)S(1)}, u32[]{:S(2)}, u32[]{:S(2)}) collective-permute-start(f32[4,64,128]{2,1,0:T(8,128)S(1)} %get-tuple-element.31), channel_id=1, source_target_pairs={{0,6},{1,7},{2,0},{3,1},{4,2},{5,3},{6,4},{7,5},{8,14},{9,15},{10,... | collective-permute-start | bytes 393224 | tf_op jit(solution)/shard_map/ppermute | solution.py:503
  49.5 0.1 collective-permute-done.5
  49.6 2.6 %collective-permute-done.6 = f32[4,64,128]{2,1,0:T(8,128)S(1)} collective-permute-done((f32[4,64,128]{2,1,0:T(8,128)S(1)}, f32[4,64,128]{2,1,0:T(8,128)S(1)}, u32[]{:S(2)}, u32[]{:S(2)}) %collective-permute-start.6) | collective-permute-done | bytes 131104 | tf_op jit(solution)/shard_map/ppermute | solution.py:503
  52.2 0.1 collective-permute-done.7
  52.3 6.9 %collective-permute-start.8 = (f32[4,64,128]{2,1,0:T(8,128)S(1)}, f32[4,64,128]{2,1,0:T(8,128)S(1)}, u32[]{:S(2)}, u32[]{:S(2)}) collective-permute-start(f32[4,64,128]{2,1,0:T(8,128)S(1)} %add_add_fusion), channel_id=1, source_target_pairs={{0,1},{1,0},{2,3},{3,2},{4,5},{5,4},{6,7},{7,6},{8,9},{9,8},{10,11... | collective-permute-start | bytes 393224 | tf_op jit(solution)/shard_map/ppermute | solution.py:504
  59.2 1.0 %collective-permute-done.8 = f32[4,64,128]{2,1,0:T(8,128)S(1)} collective-permute-done((f32[4,64,128]{2,1,0:T(8,128)S(1)}, f32[4,64,128]{2,1,0:T(8,128)S(1)}, u32[]{:S(2)}, u32[]{:S(2)}) %collective-permute-start.8) | collective-permute-done | bytes 131104 | tf_op jit(solution)/shard_map/ppermute | solution.py:504
  60.2 0.7 %broadcast_subtract_fusion = f32[2,4,64,128]{3,2,1,0:T(8,128)} fusion(f32[2,4,64,128]{3,2,1,0:T(8,128)S(1)} %copy-done.7, f32[4,64,128]{2,1,0:T(8,128)S(1)} %add_multiply_fusion), kind=kLoop, calls=%fused_computation | loop fusion | flops 65536 | bytes 655360 | tf_op jit(solution)/shard_map/sub | solution.py:505
  (19 shorter events, 0.1 us)
Async XLA Ops:
  1.3 10.7 %copy-start = (f32[2,4,64,128]{3,2,1,0:T(8,128)S(1)}, f32[2,4,64,128]{3,2,1,0:T(8,128)}, u32[]{:S(2)}) copy-start(f32[2,4,64,128]{3,2,1,0:T(8,128)} %head_ref.1) | copy-start | bytes 786436
  1.3 10.7 %copy-start.1 = (f32[4,64,128]{2,1,0:T(8,128)S(1)}, f32[4,64,128]{2,1,0:T(8,128)}, u32[]{:S(2)}) copy-start(f32[4,64,128]{2,1,0:T(8,128)} %storage_ref.1) | copy-start | bytes 393220
  1.3 10.7 %copy-start.2 = (f32[4,64,128]{2,1,0:T(8,128)S(1)}, f32[4,64,128]{2,1,0:T(8,128)}, u32[]{:S(2)}) copy-start(f32[4,64,128]{2,1,0:T(8,128)} %flow_ref.1) | copy-start | bytes 393220
  1.3 10.7 %copy-start.3 = (f32[4,64,128]{2,1,0:T(8,128)S(1)}, f32[4,64,128]{2,1,0:T(8,128)}, u32[]{:S(2)}) copy-start(f32[4,64,128]{2,1,0:T(8,128)} %cross_ref.1) | copy-start | bytes 393220
  1.3 10.7 %copy-start.4 = (f32[4,64,128]{2,1,0:T(8,128)S(1)}, f32[4,64,128]{2,1,0:T(8,128)}, u32[]{:S(2)}) copy-start(f32[4,64,128]{2,1,0:T(8,128)} %vert_ref.1) | copy-start | bytes 393220
  1.3 10.7 %copy-start.5 = (s32[4,64,128]{2,1,0:T(8,128)S(1)}, s32[4,64,128]{2,1,0:T(8,128)}, u32[]{:S(2)}) copy-start(s32[4,64,128]{2,1,0:T(8,128)} %active_ref.1) | copy-start | bytes 393220
  6.6 6.7 %collective-permute-start = (f32[128,128]{1,0:T(8,128)}, f32[128,128]{1,0:T(8,128)S(1)}, u32[]{:S(2)}, u32[]{:S(2)}) collective-permute-start(f32[128,128]{1,0:T(8,128)} %get-tuple-element.21), channel_id=1, source_target_pairs={{0,8},{8,16},{16,24},{24,32},{32,40},{40,48},{48,56},{56,64},{64,7... | collective-permute-start | bytes 196616 | tf_op jit(solution)/shard_map/ppermute | solution.py:460
  10.6 5.4 %copy-start.6 = (f32[128,128]{1,0:T(8,128)S(1)}, f32[128,128]{1,0:T(8,128)}, u32[]{:S(2)}) copy-start(f32[128,128]{1,0:T(8,128)} %get-tuple-element.20.own_ref) | copy-start | bytes 196612
  10.6 5.4 %collective-permute-start.1 = (f32[128,128]{1,0:T(8,128)}, f32[128,128]{1,0:T(8,128)S(1)}, u32[]{:S(2)}, u32[]{:S(2)}) collective-permute-start(f32[128,128]{1,0:T(8,128)} %get-tuple-element.22), channel_id=1, source_target_pairs={{8,0},{16,8},{24,16},{32,24},{40,32},{48,40},{56,48},{64,56},{72,6... | collective-permute-start | bytes 196616 | tf_op jit(solution)/shard_map/ppermute | solution.py:459
  16.6 6.2 %collective-permute-start.2 = (f32[48,128]{1,0:T(8,128)S(1)}, f32[48,128]{1,0:T(8,128)S(1)}, u32[]{:S(2)}, u32[]{:S(2)}) collective-permute-start(f32[48,128]{1,0:T(8,128)S(1)} %get-tuple-element.24.own_ref), channel_id=1, source_target_pairs={{0,8},{8,16},{16,24},{24,0},{32,40},{40,48},{48,56},{56,32},{64,72... | collective-permute-start | bytes 73736 | tf_op jit(solution)/shard_map/ppermute | solution.py:480
  17.8 6.4 %collective-permute-start.3 = (f32[48,128]{1,0:T(8,128)S(1)}, f32[48,128]{1,0:T(8,128)S(1)}, u32[]{:S(2)}, u32[]{:S(2)}) collective-permute-start(f32[48,128]{1,0:T(8,128)S(1)} %get-tuple-element.24.own_ref), channel_id=1, source_target_pairs={{0,16},{8,24},{16,0},{24,8},{32,48},{40,56},{48,32},{56,40},{64,80... | collective-permute-start | bytes 73736 | tf_op jit(solution)/shard_map/ppermute | solution.py:480
  22.7 2.7 %collective-permute-start.4 = (f32[48,128]{1,0:T(8,128)S(1)}, f32[48,128]{1,0:T(8,128)S(1)}, u32[]{:S(2)}, u32[]{:S(2)}) collective-permute-start(f32[48,128]{1,0:T(8,128)S(1)} %get-tuple-element.24.own_ref), channel_id=1, source_target_pairs={{0,24},{8,0},{16,8},{24,16},{32,56},{40,32},{48,40},{56,48},{64,88... | collective-permute-start | bytes 73736 | tf_op jit(solution)/shard_map/ppermute | solution.py:480
  44.5 5.1 %collective-permute-start.5 = (f32[4,64,128]{2,1,0:T(8,128)S(1)}, f32[4,64,128]{2,1,0:T(8,128)S(1)}, u32[]{:S(2)}, u32[]{:S(2)}) collective-permute-start(f32[4,64,128]{2,1,0:T(8,128)S(1)} %get-tuple-element.31), channel_id=1, source_target_pairs={{0,2},{1,3},{2,4},{3,5},{4,6},{5,7},{6,0},{7,1},{8,10},{9,11},{10,... | collective-permute-start | bytes 393224 | tf_op jit(solution)/shard_map/ppermute | solution.py:503
  45.8 6.4 %collective-permute-start.6 = (f32[4,64,128]{2,1,0:T(8,128)S(1)}, f32[4,64,128]{2,1,0:T(8,128)S(1)}, u32[]{:S(2)}, u32[]{:S(2)}) collective-permute-start(f32[4,64,128]{2,1,0:T(8,128)S(1)} %get-tuple-element.31), channel_id=1, source_target_pairs={{0,4},{1,5},{2,6},{3,7},{4,0},{5,1},{6,2},{7,3},{8,12},{9,13},{10,... | collective-permute-start | bytes 393224 | tf_op jit(solution)/shard_map/ppermute | solution.py:503
  48.4 3.8 %collective-permute-start.7 = (f32[4,64,128]{2,1,0:T(8,128)S(1)}, f32[4,64,128]{2,1,0:T(8,128)S(1)}, u32[]{:S(2)}, u32[]{:S(2)}) collective-permute-start(f32[4,64,128]{2,1,0:T(8,128)S(1)} %get-tuple-element.31), channel_id=1, source_target_pairs={{0,6},{1,7},{2,0},{3,1},{4,2},{5,3},{6,4},{7,5},{8,14},{9,15},{10,... | collective-permute-start | bytes 393224 | tf_op jit(solution)/shard_map/ppermute | solution.py:503
  52.3 8.0 %copy-start.7 = (f32[2,4,64,128]{3,2,1,0:T(8,128)S(1)}, f32[2,4,64,128]{3,2,1,0:T(8,128)}, u32[]{:S(2)}) copy-start(f32[2,4,64,128]{3,2,1,0:T(8,128)} %get-tuple-element.15) | copy-start | bytes 786436
  52.3 7.9 %collective-permute-start.8 = (f32[4,64,128]{2,1,0:T(8,128)S(1)}, f32[4,64,128]{2,1,0:T(8,128)S(1)}, u32[]{:S(2)}, u32[]{:S(2)}) collective-permute-start(f32[4,64,128]{2,1,0:T(8,128)S(1)} %add_add_fusion), channel_id=1, source_target_pairs={{0,1},{1,0},{2,3},{3,2},{4,5},{5,4},{6,7},{7,6},{8,9},{9,8},{10,11... | collective-permute-start | bytes 393224 | tf_op jit(solution)/shard_map/ppermute | solution.py:504

commit v4 on v3

--- a/solution.py
+++ b/solution.py
@@ -131,7 +131,7 @@
 
 
 def scatter_kernel(cells_ref, area_ref, land_ref, bmp_ref, rain_ref, table_ref, live_ref,
-                   before_ref, own_ref, after_ref, amount_ref, window_ref):
+                   place_ref, first_ref, own_ref, second_ref, amount_ref, window_ref):
     slots = land_ref.shape[1]
     land = land_ref[...]
     rates = jnp.zeros((8, slots), F32)
@@ -168,8 +168,10 @@
                 window_ref[k, pl.ds(64 * s + odd, 32, stride=2), :] = summed[
                     32 * k : 32 * k + 32, 128 * odd : 128 * odd + 128
                 ]
-    for k, ref in enumerate((before_ref, own_ref, after_ref)):
-        ref[...] = window_ref[k].T
+    odd = lax.rem(place_ref[0], 2)
+    own_ref[...] = window_ref[1].T
+    first_ref[...] = window_ref[2 - 2 * odd].T
+    second_ref[...] = window_ref[2 * odd].T
 
 
 def coefficient_kernel(head_ref, storage_ref, flow_ref, cross_ref, vert_ref, active_ref,
@@ -318,7 +320,7 @@
     per = blocks_ref.shape[0]
     place = lax.rem(place_ref[0], per)
     for k, ref in enumerate((own_ref, from1_ref, from2_ref, from3_ref)):
-        blocks_ref[lax.rem(place + per - k, per)] = ref[...]
+        blocks_ref[lax.bitwise_xor(place, k)] = ref[...]
     got = [member(blocks_ref, p) for p in range(per)]
     leak, face = [], []
     for p in range(per):
@@ -443,21 +445,22 @@
     devices = lax.axis_size("flow")
     tile = (128, 128)
     blocks = [(4, slots), (4, slots), (1, slots), (2, slots), (1, slots), (8, 16)]
-    before, own, after = pl.pallas_call(
+    place = lax.axis_index("flow").astype(jnp.int32).reshape(1)
+    first, own, second = pl.pallas_call(
         scatter_kernel,
         name="scatter",
         grid=(1,),
-        in_specs=[pl.BlockSpec(shape, lambda i: (0, 0)) for shape in blocks] + [SMEM],
+        in_specs=[pl.BlockSpec(shape, lambda i: (0, 0)) for shape in blocks] + [SMEM] * 2,
         out_specs=[pl.BlockSpec(tile, lambda i: (0, 0))] * 3,
         out_shape=[jax.ShapeDtypeStruct(tile, F32)] * 3,
         scratch_shapes=[pltpu.VMEM((4, 4, slots), F32), pltpu.VMEM((3,) + tile, F32)],
         compiler_params=pltpu.CompilerParams(vmem_limit_bytes=60 * 2**20),
         cost_estimate=pl.CostEstimate(flops=4 * 10**9, bytes_accessed=2 * 2**20, transcendentals=0),
     )(
-        hru_cells.T, hru_area.T, hru_land.reshape(1, slots), hru_bmp, rain.reshape(1, slots), perc_table.T, hru_live
+        hru_cells.T, hru_area.T, hru_land.reshape(1, slots), hru_bmp, rain.reshape(1, slots), perc_table.T, hru_live, place
     )
-    high = lax.ppermute(before, "flow", [(i + 1, i) for i in range(devices - 1)])
-    low = lax.ppermute(after, "flow", [(i, i + 1) for i in range(devices - 1)])
+    low = lax.ppermute(first, "flow", [(i, i ^ 1) for i in range(devices)])
+    high = lax.ppermute(second, "flow", [(i, i - 1 + 2 * (i % 2)) for i in range(1, devices - 1)])
     fields, small, base, coefs = kernel_call(
         coefficient_kernel,
         "coefficients",
@@ -474,10 +477,9 @@
         [tile],
         10**9,
     )(fields, small, base, own, low, high, coefs)
-    place = lax.axis_index("flow").astype(jnp.int32).reshape(1)
     per = devices // SUBS
     around = [
-        lax.ppermute(block, "flow", [(i, i - i % per + (i + k) % per) for i in range(devices)]) for k in range(1, per)
+        lax.ppermute(block, "flow", [(i, i ^ k) for i in range(devices)]) for k in range(1, per)
     ]
     blocks, saved, block = kernel_call(
         group_kernel,
@@ -500,7 +502,7 @@
     lanes = lax.axis_size("lane")
     whole = total
     for k in range(2, lanes, 2):
-        whole = whole + lax.ppermute(total, "lane", [(i, (i + k) % lanes) for i in range(lanes)])
+        whole = whole + lax.ppermute(total, "lane", [(i, i ^ k) for i in range(lanes)])
     whole = whole + lax.ppermute(whole, "lane", [(i, i ^ 1) for i in range(lanes)])
     anomaly = head - whole[None] / (2 * lanes)
     return head, anomaly

time: 61.2 us -> 58.5 us (0.956)
  starting transfers between devices: 23.5 us -> 20.4 us
    ppermute x8, starting transfers between devices: 16.5 us -> 14 us  [the longest x3 7.86 us: on_device(): lax.ppermute(block, 'flow', [(i, i ^ k) for i in range(devices)])]
  transfers between devices with their start and end apart: 9 -> 9, of which waited for: 7 -> 5; matrix products, arithmetic and copies ran while one was open for 0% -> 0% of each run, Pallas kernels for 2% -> 2%
where the time goes in v4:
time: 58.5 us; the launch traced here: 58.3 us
  starting transfers between devices  20.4 us (35%)
  blocking collectives  16.7 us (29%)
  Pallas kernels  9.75 us (17%)
  waiting for transfers between devices  9.24 us (16%)
  between operations  1.46 us (2%)
  other arithmetic  0.78 us (1%)
    all_to_all x1, blocking collectives, on_device(): lax.all_to_all(block, 'flow', split_axis=0, concat_axis=0, axis_index_gro...  16.7 us
    ppermute x3, starting transfers between devices, on_device(): lax.ppermute(block, 'flow', [(i, i ^ k) for i in range(devices)])  7.86 us
    ppermute x1, starting transfers between devices, on_device(): lax.ppermute(whole, 'lane', [(i, i ^ 1) for i in range(lanes)])  6.37 us
    pallas_call x1, Pallas kernels, on_device(): pl.pallas_call(scatter_kernel, name='scatter', grid=(1,), in_specs=[pl.Bl...  5.3 us
    ppermute x3, waiting for transfers between devices, on_device(): lax.ppermute(total, 'lane', [(i, i ^ k) for i in range(lanes)])  4.74 us
    ppermute x3, waiting for transfers between devices, on_device(): lax.ppermute(block, 'flow', [(i, i ^ k) for i in range(devices)])  3.51 us
    ppermute x3, starting transfers between devices, on_device(): lax.ppermute(total, 'lane', [(i, i ^ k) for i in range(lanes)])  3.32 us
    pallas_call x1, Pallas kernels, on_device(): kernel_call(sweep_kernel, 'sweeps', [SMEM] + [VMEM] * 7, [head_prev.shape...  2.17 us
  transfers between devices with their start and end apart: 9, of which 5 were waited for; matrix products, arithmetic and copies ran while one was open for 0% of the time, Pallas kernels for 2%

profile of v4, /device:TPU:1, one launch (start us, length us, event | category | flops | bytes accessed | tf_op | source)
XLA Modules:
  0.0 58.3 jit_solution(1556584803091864950)
XLA Ops:
  1.3 5.3 %scatter.1 = (f32[128,128]{1,0:T(8,128)}, f32[128,128]{1,0:T(8,128)}, f32[128,128]{1,0:T(8,128)}) custom-call(s32[4,4096]{1,0:T(4,128)} %bitcast.8, f32[4,4096]{1,0:T(4,128)} %bitcast.9, s32[1,4096]{1,0:T(1,128)} %bitcast.10, s32[2,4096]{1,0:T(2,128)} %bmp_ref.1, f32[1,4096]{1,0:T(1,128)} %bitcast.11, f32[8,16]{1,0:T(8,128)} %bitcast.12, ...), custom_call_target="tpu_custom_call" | custom-call | flops 4000000000 | bytes 2097152 | tf_op jit(solution)/shard_map/scatter/pallas_call | solution.py:449
  6.6 2.0 %collective-permute-start = (f32[128,128]{1,0:T(8,128)}, f32[128,128]{1,0:T(8,128)S(1)}, u32[]{:S(2)}, u32[]{:S(2)}) collective-permute-start(f32[128,128]{1,0:T(8,128)} %get-tuple-element.21), channel_id=1, source_target_pairs={{0,8},{8,0},{16,24},{24,16},{32,40},{40,32},{48,56},{56,48},{64,72... | collective-permute-start | bytes 196616 | tf_op jit(solution)/shard_map/ppermute | solution.py:462
  8.7 0.8 %collective-permute-start.1 = (f32[128,128]{1,0:T(8,128)}, f32[128,128]{1,0:T(8,128)S(1)}, u32[]{:S(2)}, u32[]{:S(2)}) collective-permute-start(f32[128,128]{1,0:T(8,128)} %get-tuple-element.22), channel_id=1, source_target_pairs={{8,16},{16,8},{24,32},{32,24},{40,48},{48,40},{56,64},{64,56},{72,... | collective-permute-start | bytes 196616 | tf_op jit(solution)/shard_map/ppermute | solution.py:463
  9.5 1.3 %coefficients.1 = (f32[8,16,8,256]{3,2,1,0:T(8,128)S(1)}, f32[3,16,256]{2,1,0:T(8,128)S(1)}, f32[4,16,8,256]{3,2,1,0:T(8,128)S(1)}, f32[16,256]{1,0:T(8,128)S(1)}) custom-call(f32[2,4,64,128]{3,2,1,0:T(8,128)S(1)} %copy-done, f32[4,64,128]{2,1,0:T(8,128)S(1)} %copy-done.1, f32[4,64,128]{2,1,0:T(8,128)S(1)} %copy-done.2, f32[4,64,128]{2,1,0:T(8,128)S(1)} %copy-done.3, ...), custom_call_target="tpu_custom_call" | custom-call | flops 4000000000 | bytes 2097152 | tf_op jit(solution)/shard_map/coefficients/pallas_call | solution.py:464
  10.8 0.0 collective-permute-done.low_ref
  10.8 0.0 collective-permute-done.1.high_ref
  10.9 0.6 %sources.1 = (f32[2,16,8,256]{3,2,1,0:T(8,128)S(1)}, f32[2,16,8,256]{3,2,1,0:T(8,128)S(1)}, f32[48,128]{1,0:T(8,128)S(1)}) custom-call(f32[8,16,8,256]{3,2,1,0:T(8,128)S(1)} %get-tuple-element.17.fields_ref, f32[3,16,256]{2,1,0:T(8,128)S(1)} %get-tuple-element.18.small_ref, f32[4,16,8,256]{3,2,1,0:T(8,128)S(1)} %get-tuple-element.19.base_ref, ...), custom_call_target="tpu_custom_call" | custom-call | flops 1000000000 | bytes 2097152 | tf_op jit(solution)/shard_map/sources/pallas_call | solution.py:472
  11.5 7.2 %collective-permute-start.4 = (f32[48,128]{1,0:T(8,128)S(1)}, f32[48,128]{1,0:T(8,128)S(1)}, u32[]{:S(2)}, u32[]{:S(2)}) collective-permute-start(f32[48,128]{1,0:T(8,128)S(1)} %get-tuple-element.24.own_ref), channel_id=1, source_target_pairs={{0,24},{8,16},{16,8},{24,0},{32,56},{40,48},{48,40},{56,32},{64,88... | collective-permute-start | bytes 73736 | tf_op jit(solution)/shard_map/ppermute | solution.py:482
  18.7 0.0 collective-permute-start.3
  18.7 0.7 %collective-permute-start.2 = (f32[48,128]{1,0:T(8,128)S(1)}, f32[48,128]{1,0:T(8,128)S(1)}, u32[]{:S(2)}, u32[]{:S(2)}) collective-permute-start(f32[48,128]{1,0:T(8,128)S(1)} %get-tuple-element.24.own_ref), channel_id=1, source_target_pairs={{0,8},{8,0},{16,24},{24,16},{32,40},{40,32},{48,56},{56,48},{64,72... | collective-permute-start | bytes 73736 | tf_op jit(solution)/shard_map/ppermute | solution.py:482
  19.4 0.5 collective-permute-done.4.from3_ref
  19.9 3.0 %collective-permute-done.3.from2_ref = f32[48,128]{1,0:T(8,128)S(1)} collective-permute-done((f32[48,128]{1,0:T(8,128)S(1)}, f32[48,128]{1,0:T(8,128)S(1)}, u32[]{:S(2)}, u32[]{:S(2)}) %collective-permute-start.3) | collective-permute-done | bytes 24608 | tf_op jit(solution)/shard_map/ppermute | solution.py:482
  22.9 0.4 groups.1
  23.2 16.7 %all_to_all.5 = f32[8,48,128]{2,1,0:T(8,128)S(1)} all-to-all(f32[8,48,128]{2,1,0:T(8,128)S(1)} %get-tuple-element.25), channel_id=1, replica_groups={{0,32,64,96,128,160,192,224},{8,40,72,104,136,168,200,232},{16,48,80,11..., dimensions={0} | all-to-all | bytes 393216 | tf_op jit(solution)/shard_map/all_to_all | solution.py:493
  39.9 2.2 %sweeps.1 = (f32[2,4,64,128]{3,2,1,0:T(8,128)}, f32[4,64,128]{2,1,0:T(8,128)S(1)}) custom-call(s32[1]{0:T(128)} %bitcast.place_ref, f32[384,128]{1,0:T(8,128)S(1)} %bitcast.7, f32[4,48,128]{2,1,0:T(8,128)S(1)} %get-tuple-element.26.blocks_ref, f32[56,256]{1,0:T(8,128)S(1)} %get-tuple-element.27.saved_ref, ...), custom_call_target="tpu_custom_call" | custom-call | flops 1000000000 | bytes 2097152 | tf_op jit(solution)/shard_map/sweeps/pallas_call | solution.py:494
  42.1 2.7 %collective-permute-start.7 = (f32[4,64,128]{2,1,0:T(8,128)S(1)}, f32[4,64,128]{2,1,0:T(8,128)S(1)}, u32[]{:S(2)}, u32[]{:S(2)}) collective-permute-start(f32[4,64,128]{2,1,0:T(8,128)S(1)} %get-tuple-element.31), channel_id=1, source_target_pairs={{0,6},{1,7},{2,4},{3,5},{4,2},{5,3},{6,0},{7,1},{8,14},{9,15},{10,... | collective-permute-start | bytes 393224 | tf_op jit(solution)/shard_map/ppermute | solution.py:505
  44.9 0.3 collective-permute-start.6
  45.2 0.2 collective-permute-start.5
  45.4 2.7 %collective-permute-done.7 = f32[4,64,128]{2,1,0:T(8,128)S(1)} collective-permute-done((f32[4,64,128]{2,1,0:T(8,128)S(1)}, f32[4,64,128]{2,1,0:T(8,128)S(1)}, u32[]{:S(2)}, u32[]{:S(2)}) %collective-permute-start.7) | collective-permute-done | bytes 131104 | tf_op jit(solution)/shard_map/ppermute | solution.py:505
  48.2 2.0 %collective-permute-done.6 = f32[4,64,128]{2,1,0:T(8,128)S(1)} collective-permute-done((f32[4,64,128]{2,1,0:T(8,128)S(1)}, f32[4,64,128]{2,1,0:T(8,128)S(1)}, u32[]{:S(2)}, u32[]{:S(2)}) %collective-permute-start.6) | collective-permute-done | bytes 131104 | tf_op jit(solution)/shard_map/ppermute | solution.py:505
  50.2 0.0 copy-start.7
  50.2 6.4 %collective-permute-start.8 = (f32[4,64,128]{2,1,0:T(8,128)S(1)}, f32[4,64,128]{2,1,0:T(8,128)S(1)}, u32[]{:S(2)}, u32[]{:S(2)}) collective-permute-start(f32[4,64,128]{2,1,0:T(8,128)S(1)} %add_add_fusion), channel_id=1, source_target_pairs={{0,1},{1,0},{2,3},{3,2},{4,5},{5,4},{6,7},{7,6},{8,9},{9,8},{10,11... | collective-permute-start | bytes 393224 | tf_op jit(solution)/shard_map/ppermute | solution.py:506
  56.6 1.0 %collective-permute-done.8 = f32[4,64,128]{2,1,0:T(8,128)S(1)} collective-permute-done((f32[4,64,128]{2,1,0:T(8,128)S(1)}, f32[4,64,128]{2,1,0:T(8,128)S(1)}, u32[]{:S(2)}, u32[]{:S(2)}) %collective-permute-start.8) | collective-permute-done | bytes 131104 | tf_op jit(solution)/shard_map/ppermute | solution.py:506
  57.6 0.7 %broadcast_subtract_fusion = f32[2,4,64,128]{3,2,1,0:T(8,128)} fusion(f32[2,4,64,128]{3,2,1,0:T(8,128)S(1)} %copy-done.7, f32[4,64,128]{2,1,0:T(8,128)S(1)} %add_multiply_fusion), kind=kLoop, calls=%fused_computation | loop fusion | flops 65536 | bytes 655360 | tf_op jit(solution)/shard_map/sub | solution.py:507
  (19 shorter events, 0.1 us)
Async XLA Ops:
  1.3 8.2 %copy-start = (f32[2,4,64,128]{3,2,1,0:T(8,128)S(1)}, f32[2,4,64,128]{3,2,1,0:T(8,128)}, u32[]{:S(2)}) copy-start(f32[2,4,64,128]{3,2,1,0:T(8,128)} %head_ref.1) | copy-start | bytes 786436
  1.3 8.2 %copy-start.1 = (f32[4,64,128]{2,1,0:T(8,128)S(1)}, f32[4,64,128]{2,1,0:T(8,128)}, u32[]{:S(2)}) copy-start(f32[4,64,128]{2,1,0:T(8,128)} %storage_ref.1) | copy-start | bytes 393220
  1.3 8.2 %copy-start.2 = (f32[4,64,128]{2,1,0:T(8,128)S(1)}, f32[4,64,128]{2,1,0:T(8,128)}, u32[]{:S(2)}) copy-start(f32[4,64,128]{2,1,0:T(8,128)} %flow_ref.1) | copy-start | bytes 393220
  1.3 8.2 %copy-start.3 = (f32[4,64,128]{2,1,0:T(8,128)S(1)}, f32[4,64,128]{2,1,0:T(8,128)}, u32[]{:S(2)}) copy-start(f32[4,64,128]{2,1,0:T(8,128)} %cross_ref.1) | copy-start | bytes 393220
  1.3 8.2 %copy-start.4 = (f32[4,64,128]{2,1,0:T(8,128)S(1)}, f32[4,64,128]{2,1,0:T(8,128)}, u32[]{:S(2)}) copy-start(f32[4,64,128]{2,1,0:T(8,128)} %vert_ref.1) | copy-start | bytes 393220
  1.3 8.2 %copy-start.5 = (s32[4,64,128]{2,1,0:T(8,128)S(1)}, s32[4,64,128]{2,1,0:T(8,128)}, u32[]{:S(2)}) copy-start(s32[4,64,128]{2,1,0:T(8,128)} %active_ref.1) | copy-start | bytes 393220
  6.6 4.2 %collective-permute-start = (f32[128,128]{1,0:T(8,128)}, f32[128,128]{1,0:T(8,128)S(1)}, u32[]{:S(2)}, u32[]{:S(2)}) collective-permute-start(f32[128,128]{1,0:T(8,128)} %get-tuple-element.21), channel_id=1, source_target_pairs={{0,8},{8,0},{16,24},{24,16},{32,40},{40,32},{48,56},{56,48},{64,72... | collective-permute-start | bytes 196616 | tf_op jit(solution)/shard_map/ppermute | solution.py:462
  8.7 2.2 %copy-start.6 = (f32[128,128]{1,0:T(8,128)S(1)}, f32[128,128]{1,0:T(8,128)}, u32[]{:S(2)}) copy-start(f32[128,128]{1,0:T(8,128)} %get-tuple-element.20.own_ref) | copy-start | bytes 196612
  8.7 2.2 %collective-permute-start.1 = (f32[128,128]{1,0:T(8,128)}, f32[128,128]{1,0:T(8,128)S(1)}, u32[]{:S(2)}, u32[]{:S(2)}) collective-permute-start(f32[128,128]{1,0:T(8,128)} %get-tuple-element.22), channel_id=1, source_target_pairs={{8,16},{16,8},{24,32},{32,24},{40,48},{48,40},{56,64},{64,56},{72,... | collective-permute-start | bytes 196616 | tf_op jit(solution)/shard_map/ppermute | solution.py:463
  11.5 8.4 %collective-permute-start.4 = (f32[48,128]{1,0:T(8,128)S(1)}, f32[48,128]{1,0:T(8,128)S(1)}, u32[]{:S(2)}, u32[]{:S(2)}) collective-permute-start(f32[48,128]{1,0:T(8,128)S(1)} %get-tuple-element.24.own_ref), channel_id=1, source_target_pairs={{0,24},{8,16},{16,8},{24,0},{32,56},{40,48},{48,40},{56,32},{64,88... | collective-permute-start | bytes 73736 | tf_op jit(solution)/shard_map/ppermute | solution.py:482
  18.7 4.2 %collective-permute-start.3 = (f32[48,128]{1,0:T(8,128)S(1)}, f32[48,128]{1,0:T(8,128)S(1)}, u32[]{:S(2)}, u32[]{:S(2)}) collective-permute-start(f32[48,128]{1,0:T(8,128)S(1)} %get-tuple-element.24.own_ref), channel_id=1, source_target_pairs={{0,16},{8,24},{16,0},{24,8},{32,48},{40,56},{48,32},{56,40},{64,80... | collective-permute-start | bytes 73736 | tf_op jit(solution)/shard_map/ppermute | solution.py:482
  18.7 4.2 %collective-permute-start.2 = (f32[48,128]{1,0:T(8,128)S(1)}, f32[48,128]{1,0:T(8,128)S(1)}, u32[]{:S(2)}, u32[]{:S(2)}) collective-permute-start(f32[48,128]{1,0:T(8,128)S(1)} %get-tuple-element.24.own_ref), channel_id=1, source_target_pairs={{0,8},{8,0},{16,24},{24,16},{32,40},{40,32},{48,56},{56,48},{64,72... | collective-permute-start | bytes 73736 | tf_op jit(solution)/shard_map/ppermute | solution.py:482
  42.1 6.1 %collective-permute-start.7 = (f32[4,64,128]{2,1,0:T(8,128)S(1)}, f32[4,64,128]{2,1,0:T(8,128)S(1)}, u32[]{:S(2)}, u32[]{:S(2)}) collective-permute-start(f32[4,64,128]{2,1,0:T(8,128)S(1)} %get-tuple-element.31), channel_id=1, source_target_pairs={{0,6},{1,7},{2,4},{3,5},{4,2},{5,3},{6,0},{7,1},{8,14},{9,15},{10,... | collective-permute-start | bytes 393224 | tf_op jit(solution)/shard_map/ppermute | solution.py:505
  44.9 5.3 %collective-permute-start.6 = (f32[4,64,128]{2,1,0:T(8,128)S(1)}, f32[4,64,128]{2,1,0:T(8,128)S(1)}, u32[]{:S(2)}, u32[]{:S(2)}) collective-permute-start(f32[4,64,128]{2,1,0:T(8,128)S(1)} %get-tuple-element.31), channel_id=1, source_target_pairs={{0,4},{1,5},{2,6},{3,7},{4,0},{5,1},{6,2},{7,3},{8,12},{9,13},{10,... | collective-permute-start | bytes 393224 | tf_op jit(solution)/shard_map/ppermute | solution.py:505
  45.2 5.0 %collective-permute-start.5 = (f32[4,64,128]{2,1,0:T(8,128)S(1)}, f32[4,64,128]{2,1,0:T(8,128)S(1)}, u32[]{:S(2)}, u32[]{:S(2)}) collective-permute-start(f32[4,64,128]{2,1,0:T(8,128)S(1)} %get-tuple-element.31), channel_id=1, source_target_pairs={{0,2},{1,3},{2,0},{3,1},{4,6},{5,7},{6,4},{7,5},{8,10},{9,11},{10,... | collective-permute-start | bytes 393224 | tf_op jit(solution)/shard_map/ppermute | solution.py:505
  50.2 7.4 %copy-start.7 = (f32[2,4,64,128]{3,2,1,0:T(8,128)S(1)}, f32[2,4,64,128]{3,2,1,0:T(8,128)}, u32[]{:S(2)}) copy-start(f32[2,4,64,128]{3,2,1,0:T(8,128)} %get-tuple-element.15) | copy-start | bytes 786436
  50.2 7.4 %collective-permute-start.8 = (f32[4,64,128]{2,1,0:T(8,128)S(1)}, f32[4,64,128]{2,1,0:T(8,128)S(1)}, u32[]{:S(2)}, u32[]{:S(2)}) collective-permute-start(f32[4,64,128]{2,1,0:T(8,128)S(1)} %add_add_fusion), channel_id=1, source_target_pairs={{0,1},{1,0},{2,3},{3,2},{4,5},{5,4},{6,7},{7,6},{8,9},{9,8},{10,11... | collective-permute-start | bytes 393224 | tf_op jit(solution)/shard_map/ppermute | solution.py:506

commit v5 on v4

--- a/solution.py
+++ b/solution.py
@@ -316,10 +316,10 @@
     return out
 
 
-def group_kernel(place_ref, own_ref, from1_ref, from2_ref, from3_ref, blocks_ref, saved_ref, out_ref, block):
+def group_kernel(place_ref, own_ref, from1_ref, from3_ref, from2_ref, blocks_ref, saved_ref, out_ref, block):
     per = blocks_ref.shape[0]
     place = lax.rem(place_ref[0], per)
-    for k, ref in enumerate((own_ref, from1_ref, from2_ref, from3_ref)):
+    for k, ref in ((0, own_ref), (1, from1_ref), (3, from3_ref), (2, from2_ref)):
         blocks_ref[lax.bitwise_xor(place, k)] = ref[...]
     got = [member(blocks_ref, p) for p in range(per)]
     leak, face = [], []
@@ -459,8 +459,8 @@
     )(
         hru_cells.T, hru_area.T, hru_land.reshape(1, slots), hru_bmp, rain.reshape(1, slots), perc_table.T, hru_live, place
     )
-    low = lax.ppermute(first, "flow", [(i, i ^ 1) for i in range(devices)])
-    high = lax.ppermute(second, "flow", [(i, i - 1 + 2 * (i % 2)) for i in range(1, devices - 1)])
+    low = lax.ppermute(second, "flow", [(i, i - 1 + 2 * (i % 2)) for i in range(1, devices - 1)])
+    high = lax.ppermute(first, "flow", [(i, i ^ 1) for i in range(devices)])
     fields, small, base, coefs = kernel_call(
         coefficient_kernel,
         "coefficients",
@@ -479,7 +479,7 @@
     )(fields, small, base, own, low, high, coefs)
     per = devices // SUBS
     around = [
-        lax.ppermute(block, "flow", [(i, i ^ k) for i in range(devices)]) for k in range(1, per)
+        lax.ppermute(block, "flow", [(i, i ^ k) for i in range(devices)]) for k in (1, 3, 2)
     ]
     blocks, saved, block = kernel_call(
         group_kernel,
@@ -501,7 +501,7 @@
     )(place, gathered.reshape(SUBS * 2 * ROWS, 128), blocks, saved, fields, small, source, inner)
     lanes = lax.axis_size("lane")
     whole = total
-    for k in range(2, lanes, 2):
+    for k in (2, 6, 4):
         whole = whole + lax.ppermute(total, "lane", [(i, i ^ k) for i in range(lanes)])
     whole = whole + lax.ppermute(whole, "lane", [(i, i ^ 1) for i in range(lanes)])
     anomaly = head - whole[None] / (2 * lanes)

time: 58.5 us -> 56.8 us (0.971)
  starting transfers between devices: 20.4 us -> 19.6 us
    ppermute x3, starting transfers between devices: 7.86 us -> 4.17 us  [on_device(): lax.ppermute(block, 'flow', [(i, i ^ k) for i in range(devices)])]
    ppermute x1, starting transfers between devices: 2.04 us -> 4.58 us  [on_device(): high = lax.ppermute(first, 'flow', [(i, i ^ 1) for i in range(devices)])]
    ppermute x3, waiting for transfers between devices: 3.51 us -> 2.89 us  [on_device(): lax.ppermute(block, 'flow', [(i, i ^ k) for i in range(devices)])]
  transfers between devices with their start and end apart: 9 -> 9, of which waited for: 5 -> 6; matrix products, arithmetic and copies ran while one was open for 0% -> 0% of each run, Pallas kernels for 2% -> 2%
where the time goes in v5:
time: 56.8 us; the launch traced here: 56.7 us
  starting transfers between devices  19.6 us (35%)
  blocking collectives  16.4 us (29%)
  Pallas kernels  9.75 us (17%)
  waiting for transfers between devices  8.67 us (15%)
  between operations  1.42 us (2%)
  other arithmetic  0.78 us (1%)
    all_to_all x1, blocking collectives, on_device(): lax.all_to_all(block, 'flow', split_axis=0, concat_axis=0, axis_index_gro...  16.4 us
    ppermute x1, starting transfers between devices, on_device(): lax.ppermute(whole, 'lane', [(i, i ^ 1) for i in range(lanes)])  6.56 us
    pallas_call x1, Pallas kernels, on_device(): pl.pallas_call(scatter_kernel, name='scatter', grid=(1,), in_specs=[pl.Bl...  5.3 us
    ppermute x1, starting transfers between devices, on_device(): high = lax.ppermute(first, 'flow', [(i, i ^ 1) for i in range(devices)])  4.58 us
    ppermute x3, waiting for transfers between devices, on_device(): lax.ppermute(total, 'lane', [(i, i ^ k) for i in range(lanes)])  4.26 us
    ppermute x3, starting transfers between devices, on_device(): lax.ppermute(block, 'flow', [(i, i ^ k) for i in range(devices)])  4.17 us
    ppermute x3, starting transfers between devices, on_device(): lax.ppermute(total, 'lane', [(i, i ^ k) for i in range(lanes)])  3.69 us
    ppermute x3, waiting for transfers between devices, on_device(): lax.ppermute(block, 'flow', [(i, i ^ k) for i in range(devices)])  2.89 us
  transfers between devices with their start and end apart: 9, of which 6 were waited for; matrix products, arithmetic and copies ran while one was open for 0% of the time, Pallas kernels for 2%

profile of v5, /device:TPU:1, one launch (start us, length us, event | category | flops | bytes accessed | tf_op | source)
XLA Modules:
  0.0 56.7 jit_solution(11798694423687659004)
XLA Ops:
  1.3 5.3 %scatter.1 = (f32[128,128]{1,0:T(8,128)}, f32[128,128]{1,0:T(8,128)}, f32[128,128]{1,0:T(8,128)}) custom-call(s32[4,4096]{1,0:T(4,128)} %bitcast.8, f32[4,4096]{1,0:T(4,128)} %bitcast.9, s32[1,4096]{1,0:T(1,128)} %bitcast.10, s32[2,4096]{1,0:T(2,128)} %bmp_ref.1, f32[1,4096]{1,0:T(1,128)} %bitcast.11, f32[8,16]{1,0:T(8,128)} %bitcast.12, ...), custom_call_target="tpu_custom_call" | custom-call | flops 4000000000 | bytes 2097152 | tf_op jit(solution)/shard_map/scatter/pallas_call | solution.py:449
  6.6 0.7 %collective-permute-start = (f32[128,128]{1,0:T(8,128)}, f32[128,128]{1,0:T(8,128)S(1)}, u32[]{:S(2)}, u32[]{:S(2)}) collective-permute-start(f32[128,128]{1,0:T(8,128)} %get-tuple-element.21), channel_id=1, source_target_pairs={{8,16},{16,8},{24,32},{32,24},{40,48},{48,40},{56,64},{64,56},{72,... | collective-permute-start | bytes 196616 | tf_op jit(solution)/shard_map/ppermute | solution.py:462
  7.3 0.0 copy-start.6
  7.3 4.6 %collective-permute-start.1 = (f32[128,128]{1,0:T(8,128)}, f32[128,128]{1,0:T(8,128)S(1)}, u32[]{:S(2)}, u32[]{:S(2)}) collective-permute-start(f32[128,128]{1,0:T(8,128)} %get-tuple-element.22), channel_id=1, source_target_pairs={{0,8},{8,0},{16,24},{24,16},{32,40},{40,32},{48,56},{56,48},{64,72... | collective-permute-start | bytes 196616 | tf_op jit(solution)/shard_map/ppermute | solution.py:463
  11.9 1.3 %coefficients.1 = (f32[8,16,8,256]{3,2,1,0:T(8,128)S(1)}, f32[3,16,256]{2,1,0:T(8,128)S(1)}, f32[4,16,8,256]{3,2,1,0:T(8,128)S(1)}, f32[16,256]{1,0:T(8,128)S(1)}) custom-call(f32[2,4,64,128]{3,2,1,0:T(8,128)S(1)} %copy-done, f32[4,64,128]{2,1,0:T(8,128)S(1)} %copy-done.1, f32[4,64,128]{2,1,0:T(8,128)S(1)} %copy-done.2, f32[4,64,128]{2,1,0:T(8,128)S(1)} %copy-done.3, ...), custom_call_target="tpu_custom_call" | custom-call | flops 4000000000 | bytes 2097152 | tf_op jit(solution)/shard_map/coefficients/pallas_call | solution.py:464
  13.2 0.0 collective-permute-done.low_ref
  13.2 0.5 collective-permute-done.1.high_ref
  13.8 0.6 %sources.1 = (f32[2,16,8,256]{3,2,1,0:T(8,128)S(1)}, f32[2,16,8,256]{3,2,1,0:T(8,128)S(1)}, f32[48,128]{1,0:T(8,128)S(1)}) custom-call(f32[8,16,8,256]{3,2,1,0:T(8,128)S(1)} %get-tuple-element.17.fields_ref, f32[3,16,256]{2,1,0:T(8,128)S(1)} %get-tuple-element.18.small_ref, f32[4,16,8,256]{3,2,1,0:T(8,128)S(1)} %get-tuple-element.19.base_ref, ...), custom_call_target="tpu_custom_call" | custom-call | flops 1000000000 | bytes 2097152 | tf_op jit(solution)/shard_map/sources/pallas_call | solution.py:472
  14.4 3.2 %collective-permute-start.4 = (f32[48,128]{1,0:T(8,128)S(1)}, f32[48,128]{1,0:T(8,128)S(1)}, u32[]{:S(2)}, u32[]{:S(2)}) collective-permute-start(f32[48,128]{1,0:T(8,128)S(1)} %get-tuple-element.24.own_ref), channel_id=1, source_target_pairs={{0,16},{8,24},{16,0},{24,8},{32,48},{40,56},{48,32},{56,40},{64,80... | collective-permute-start | bytes 73736 | tf_op jit(solution)/shard_map/ppermute | solution.py:482
  17.6 0.9 %collective-permute-start.3 = (f32[48,128]{1,0:T(8,128)S(1)}, f32[48,128]{1,0:T(8,128)S(1)}, u32[]{:S(2)}, u32[]{:S(2)}) collective-permute-start(f32[48,128]{1,0:T(8,128)S(1)} %get-tuple-element.24.own_ref), channel_id=1, source_target_pairs={{0,24},{8,16},{16,8},{24,0},{32,56},{40,48},{48,40},{56,32},{64,88... | collective-permute-start | bytes 73736 | tf_op jit(solution)/shard_map/ppermute | solution.py:482
  18.4 0.1 collective-permute-start.2
  18.6 0.2 collective-permute-done.4.from2_ref
  18.8 2.7 %collective-permute-done.3.from3_ref = f32[48,128]{1,0:T(8,128)S(1)} collective-permute-done((f32[48,128]{1,0:T(8,128)S(1)}, f32[48,128]{1,0:T(8,128)S(1)}, u32[]{:S(2)}, u32[]{:S(2)}) %collective-permute-start.3) | collective-permute-done | bytes 24608 | tf_op jit(solution)/shard_map/ppermute | solution.py:482
  21.5 0.4 groups.1
  21.8 16.4 %all_to_all.5 = f32[8,48,128]{2,1,0:T(8,128)S(1)} all-to-all(f32[8,48,128]{2,1,0:T(8,128)S(1)} %get-tuple-element.25), channel_id=1, replica_groups={{0,32,64,96,128,160,192,224},{8,40,72,104,136,168,200,232},{16,48,80,11..., dimensions={0} | all-to-all | bytes 393216 | tf_op jit(solution)/shard_map/all_to_all | solution.py:493
  38.2 2.2 %sweeps.1 = (f32[2,4,64,128]{3,2,1,0:T(8,128)}, f32[4,64,128]{2,1,0:T(8,128)S(1)}) custom-call(s32[1]{0:T(128)} %bitcast.place_ref, f32[384,128]{1,0:T(8,128)S(1)} %bitcast.7, f32[4,48,128]{2,1,0:T(8,128)S(1)} %get-tuple-element.26.blocks_ref, f32[56,256]{1,0:T(8,128)S(1)} %get-tuple-element.27.saved_ref, ...), custom_call_target="tpu_custom_call" | custom-call | flops 1000000000 | bytes 2097152 | tf_op jit(solution)/shard_map/sweeps/pallas_call | solution.py:494
  40.4 2.9 %collective-permute-start.7 = (f32[4,64,128]{2,1,0:T(8,128)S(1)}, f32[4,64,128]{2,1,0:T(8,128)S(1)}, u32[]{:S(2)}, u32[]{:S(2)}) collective-permute-start(f32[4,64,128]{2,1,0:T(8,128)S(1)} %get-tuple-element.31), channel_id=1, source_target_pairs={{0,4},{1,5},{2,6},{3,7},{4,0},{5,1},{6,2},{7,3},{8,12},{9,13},{10,... | collective-permute-start | bytes 393224 | tf_op jit(solution)/shard_map/ppermute | solution.py:505
  43.3 0.8 %collective-permute-start.6 = (f32[4,64,128]{2,1,0:T(8,128)S(1)}, f32[4,64,128]{2,1,0:T(8,128)S(1)}, u32[]{:S(2)}, u32[]{:S(2)}) collective-permute-start(f32[4,64,128]{2,1,0:T(8,128)S(1)} %get-tuple-element.31), channel_id=1, source_target_pairs={{0,6},{1,7},{2,4},{3,5},{4,2},{5,3},{6,0},{7,1},{8,14},{9,15},{10,... | collective-permute-start | bytes 393224 | tf_op jit(solution)/shard_map/ppermute | solution.py:505
  44.1 1.6 %collective-permute-done.7 = f32[4,64,128]{2,1,0:T(8,128)S(1)} collective-permute-done((f32[4,64,128]{2,1,0:T(8,128)S(1)}, f32[4,64,128]{2,1,0:T(8,128)S(1)}, u32[]{:S(2)}, u32[]{:S(2)}) %collective-permute-start.7) | collective-permute-done | bytes 131104 | tf_op jit(solution)/shard_map/ppermute | solution.py:505
  45.7 2.6 %collective-permute-done.6 = f32[4,64,128]{2,1,0:T(8,128)S(1)} collective-permute-done((f32[4,64,128]{2,1,0:T(8,128)S(1)}, f32[4,64,128]{2,1,0:T(8,128)S(1)}, u32[]{:S(2)}, u32[]{:S(2)}) %collective-permute-start.6) | collective-permute-done | bytes 131104 | tf_op jit(solution)/shard_map/ppermute | solution.py:505
  48.4 0.0 copy-start.7
  48.4 6.6 %collective-permute-start.8 = (f32[4,64,128]{2,1,0:T(8,128)S(1)}, f32[4,64,128]{2,1,0:T(8,128)S(1)}, u32[]{:S(2)}, u32[]{:S(2)}) collective-permute-start(f32[4,64,128]{2,1,0:T(8,128)S(1)} %add_add_fusion), channel_id=1, source_target_pairs={{0,1},{1,0},{2,3},{3,2},{4,5},{5,4},{6,7},{7,6},{8,9},{9,8},{10,11... | collective-permute-start | bytes 393224 | tf_op jit(solution)/shard_map/ppermute | solution.py:506
  54.9 1.0 %collective-permute-done.8 = f32[4,64,128]{2,1,0:T(8,128)S(1)} collective-permute-done((f32[4,64,128]{2,1,0:T(8,128)S(1)}, f32[4,64,128]{2,1,0:T(8,128)S(1)}, u32[]{:S(2)}, u32[]{:S(2)}) %collective-permute-start.8) | collective-permute-done | bytes 131104 | tf_op jit(solution)/shard_map/ppermute | solution.py:506
  55.9 0.7 %broadcast_subtract_fusion = f32[2,4,64,128]{3,2,1,0:T(8,128)} fusion(f32[2,4,64,128]{3,2,1,0:T(8,128)S(1)} %copy-done.7, f32[4,64,128]{2,1,0:T(8,128)S(1)} %add_multiply_fusion), kind=kLoop, calls=%fused_computation | loop fusion | flops 65536 | bytes 655360 | tf_op jit(solution)/shard_map/sub | solution.py:507
  (19 shorter events, 0.1 us)
Async XLA Ops:
  1.3 10.6 %copy-start = (f32[2,4,64,128]{3,2,1,0:T(8,128)S(1)}, f32[2,4,64,128]{3,2,1,0:T(8,128)}, u32[]{:S(2)}) copy-start(f32[2,4,64,128]{3,2,1,0:T(8,128)} %head_ref.1) | copy-start | bytes 786436
  1.3 10.6 %copy-start.1 = (f32[4,64,128]{2,1,0:T(8,128)S(1)}, f32[4,64,128]{2,1,0:T(8,128)}, u32[]{:S(2)}) copy-start(f32[4,64,128]{2,1,0:T(8,128)} %storage_ref.1) | copy-start | bytes 393220
  1.3 10.6 %copy-start.2 = (f32[4,64,128]{2,1,0:T(8,128)S(1)}, f32[4,64,128]{2,1,0:T(8,128)}, u32[]{:S(2)}) copy-start(f32[4,64,128]{2,1,0:T(8,128)} %flow_ref.1) | copy-start | bytes 393220
  1.3 10.6 %copy-start.3 = (f32[4,64,128]{2,1,0:T(8,128)S(1)}, f32[4,64,128]{2,1,0:T(8,128)}, u32[]{:S(2)}) copy-start(f32[4,64,128]{2,1,0:T(8,128)} %cross_ref.1) | copy-start | bytes 393220
  1.3 10.6 %copy-start.4 = (f32[4,64,128]{2,1,0:T(8,128)S(1)}, f32[4,64,128]{2,1,0:T(8,128)}, u32[]{:S(2)}) copy-start(f32[4,64,128]{2,1,0:T(8,128)} %vert_ref.1) | copy-start | bytes 393220
  1.3 10.6 %copy-start.5 = (s32[4,64,128]{2,1,0:T(8,128)S(1)}, s32[4,64,128]{2,1,0:T(8,128)}, u32[]{:S(2)}) copy-start(s32[4,64,128]{2,1,0:T(8,128)} %active_ref.1) | copy-start | bytes 393220
  6.6 6.6 %collective-permute-start = (f32[128,128]{1,0:T(8,128)}, f32[128,128]{1,0:T(8,128)S(1)}, u32[]{:S(2)}, u32[]{:S(2)}) collective-permute-start(f32[128,128]{1,0:T(8,128)} %get-tuple-element.21), channel_id=1, source_target_pairs={{8,16},{16,8},{24,32},{32,24},{40,48},{48,40},{56,64},{64,56},{72,... | collective-permute-start | bytes 196616 | tf_op jit(solution)/shard_map/ppermute | solution.py:462
  7.3 6.5 %copy-start.6 = (f32[128,128]{1,0:T(8,128)S(1)}, f32[128,128]{1,0:T(8,128)}, u32[]{:S(2)}) copy-start(f32[128,128]{1,0:T(8,128)} %get-tuple-element.20.own_ref) | copy-start | bytes 196612
  7.3 6.4 %collective-permute-start.1 = (f32[128,128]{1,0:T(8,128)}, f32[128,128]{1,0:T(8,128)S(1)}, u32[]{:S(2)}, u32[]{:S(2)}) collective-permute-start(f32[128,128]{1,0:T(8,128)} %get-tuple-element.22), channel_id=1, source_target_pairs={{0,8},{8,0},{16,24},{24,16},{32,40},{40,32},{48,56},{56,48},{64,72... | collective-permute-start | bytes 196616 | tf_op jit(solution)/shard_map/ppermute | solution.py:463
  14.4 4.4 %collective-permute-start.4 = (f32[48,128]{1,0:T(8,128)S(1)}, f32[48,128]{1,0:T(8,128)S(1)}, u32[]{:S(2)}, u32[]{:S(2)}) collective-permute-start(f32[48,128]{1,0:T(8,128)S(1)} %get-tuple-element.24.own_ref), channel_id=1, source_target_pairs={{0,16},{8,24},{16,0},{24,8},{32,48},{40,56},{48,32},{56,40},{64,80... | collective-permute-start | bytes 73736 | tf_op jit(solution)/shard_map/ppermute | solution.py:482
  17.6 3.9 %collective-permute-start.3 = (f32[48,128]{1,0:T(8,128)S(1)}, f32[48,128]{1,0:T(8,128)S(1)}, u32[]{:S(2)}, u32[]{:S(2)}) collective-permute-start(f32[48,128]{1,0:T(8,128)S(1)} %get-tuple-element.24.own_ref), channel_id=1, source_target_pairs={{0,24},{8,16},{16,8},{24,0},{32,56},{40,48},{48,40},{56,32},{64,88... | collective-permute-start | bytes 73736 | tf_op jit(solution)/shard_map/ppermute | solution.py:482
  18.4 3.0 %collective-permute-start.2 = (f32[48,128]{1,0:T(8,128)S(1)}, f32[48,128]{1,0:T(8,128)S(1)}, u32[]{:S(2)}, u32[]{:S(2)}) collective-permute-start(f32[48,128]{1,0:T(8,128)S(1)} %get-tuple-element.24.own_ref), channel_id=1, source_target_pairs={{0,8},{8,0},{16,24},{24,16},{32,40},{40,32},{48,56},{56,48},{64,72... | collective-permute-start | bytes 73736 | tf_op jit(solution)/shard_map/ppermute | solution.py:482
  40.4 5.3 %collective-permute-start.7 = (f32[4,64,128]{2,1,0:T(8,128)S(1)}, f32[4,64,128]{2,1,0:T(8,128)S(1)}, u32[]{:S(2)}, u32[]{:S(2)}) collective-permute-start(f32[4,64,128]{2,1,0:T(8,128)S(1)} %get-tuple-element.31), channel_id=1, source_target_pairs={{0,4},{1,5},{2,6},{3,7},{4,0},{5,1},{6,2},{7,3},{8,12},{9,13},{10,... | collective-permute-start | bytes 393224 | tf_op jit(solution)/shard_map/ppermute | solution.py:505
  43.3 5.0 %collective-permute-start.6 = (f32[4,64,128]{2,1,0:T(8,128)S(1)}, f32[4,64,128]{2,1,0:T(8,128)S(1)}, u32[]{:S(2)}, u32[]{:S(2)}) collective-permute-start(f32[4,64,128]{2,1,0:T(8,128)S(1)} %get-tuple-element.31), channel_id=1, source_target_pairs={{0,6},{1,7},{2,4},{3,5},{4,2},{5,3},{6,0},{7,1},{8,14},{9,15},{10,... | collective-permute-start | bytes 393224 | tf_op jit(solution)/shard_map/ppermute | solution.py:505
  44.1 4.3 %collective-permute-start.5 = (f32[4,64,128]{2,1,0:T(8,128)S(1)}, f32[4,64,128]{2,1,0:T(8,128)S(1)}, u32[]{:S(2)}, u32[]{:S(2)}) collective-permute-start(f32[4,64,128]{2,1,0:T(8,128)S(1)} %get-tuple-element.31), channel_id=1, source_target_pairs={{0,2},{1,3},{2,0},{3,1},{4,6},{5,7},{6,4},{7,5},{8,10},{9,11},{10,... | collective-permute-start | bytes 393224 | tf_op jit(solution)/shard_map/ppermute | solution.py:505
  48.4 7.6 %copy-start.7 = (f32[2,4,64,128]{3,2,1,0:T(8,128)S(1)}, f32[2,4,64,128]{3,2,1,0:T(8,128)}, u32[]{:S(2)}) copy-start(f32[2,4,64,128]{3,2,1,0:T(8,128)} %get-tuple-element.15) | copy-start | bytes 786436
  48.4 7.5 %collective-permute-start.8 = (f32[4,64,128]{2,1,0:T(8,128)S(1)}, f32[4,64,128]{2,1,0:T(8,128)S(1)}, u32[]{:S(2)}, u32[]{:S(2)}) collective-permute-start(f32[4,64,128]{2,1,0:T(8,128)S(1)} %add_add_fusion), channel_id=1, source_target_pairs={{0,1},{1,0},{2,3},{3,2},{4,5},{5,4},{6,7},{7,6},{8,9},{9,8},{10,11... | collective-permute-start | bytes 393224 | tf_op jit(solution)/shard_map/ppermute | solution.py:506

commit v6 on v5

--- a/solution.py
+++ b/solution.py
@@ -316,11 +316,20 @@
     return out
 
 
-def group_kernel(place_ref, own_ref, from1_ref, from3_ref, from2_ref, blocks_ref, saved_ref, out_ref, block):
+def swaps(per):
+    return (1, 3, 2) if per == 4 else (1,)
+
+
+def in_order(blocks_ref, place, received):
     per = blocks_ref.shape[0]
-    place = lax.rem(place_ref[0], per)
-    for k, ref in ((0, own_ref), (1, from1_ref), (3, from3_ref), (2, from2_ref)):
+    for k, ref in zip((0,) + swaps(per), received):
         blocks_ref[lax.bitwise_xor(place, k)] = ref[...]
+
+
+def group_kernel(stride, place_ref, *refs):
+    blocks_ref, saved_ref, out_ref = refs[-3:]
+    per = blocks_ref.shape[0]
+    in_order(blocks_ref, lax.rem(place_ref[0] // stride, per), refs[:per])
     got = [member(blocks_ref, p) for p in range(per)]
     leak, face = [], []
     for p in range(per):
@@ -355,42 +364,47 @@
         for i in range(nodes):
             saved_ref[nodes * (5 + s) + i : nodes * (5 + s) + i + 1] = inner[i]
             saved_ref[nodes * (3 + s) + i : nodes * (3 + s) + i + 1] = basis[s][i]
-    put_block(block, rows)
-    for k in range(out_ref.shape[0]):
-        out_ref[k] = block[...]
-
-
-def sweep_kernel(place_ref, gathered_ref, blocks_ref, saved_ref, fields_ref, small_ref, source_ref, inner_ref,
-                 head_ref, total_ref, ends_scratch, turned):
-    per = blocks_ref.shape[0]
-    groups = gathered_ref.shape[0] // (2 * ROWS)
+    put_block(out_ref, rows)
+
+
+def sweep_kernel(strides, place_ref, *refs):
+    top = refs[-3].shape[0]
+    blocks1_ref, saved1_ref, blocks2_ref, saved2_ref, fields_ref, small_ref, source_ref, inner_ref = refs[top : top + 8]
+    head_ref, total_ref, top_ref, ends_scratch, turned = refs[top + 8 :]
     place = place_ref[0]
-
-    def got(row):
-        return both(lambda h: gathered_ref[pl.ds(ROWS * h + row, groups, stride=2 * ROWS), :])
-
-    face = got(3) * pltpu.roll(got(4), groups - 1, 0)
-    inv, ratio = full_factor(interleave(got(0), got(1)), interleave(got(2), face)[: 2 * groups - 1])
-    nodes = 2 * per
-    saved = [[saved_ref[nodes * k + i : nodes * k + i + 1] for i in range(nodes)] for k in range(7)]
-    at = pl.ds(place // per, 1)
-    pick = pl.ds(lax.rem(place, per), 1)
+    side = place // strides[2]
+    in_order(top_ref, side, refs[:top])
+    got = [member(top_ref, p) for p in range(top)]
+    face = []
+    for p in range(top):
+        face.append(got[p](2))
+        if p + 1 < top:
+            face.append(got[p](3) * got[p + 1](4))
+    inv, ratio = full_factor([got[p](e) for p in range(top) for e in range(2)], face)
+    levels = []
+    for stride, blocks_ref, saved_ref in ((strides[1], blocks2_ref, saved2_ref), (strides[0], blocks1_ref, saved1_ref)):
+        nodes = 2 * blocks_ref.shape[0]
+        rows = [[saved_ref[nodes * k + i : nodes * k + i + 1] for i in range(nodes)] for k in range(7)]
+        levels.append((blocks_ref, rows, pl.ds(lax.rem(place // stride, blocks_ref.shape[0]), 1)))
+
+    def pick(first, second, at):
+        for k, values in enumerate((first[0::2], first[1::2], second[0::2], second[1::2])):
+            for p in range(len(values)):
+                ends_scratch[k, p : p + 1] = values[p]
+        return [ends_scratch[k, at, :] for k in range(4)]
+
     ends = []
     for s in range(2):
-        row = 13 + 4 * s
-        low, high = stack_ends(full_solve(inv, ratio, interleave(got(row), got(row + 1))))
-        later = coupled_ends(got, (got(row + 2), got(row + 3)), low, high)
-        low2, high2 = stack_ends(full_solve(inv, ratio, interleave(*later)))
-        for k, value in enumerate((low, high, low2, high2)):
-            ends_scratch[k] = value
-        low, high, low2, high2 = [ends_scratch[k, at, :] for k in range(4)]
-        first = [saved[5 + s][i] + saved[3][i] * low + saved[4][i] * high for i in range(nodes)]
-        part, _, _ = reduce_source(saved[1], saved[2], group_later(blocks_ref, s, first))
-        second = fill_chain(tuple(saved[:3]), part, low2, high2)
-        for k, values in enumerate((first[0::2], first[1::2], second[0::2], second[1::2])):
-            for p in range(per):
-                ends_scratch[k, p : p + 1] = values[p]
-        ends.append([ends_scratch[k, pick, :] for k in range(4)])
+        first = full_solve(inv, ratio, [got[p](13 + 4 * s + e) for p in range(top) for e in range(2)])
+        second = full_solve(inv, ratio, group_later(top_ref, s, first))
+        low, high, low2, high2 = pick(first, second, pl.ds(side, 1))
+        for blocks_ref, saved, at in levels:
+            nodes = 2 * blocks_ref.shape[0]
+            first = [saved[5 + s][i] + saved[3][i] * low + saved[4][i] * high for i in range(nodes)]
+            part, _, _ = reduce_source(saved[1], saved[2], group_later(blocks_ref, s, first))
+            second = fill_chain(tuple(saved[:3]), part, low2, high2)
+            low, high, low2, high2 = pick(first, second, at)
+        ends.append((low, high, low2, high2))
     coef, coef1 = load_coef(fields_ref, small_ref)
     for s in range(2):
         low1, high1, low2, high2 = ends[s]
@@ -477,28 +491,33 @@
         [tile],
         10**9,
     )(fields, small, base, own, low, high, coefs)
-    per = devices // SUBS
-    around = [
-        lax.ppermute(block, "flow", [(i, i ^ k) for i in range(devices)]) for k in (1, 3, 2)
-    ]
-    blocks, saved, block = kernel_call(
-        group_kernel,
-        "groups",
-        [SMEM] + [VMEM] * per,
-        [(per, 2 * ROWS, 128), (14 * per, 256), (SUBS, 2 * ROWS, 128)],
-        [(2 * ROWS, 128)],
+    sizes = (4, 4, 2)
+    strides = (1, 4, 16)
+    levels = []
+    for stride, per in zip(strides, sizes):
+        size = stride * per
+        around = [
+            lax.ppermute(block, "flow", [(i, i ^ (k * stride)) for i in range(devices)]) for k in swaps(per)
+        ]
+        if size == devices:
+            break
+        blocks, saved, block = kernel_call(
+            functools.partial(group_kernel, stride),
+            "groups",
+            [SMEM] + [VMEM] * per,
+            [(per, 2 * ROWS, 128), (14 * per, 256), (2 * ROWS, 128)],
+            [],
+            10**9,
+        )(place, block, *around)
+        levels += [blocks, saved]
+    head, total = kernel_call(
+        functools.partial(sweep_kernel, strides),
+        "sweeps",
+        [SMEM] + [VMEM] * (sizes[2] + 8),
+        [head_prev.shape, storage.shape],
+        [(sizes[2], 2 * ROWS, 128), (4, SUBS, 256), (2, 2, 128, 128)],
         10**9,
-    )(place, block, *around)
-    same = [[i + per * k for k in range(SUBS)] for i in range(per)]
-    gathered = lax.all_to_all(block, "flow", split_axis=0, concat_axis=0, axis_index_groups=same, tiled=True)
-    head, total = kernel_call(
-        sweep_kernel,
-        "sweeps",
-        [SMEM] + [VMEM] * 7,
-        [head_prev.shape, storage.shape],
-        [(4, SUBS, 256), (2, 2, 128, 128)],
-        10**9,
-    )(place, gathered.reshape(SUBS * 2 * ROWS, 128), blocks, saved, fields, small, source, inner)
+    )(place, block, *around, *levels, fields, small, source, inner)
     lanes = lax.axis_size("lane")
     whole = total
     for k in (2, 6, 4):

time: 56.8 us -> 56.5 us (level)
  blocking collectives: 16.4 us -> 0 us
  starting transfers between devices: 19.6 us -> 30.3 us
  waiting for transfers between devices: 8.67 us -> 13.6 us
    all_to_all x1 -> x0, blocking collectives: 16.4 us -> none  [on_device(): lax.all_to_all(block, 'flow', split_axis=0, concat_axis=0, axis_index_gro...]
    ppermute x3 -> x7, starting transfers between devices: 4.17 us -> 14.6 us  [on_device(): lax.ppermute(block, 'flow', [(i, i ^ k * stride) for i in range(devices)])]
    ppermute x3 -> x7, waiting for transfers between devices: 2.89 us -> 7.78 us  [on_device(): lax.ppermute(block, 'flow', [(i, i ^ k * stride) for i in range(devices)])]
    pallas_call x2 -> x3, Pallas kernels: 2.53 us -> 2.98 us  [the longest x1 2.28 us: on_device(): kernel_call(functools.partial(sweep_kernel, strides), 'sweeps', [SMEM] +...]
  transfers between devices with their start and end apart: 9 -> 13, of which waited for: 6 -> 9; matrix products, arithmetic and copies ran while one was open for 0% -> 0% of each run, Pallas kernels for 2% -> 2%
where the time goes in v6:
time: 56.5 us; the launch traced here: 56.3 us
  starting transfers between devices  30.3 us (54%)
  waiting for transfers between devices  13.6 us (24%)
  Pallas kernels  10.2 us (18%)
  between operations  1.44 us (3%)
  other arithmetic  0.77 us (1%)
    ppermute x7, starting transfers between devices, on_device(): lax.ppermute(block, 'flow', [(i, i ^ k * stride) for i in range(devices)])  14.6 us
    ppermute x7, waiting for transfers between devices, on_device(): lax.ppermute(block, 'flow', [(i, i ^ k * stride) for i in range(devices)])  7.78 us
    ppermute x1, starting transfers between devices, on_device(): lax.ppermute(whole, 'lane', [(i, i ^ 1) for i in range(lanes)])  6.83 us
    pallas_call x1, Pallas kernels, on_device(): pl.pallas_call(scatter_kernel, name='scatter', grid=(1,), in_specs=[pl.Bl...  5.31 us
    ppermute x1, starting transfers between devices, on_device(): high = lax.ppermute(first, 'flow', [(i, i ^ 1) for i in range(devices)])  4.58 us
    ppermute x3, waiting for transfers between devices, on_device(): lax.ppermute(total, 'lane', [(i, i ^ k) for i in range(lanes)])  4.26 us
    ppermute x3, starting transfers between devices, on_device(): lax.ppermute(total, 'lane', [(i, i ^ k) for i in range(lanes)])  3.69 us
    pallas_call x1, Pallas kernels, on_device(): kernel_call(functools.partial(sweep_kernel, strides), 'sweeps', [SMEM] +...  2.28 us
  transfers between devices with their start and end apart: 13, of which 9 were waited for; matrix products, arithmetic and copies ran while one was open for 0% of the time, Pallas kernels for 2%

profile of v6, /device:TPU:1, one launch (start us, length us, event | category | flops | bytes accessed | tf_op | source)
XLA Modules:
  0.0 56.3 jit_solution(5751880633892562462)
XLA Ops:
  1.3 5.3 %scatter.1 = (f32[128,128]{1,0:T(8,128)}, f32[128,128]{1,0:T(8,128)}, f32[128,128]{1,0:T(8,128)}) custom-call(s32[4,4096]{1,0:T(4,128)} %bitcast.6, f32[4,4096]{1,0:T(4,128)} %bitcast.7, s32[1,4096]{1,0:T(1,128)} %bitcast.8, s32[2,4096]{1,0:T(2,128)} %bmp_ref.1, f32[1,4096]{1,0:T(1,128)} %bitcast.9, f32[8,16]{1,0:T(8,128)} %bitcast.10, s32[1]{0:T(128)S(6)} %copy.15.live_ref, ...), custom_call_target="tpu_custom_call" | custom-call | flops 4000000000 | bytes 2097152 | tf_op jit(solution)/shard_map/scatter/pallas_call | solution.py:463
  6.7 0.7 %collective-permute-start = (f32[128,128]{1,0:T(8,128)}, f32[128,128]{1,0:T(8,128)S(1)}, u32[]{:S(2)}, u32[]{:S(2)}) collective-permute-start(f32[128,128]{1,0:T(8,128)} %get-tuple-element.24), channel_id=1, source_target_pairs={{8,16},{16,8},{24,32},{32,24},{40,48},{48,40},{56,64},{64,56},{72,... | collective-permute-start | bytes 196616 | tf_op jit(solution)/shard_map/ppermute | solution.py:476
  7.3 4.6 %collective-permute-start.1 = (f32[128,128]{1,0:T(8,128)}, f32[128,128]{1,0:T(8,128)S(1)}, u32[]{:S(2)}, u32[]{:S(2)}) collective-permute-start(f32[128,128]{1,0:T(8,128)} %get-tuple-element.25), channel_id=1, source_target_pairs={{0,8},{8,0},{16,24},{24,16},{32,40},{40,32},{48,56},{56,48},{64,72... | collective-permute-start | bytes 196616 | tf_op jit(solution)/shard_map/ppermute | solution.py:477
  11.9 1.3 %coefficients.1 = (f32[8,16,8,256]{3,2,1,0:T(8,128)S(1)}, f32[3,16,256]{2,1,0:T(8,128)S(1)}, f32[4,16,8,256]{3,2,1,0:T(8,128)S(1)}, f32[16,256]{1,0:T(8,128)S(1)}) custom-call(f32[2,4,64,128]{3,2,1,0:T(8,128)S(1)} %copy-done, f32[4,64,128]{2,1,0:T(8,128)S(1)} %copy-done.1, f32[4,64,128]{2,1,0:T(8,128)S(1)} %copy-done.2, f32[4,64,128]{2,1,0:T(8,128)S(1)} %copy-done.3, ...), custom_call_target="tpu_custom_call" | custom-call | flops 4000000000 | bytes 2097152 | tf_op jit(solution)/shard_map/coefficients/pallas_call | solution.py:478
  13.2 0.5 collective-permute-done.1.high_ref
  13.8 0.6 %sources.1 = (f32[2,16,8,256]{3,2,1,0:T(8,128)S(1)}, f32[2,16,8,256]{3,2,1,0:T(8,128)S(1)}, f32[48,128]{1,0:T(8,128)S(1)}) custom-call(f32[8,16,8,256]{3,2,1,0:T(8,128)S(1)} %get-tuple-element.20.fields_ref.refs_6_, f32[3,16,256]{2,1,0:T(8,128)S(1)} %get-tuple-element.21.small_ref.refs_7_, f32[4,16,8,256]{3,2,1,0:T(8,128)S(1)} %get-tuple-element.22.base_ref, ...), custom_call_target="tpu_custom_call" | custom-call | flops 1000000000 | bytes 2097152 | tf_op jit(solution)/shard_map/sources/pallas_call | solution.py:486
  14.4 3.2 %collective-permute-start.4 = (f32[48,128]{1,0:T(8,128)S(1)}, f32[48,128]{1,0:T(8,128)S(1)}, u32[]{:S(2)}, u32[]{:S(2)}) collective-permute-start(f32[48,128]{1,0:T(8,128)S(1)} %get-tuple-element.27.refs_0_), channel_id=1, source_target_pairs={{0,16},{8,24},{16,0},{24,8},{32,48},{40,56},{48,32},{56,40},{64,80... | collective-permute-start | bytes 73736 | tf_op jit(solution)/shard_map/ppermute | solution.py:500
  17.6 0.9 %collective-permute-start.3 = (f32[48,128]{1,0:T(8,128)S(1)}, f32[48,128]{1,0:T(8,128)S(1)}, u32[]{:S(2)}, u32[]{:S(2)}) collective-permute-start(f32[48,128]{1,0:T(8,128)S(1)} %get-tuple-element.27.refs_0_), channel_id=1, source_target_pairs={{0,24},{8,16},{16,8},{24,0},{32,56},{40,48},{48,40},{56,32},{64,88... | collective-permute-start | bytes 73736 | tf_op jit(solution)/shard_map/ppermute | solution.py:500
  18.8 2.7 %collective-permute-done.3.refs_2_ = f32[48,128]{1,0:T(8,128)S(1)} collective-permute-done((f32[48,128]{1,0:T(8,128)S(1)}, f32[48,128]{1,0:T(8,128)S(1)}, u32[]{:S(2)}, u32[]{:S(2)}) %collective-permute-start.3) | collective-permute-done | bytes 24608 | tf_op jit(solution)/shard_map/ppermute | solution.py:500
  21.5 0.4 groups.2
  21.8 3.1 %collective-permute-start.7 = (f32[48,128]{1,0:T(8,128)S(1)}, f32[48,128]{1,0:T(8,128)S(1)}, u32[]{:S(2)}, u32[]{:S(2)}) collective-permute-start(f32[48,128]{1,0:T(8,128)S(1)} %get-tuple-element.28.refs_0_), channel_id=1, source_target_pairs={{0,64},{8,72},{16,80},{24,88},{32,96},{40,104},{48,112},{56,120},{... | collective-permute-start | bytes 73736 | tf_op jit(solution)/shard_map/ppermute | solution.py:500
  24.9 2.6 %collective-permute-start.6 = (f32[48,128]{1,0:T(8,128)S(1)}, f32[48,128]{1,0:T(8,128)S(1)}, u32[]{:S(2)}, u32[]{:S(2)}) collective-permute-start(f32[48,128]{1,0:T(8,128)S(1)} %get-tuple-element.28.refs_0_), channel_id=1, source_target_pairs={{0,96},{8,104},{16,112},{24,120},{32,64},{40,72},{48,80},{56,88},{... | collective-permute-start | bytes 73736 | tf_op jit(solution)/shard_map/ppermute | solution.py:500
  27.7 1.7 %collective-permute-done.6.refs_2_ = f32[48,128]{1,0:T(8,128)S(1)} collective-permute-done((f32[48,128]{1,0:T(8,128)S(1)}, f32[48,128]{1,0:T(8,128)S(1)}, u32[]{:S(2)}, u32[]{:S(2)}) %collective-permute-start.6) | collective-permute-done | bytes 24608 | tf_op jit(solution)/shard_map/ppermute | solution.py:500
  29.4 0.8 %collective-permute-done.5.refs_1_ = f32[48,128]{1,0:T(8,128)S(1)} collective-permute-done((f32[48,128]{1,0:T(8,128)S(1)}, f32[48,128]{1,0:T(8,128)S(1)}, u32[]{:S(2)}, u32[]{:S(2)}) %collective-permute-start.5) | collective-permute-done | bytes 24608 | tf_op jit(solution)/shard_map/ppermute | solution.py:500
  30.5 4.6 %collective-permute-start.8 = (f32[48,128]{1,0:T(8,128)S(1)}, f32[48,128]{1,0:T(8,128)S(1)}, u32[]{:S(2)}, u32[]{:S(2)}) collective-permute-start(f32[48,128]{1,0:T(8,128)S(1)} %get-tuple-element.29.refs_0_), channel_id=1, source_target_pairs={{0,128},{8,136},{16,144},{24,152},{32,160},{40,168},{48,176},{56,1... | collective-permute-start | bytes 73736 | tf_op jit(solution)/shard_map/ppermute | solution.py:500
  35.1 2.4 %collective-permute-done.8.refs_1_ = f32[48,128]{1,0:T(8,128)S(1)} collective-permute-done((f32[48,128]{1,0:T(8,128)S(1)}, f32[48,128]{1,0:T(8,128)S(1)}, u32[]{:S(2)}, u32[]{:S(2)}) %collective-permute-start.8) | collective-permute-done | bytes 24608 | tf_op jit(solution)/shard_map/ppermute | solution.py:500
  37.5 2.3 %sweeps.1 = (f32[2,4,64,128]{3,2,1,0:T(8,128)}, f32[4,64,128]{2,1,0:T(8,128)S(1)}) custom-call(s32[1]{0:T(128)} %bitcast.place_ref, f32[48,128]{1,0:T(8,128)S(1)} %get-tuple-element.29.refs_0_, f32[48,128]{1,0:T(8,128)S(1)} %collective-permute-done.8.refs_1_, f32[4,48,128]{2,1,0:T(8,128)S(1)} %get-tuple-element.30.refs_2_, ...), custom_call_target="tpu_custom_call" | custom-call | flops 1000000000 | bytes 2097152 | tf_op jit(solution)/shard_map/sweeps/pallas_call | solution.py:513
  39.8 2.9 %collective-permute-start.11 = (f32[4,64,128]{2,1,0:T(8,128)S(1)}, f32[4,64,128]{2,1,0:T(8,128)S(1)}, u32[]{:S(2)}, u32[]{:S(2)}) collective-permute-start(f32[4,64,128]{2,1,0:T(8,128)S(1)} %get-tuple-element.37), channel_id=1, source_target_pairs={{0,4},{1,5},{2,6},{3,7},{4,0},{5,1},{6,2},{7,3},{8,12},{9,13},{10,... | collective-permute-start | bytes 393224 | tf_op jit(solution)/shard_map/ppermute | solution.py:524
  42.7 0.8 %collective-permute-start.10 = (f32[4,64,128]{2,1,0:T(8,128)S(1)}, f32[4,64,128]{2,1,0:T(8,128)S(1)}, u32[]{:S(2)}, u32[]{:S(2)}) collective-permute-start(f32[4,64,128]{2,1,0:T(8,128)S(1)} %get-tuple-element.37), channel_id=1, source_target_pairs={{0,6},{1,7},{2,4},{3,5},{4,2},{5,3},{6,0},{7,1},{8,14},{9,15},{10,... | collective-permute-start | bytes 393224 | tf_op jit(solution)/shard_map/ppermute | solution.py:524
  43.5 1.6 %collective-permute-done.11 = f32[4,64,128]{2,1,0:T(8,128)S(1)} collective-permute-done((f32[4,64,128]{2,1,0:T(8,128)S(1)}, f32[4,64,128]{2,1,0:T(8,128)S(1)}, u32[]{:S(2)}, u32[]{:S(2)}) %collective-permute-start.11) | collective-permute-done | bytes 131104 | tf_op jit(solution)/shard_map/ppermute | solution.py:524
  45.1 2.6 %collective-permute-done.10 = f32[4,64,128]{2,1,0:T(8,128)S(1)} collective-permute-done((f32[4,64,128]{2,1,0:T(8,128)S(1)}, f32[4,64,128]{2,1,0:T(8,128)S(1)}, u32[]{:S(2)}, u32[]{:S(2)}) %collective-permute-start.10) | collective-permute-done | bytes 131104 | tf_op jit(solution)/shard_map/ppermute | solution.py:524
  47.8 6.8 %collective-permute-start.12 = (f32[4,64,128]{2,1,0:T(8,128)S(1)}, f32[4,64,128]{2,1,0:T(8,128)S(1)}, u32[]{:S(2)}, u32[]{:S(2)}) collective-permute-start(f32[4,64,128]{2,1,0:T(8,128)S(1)} %add_add_fusion), channel_id=1, source_target_pairs={{0,1},{1,0},{2,3},{3,2},{4,5},{5,4},{6,7},{7,6},{8,9},{9,8},{10,11... | collective-permute-start | bytes 393224 | tf_op jit(solution)/shard_map/ppermute | solution.py:525
  54.6 1.0 %collective-permute-done.12 = f32[4,64,128]{2,1,0:T(8,128)S(1)} collective-permute-done((f32[4,64,128]{2,1,0:T(8,128)S(1)}, f32[4,64,128]{2,1,0:T(8,128)S(1)}, u32[]{:S(2)}, u32[]{:S(2)}) %collective-permute-start.12) | collective-permute-done | bytes 131104 | tf_op jit(solution)/shard_map/ppermute | solution.py:525
  55.6 0.7 %broadcast_subtract_fusion = f32[2,4,64,128]{3,2,1,0:T(8,128)} fusion(f32[2,4,64,128]{3,2,1,0:T(8,128)S(1)} %copy-done.7, f32[4,64,128]{2,1,0:T(8,128)S(1)} %add_multiply_fusion), kind=kLoop, calls=%fused_computation | loop fusion | flops 65536 | bytes 655360 | tf_op jit(solution)/shard_map/sub | solution.py:526
  (27 shorter events, 1.0 us)
Async XLA Ops:
  1.3 10.6 %copy-start = (f32[2,4,64,128]{3,2,1,0:T(8,128)S(1)}, f32[2,4,64,128]{3,2,1,0:T(8,128)}, u32[]{:S(2)}) copy-start(f32[2,4,64,128]{3,2,1,0:T(8,128)} %head_ref.1) | copy-start | bytes 786436
  1.3 10.6 %copy-start.1 = (f32[4,64,128]{2,1,0:T(8,128)S(1)}, f32[4,64,128]{2,1,0:T(8,128)}, u32[]{:S(2)}) copy-start(f32[4,64,128]{2,1,0:T(8,128)} %storage_ref.1) | copy-start | bytes 393220
  1.3 10.6 %copy-start.2 = (f32[4,64,128]{2,1,0:T(8,128)S(1)}, f32[4,64,128]{2,1,0:T(8,128)}, u32[]{:S(2)}) copy-start(f32[4,64,128]{2,1,0:T(8,128)} %flow_ref.1) | copy-start | bytes 393220
  1.3 10.6 %copy-start.3 = (f32[4,64,128]{2,1,0:T(8,128)S(1)}, f32[4,64,128]{2,1,0:T(8,128)}, u32[]{:S(2)}) copy-start(f32[4,64,128]{2,1,0:T(8,128)} %cross_ref.1) | copy-start | bytes 393220
  1.3 10.6 %copy-start.4 = (f32[4,64,128]{2,1,0:T(8,128)S(1)}, f32[4,64,128]{2,1,0:T(8,128)}, u32[]{:S(2)}) copy-start(f32[4,64,128]{2,1,0:T(8,128)} %vert_ref.1) | copy-start | bytes 393220
  1.3 10.6 %copy-start.5 = (s32[4,64,128]{2,1,0:T(8,128)S(1)}, s32[4,64,128]{2,1,0:T(8,128)}, u32[]{:S(2)}) copy-start(s32[4,64,128]{2,1,0:T(8,128)} %active_ref.1) | copy-start | bytes 393220
  6.7 6.6 %collective-permute-start = (f32[128,128]{1,0:T(8,128)}, f32[128,128]{1,0:T(8,128)S(1)}, u32[]{:S(2)}, u32[]{:S(2)}) collective-permute-start(f32[128,128]{1,0:T(8,128)} %get-tuple-element.24), channel_id=1, source_target_pairs={{8,16},{16,8},{24,32},{32,24},{40,48},{48,40},{56,64},{64,56},{72,... | collective-permute-start | bytes 196616 | tf_op jit(solution)/shard_map/ppermute | solution.py:476
  7.3 6.5 %copy-start.6 = (f32[128,128]{1,0:T(8,128)S(1)}, f32[128,128]{1,0:T(8,128)}, u32[]{:S(2)}) copy-start(f32[128,128]{1,0:T(8,128)} %get-tuple-element.23.own_ref) | copy-start | bytes 196612
  7.3 6.4 %collective-permute-start.1 = (f32[128,128]{1,0:T(8,128)}, f32[128,128]{1,0:T(8,128)S(1)}, u32[]{:S(2)}, u32[]{:S(2)}) collective-permute-start(f32[128,128]{1,0:T(8,128)} %get-tuple-element.25), channel_id=1, source_target_pairs={{0,8},{8,0},{16,24},{24,16},{32,40},{40,32},{48,56},{56,48},{64,72... | collective-permute-start | bytes 196616 | tf_op jit(solution)/shard_map/ppermute | solution.py:477
  14.4 4.4 %collective-permute-start.4 = (f32[48,128]{1,0:T(8,128)S(1)}, f32[48,128]{1,0:T(8,128)S(1)}, u32[]{:S(2)}, u32[]{:S(2)}) collective-permute-start(f32[48,128]{1,0:T(8,128)S(1)} %get-tuple-element.27.refs_0_), channel_id=1, source_target_pairs={{0,16},{8,24},{16,0},{24,8},{32,48},{40,56},{48,32},{56,40},{64,80... | collective-permute-start | bytes 73736 | tf_op jit(solution)/shard_map/ppermute | solution.py:500
  17.6 3.9 %collective-permute-start.3 = (f32[48,128]{1,0:T(8,128)S(1)}, f32[48,128]{1,0:T(8,128)S(1)}, u32[]{:S(2)}, u32[]{:S(2)}) collective-permute-start(f32[48,128]{1,0:T(8,128)S(1)} %get-tuple-element.27.refs_0_), channel_id=1, source_target_pairs={{0,24},{8,16},{16,8},{24,0},{32,56},{40,48},{48,40},{56,32},{64,88... | collective-permute-start | bytes 73736 | tf_op jit(solution)/shard_map/ppermute | solution.py:500
  18.4 3.0 %collective-permute-start.2 = (f32[48,128]{1,0:T(8,128)S(1)}, f32[48,128]{1,0:T(8,128)S(1)}, u32[]{:S(2)}, u32[]{:S(2)}) collective-permute-start(f32[48,128]{1,0:T(8,128)S(1)} %get-tuple-element.27.refs_0_), channel_id=1, source_target_pairs={{0,8},{8,0},{16,24},{24,16},{32,40},{40,32},{48,56},{56,48},{64,72... | collective-permute-start | bytes 73736 | tf_op jit(solution)/shard_map/ppermute | solution.py:500
  21.8 5.8 %collective-permute-start.7 = (f32[48,128]{1,0:T(8,128)S(1)}, f32[48,128]{1,0:T(8,128)S(1)}, u32[]{:S(2)}, u32[]{:S(2)}) collective-permute-start(f32[48,128]{1,0:T(8,128)S(1)} %get-tuple-element.28.refs_0_), channel_id=1, source_target_pairs={{0,64},{8,72},{16,80},{24,88},{32,96},{40,104},{48,112},{56,120},{... | collective-permute-start | bytes 73736 | tf_op jit(solution)/shard_map/ppermute | solution.py:500
  24.9 4.5 %collective-permute-start.6 = (f32[48,128]{1,0:T(8,128)S(1)}, f32[48,128]{1,0:T(8,128)S(1)}, u32[]{:S(2)}, u32[]{:S(2)}) collective-permute-start(f32[48,128]{1,0:T(8,128)S(1)} %get-tuple-element.28.refs_0_), channel_id=1, source_target_pairs={{0,96},{8,104},{16,112},{24,120},{32,64},{40,72},{48,80},{56,88},{... | collective-permute-start | bytes 73736 | tf_op jit(solution)/shard_map/ppermute | solution.py:500
  27.5 2.7 %collective-permute-start.5 = (f32[48,128]{1,0:T(8,128)S(1)}, f32[48,128]{1,0:T(8,128)S(1)}, u32[]{:S(2)}, u32[]{:S(2)}) collective-permute-start(f32[48,128]{1,0:T(8,128)S(1)} %get-tuple-element.28.refs_0_), channel_id=1, source_target_pairs={{0,32},{8,40},{16,48},{24,56},{32,0},{40,8},{48,16},{56,24},{64,96... | collective-permute-start | bytes 73736 | tf_op jit(solution)/shard_map/ppermute | solution.py:500
  30.5 7.0 %collective-permute-start.8 = (f32[48,128]{1,0:T(8,128)S(1)}, f32[48,128]{1,0:T(8,128)S(1)}, u32[]{:S(2)}, u32[]{:S(2)}) collective-permute-start(f32[48,128]{1,0:T(8,128)S(1)} %get-tuple-element.29.refs_0_), channel_id=1, source_target_pairs={{0,128},{8,136},{16,144},{24,152},{32,160},{40,168},{48,176},{56,1... | collective-permute-start | bytes 73736 | tf_op jit(solution)/shard_map/ppermute | solution.py:500
  39.8 5.3 %collective-permute-start.11 = (f32[4,64,128]{2,1,0:T(8,128)S(1)}, f32[4,64,128]{2,1,0:T(8,128)S(1)}, u32[]{:S(2)}, u32[]{:S(2)}) collective-permute-start(f32[4,64,128]{2,1,0:T(8,128)S(1)} %get-tuple-element.37), channel_id=1, source_target_pairs={{0,4},{1,5},{2,6},{3,7},{4,0},{5,1},{6,2},{7,3},{8,12},{9,13},{10,... | collective-permute-start | bytes 393224 | tf_op jit(solution)/shard_map/ppermute | solution.py:524
  42.7 5.0 %collective-permute-start.10 = (f32[4,64,128]{2,1,0:T(8,128)S(1)}, f32[4,64,128]{2,1,0:T(8,128)S(1)}, u32[]{:S(2)}, u32[]{:S(2)}) collective-permute-start(f32[4,64,128]{2,1,0:T(8,128)S(1)} %get-tuple-element.37), channel_id=1, source_target_pairs={{0,6},{1,7},{2,4},{3,5},{4,2},{5,3},{6,0},{7,1},{8,14},{9,15},{10,... | collective-permute-start | bytes 393224 | tf_op jit(solution)/shard_map/ppermute | solution.py:524
  43.5 4.3 %collective-permute-start.9 = (f32[4,64,128]{2,1,0:T(8,128)S(1)}, f32[4,64,128]{2,1,0:T(8,128)S(1)}, u32[]{:S(2)}, u32[]{:S(2)}) collective-permute-start(f32[4,64,128]{2,1,0:T(8,128)S(1)} %get-tuple-element.37), channel_id=1, source_target_pairs={{0,2},{1,3},{2,0},{3,1},{4,6},{5,7},{6,4},{7,5},{8,10},{9,11},{10,... | collective-permute-start | bytes 393224 | tf_op jit(solution)/shard_map/ppermute | solution.py:524
  47.8 7.9 %copy-start.7 = (f32[2,4,64,128]{3,2,1,0:T(8,128)S(1)}, f32[2,4,64,128]{3,2,1,0:T(8,128)}, u32[]{:S(2)}) copy-start(f32[2,4,64,128]{3,2,1,0:T(8,128)} %get-tuple-element.18) | copy-start | bytes 786436
  47.8 7.8 %collective-permute-start.12 = (f32[4,64,128]{2,1,0:T(8,128)S(1)}, f32[4,64,128]{2,1,0:T(8,128)S(1)}, u32[]{:S(2)}, u32[]{:S(2)}) collective-permute-start(f32[4,64,128]{2,1,0:T(8,128)S(1)} %add_add_fusion), channel_id=1, source_target_pairs={{0,1},{1,0},{2,3},{3,2},{4,5},{5,4},{6,7},{7,6},{8,9},{9,8},{10,11... | collective-permute-start | bytes 393224 | tf_op jit(solution)/shard_map/ppermute | solution.py:525
